TPU v7x, 128 devices: a whole 4x4x4 slice. The times are simulated.
128 devices in a mesh: db: 32 (over x, y, core), pb: 4 (over z).
Axes of the slice: x: 4, y: 4, z: 4, core: 2. Of those that a mesh axis runs over, the one named last changes fastest.
Arguments:
- query_maps: bfloat16 [128, 256, 256], P(('db', 'pb')), may hold values from -6 to 6
- database: bfloat16 [4096, 256, 256], P(('db', 'pb')), may hold values from -6 to 6
- shortlist: int32 [128, 128], P(('db', 'pb')), may hold values from 0 to 4095, as said below
- kernel_query: bfloat16 [3, 3], replicated, may hold values from -1.5 to 1.5
- kernel_db: bfloat16 [3, 3], replicated, may hold values from -1.5 to 1.5
Outputs:
- scores: float32 [128, 128], P(('db', 'pb'))
- top_scores: float32 [128, 100], P(('db', 'pb'))
Inputs may be any that keep to these rules, and one draw needn't show every extreme that they name: Within one query the ids are distinct. Among the 128 shortlist entries of the query held by device q (query q), at most 2 lie in any one shard of images (ids s * 32 to (s + 1) * 32 - 1), and some shard holds exactly 2 of them for every device.
All inputs are finite; a program needn't handle non-finite values.
Results may differ from a plain program's by a relative error of at most 0.0003.
Values may be sent and summed in bfloat16 or wider, within the bound.
No kernel may reach another device: no remote copies, remote signals or barrier semaphores. Data moves between devices by JAX's collectives and lax.ppermute only.
A program may use at most 128 MiB of HBM per device.

v0:
```python
import math

import jax
import jax.numpy as jnp
from jax import lax
from jax.sharding import PartitionSpec as P

GRID = 16
TOPK = 100


epsilon = 1e-06
score_scale = 8.0


def unit_maps(maps):
    values = maps.astype(jnp.float32)
    squares = jnp.sum(values * values, axis=1, keepdims=True)
    return (values * lax.rsqrt(squares + epsilon)).astype(jnp.bfloat16)


def conv_matrix(kernel):
    cell_count = GRID * GRID
    cell_index = jnp.arange(cell_count)
    row_out = (cell_index // GRID)[:, None]
    col_out = (cell_index % GRID)[:, None]
    row_in = (cell_index // GRID)[None, :]
    col_in = (cell_index % GRID)[None, :]
    weights = kernel.astype(jnp.float32)
    matrix = jnp.zeros((cell_count, cell_count), jnp.float32)
    for i in range(3):
        for j in range(3):
            hit = (row_in == row_out + i - 1) & (col_in == col_out + j - 1)
            matrix = matrix + weights[i, j] * hit.astype(jnp.float32)
    return matrix.astype(jnp.bfloat16)


def finish_pairs(correlation, conv_query, conv_db):
    rectified = jnp.maximum(correlation, 0.0).astype(jnp.bfloat16)
    filtered = jnp.einsum("qa,nab->nqb", conv_query, rectified, preferred_element_type=jnp.float32)
    filtered = filtered + jnp.einsum(
        "nqa,ba->nqb", rectified, conv_db, preferred_element_type=jnp.float32
    )
    return score_scale * jnp.mean(jnp.max(filtered, axis=1), axis=-1)


def shard_scores(gathered, slots, db_unit, conv_query, conv_db):
    source_count, width = slots.shape
    per_query = gathered.shape[0] // source_count
    grouped = gathered.reshape(source_count, per_query, gathered.shape[1], gathered.shape[2])
    step_size = math.gcd(source_count, max(1, 32 // width))

    def score_block(start):
        slot_block = lax.dynamic_slice_in_dim(slots, start, step_size, 0)
        group_block = lax.dynamic_slice_in_dim(grouped, start, step_size, 0)
        images = db_unit[slot_block]
        correlation = jnp.einsum(
            "scq,skcd->skqd", group_block[:, 0], images, preferred_element_type=jnp.float32
        )
        correlation = correlation.reshape(
            step_size * width, correlation.shape[-2], correlation.shape[-1]
        )
        return finish_pairs(correlation, conv_query, conv_db)

    starts = jnp.arange(source_count // step_size, dtype=jnp.int32) * step_size
    return lax.map(score_block, starts).reshape(source_count, width)


def body(query_maps, database, shortlist, kernel_query, kernel_db):
    query_unit = unit_maps(query_maps)
    db_unit = unit_maps(database)
    conv_query = conv_matrix(kernel_query)
    conv_db = conv_matrix(kernel_db)
    db_count = lax.axis_size("db")
    pb_count = lax.axis_size("pb")
    shard_count = db_count * pb_count
    per_query = query_maps.shape[0]
    cand_count = shortlist.shape[1]
    image_count = database.shape[0]
    flat_ids = shortlist.reshape(-1)
    row_count = flat_ids.shape[0]
    capacity = 2 * row_count // shard_count
    shard_of = flat_ids // image_count
    slot_of = flat_ids % image_count
    one_hot = (shard_of[:, None] == jnp.arange(shard_count, dtype=jnp.int32)[None, :]).astype(
        jnp.int32
    )
    bucket_pos = jnp.sum(jnp.cumsum(one_hot, axis=0) * one_hot, axis=1) - 1
    row_ids = jnp.arange(row_count, dtype=jnp.int32)
    query_of = row_ids // cand_count
    empty = jnp.zeros((shard_count, capacity), jnp.int32)
    send_slot = empty.at[shard_of, bucket_pos].set(slot_of)
    send_query = empty.at[shard_of, bucket_pos].set(query_of)
    requests = jnp.stack([send_slot, send_query])
    gathered = lax.all_gather(query_unit, ("db", "pb"), axis=0, tiled=True)
    found = shard_scores(
        gathered,
        lax.all_to_all(requests, ("db", "pb"), split_axis=1, concat_axis=1, tiled=True)[0],
        db_unit,
        conv_query,
        conv_db,
    )
    returned = lax.all_to_all(found, ("db", "pb"), split_axis=0, concat_axis=0, tiled=True)
    scores = returned[shard_of, bucket_pos].reshape(per_query, cand_count)
    top_scores = lax.top_k(scores, TOPK)[0]
    return (scores, top_scores)


def solution(mesh):
    in_specs = (
        P(("db", "pb"), None, None),
        P(("db", "pb"), None, None),
        P(("db", "pb"), None),
        P(),
        P(),
    )
    out_specs = (P(("db", "pb"), None), P(("db", "pb"), None))
    return jax.shard_map(body, mesh=mesh, in_specs=in_specs, out_specs=out_specs, check_vma=False)
```

profile of v0, /device:TPU:0, one launch (start us, length us, event | category | flops | bytes accessed | tf_op | source)
XLA Modules:
  0.0 346.6 jit_solution(9648573809774318235)
XLA Ops:
  7.2 1.0 fusion.53
  8.2 1.6 fusion.54
  9.8 0.7 and_select_fusion.3
  10.5 0.2 reduce_window_sum.11
  10.7 0.2 select_reduce_fusion
  10.9 0.7 fusion.61
  11.6 6.4 %scatter_fusion = s32[128,2]{0,1:T(2,128)S(1)} fusion(s32[128,2]{0,1:T(2,128)S(1)} %broadcast_in_dim.11.clone.1, s32[128]{0:T(128)S(1)} %fusion.60, s32[128]{0:T(128)S(1)} %get-tuple-element.427), kind=kCustom, calls=%fused_computation.2 | custom fusion | bytes 2560 | tf_op jit(solution)/shard_map/scatter | solution.py:92
  18.0 6.4 %scatter_fusion.1 = s32[128,2]{0,1:T(2,128)S(1)} fusion(s32[128,2]{0,1:T(2,128)S(1)} %broadcast_in_dim.11.clone, s32[128]{0:T(128)S(1)} %fusion.60, s32[128]{0:T(128)S(1)} %and_select_fusion.2), kind=kCustom, calls=%fused_computation.3 | custom fusion | bytes 2560 | tf_op jit(solution)/shard_map/scatter | solution.py:93
  24.4 0.8 copy.23
  25.1 11.1 %all-to-all-start = ((s32[2,128,2]{2,0,1:T(2,128)}), s32[2,128,2]{2,0,1:T(2,128)S(1)}, u32[]{:S(2)}, u32[]{:S(2)}) async-start(s32[2,128,2]{2,0,1:T(2,128)} %copy.23), calls=%async_computation | async-start | bytes 262144 | tf_op jit(solution)/shard_map/all_to_all | solution.py:98
  36.3 1.7 fusion.63
  38.0 1.7 fusion.62
  39.7 3.1 fusion.51
  42.8 3.0 fusion.52
  45.9 48.1 %all-gather.2.cloned.1.call-done = bf16[128,256,256]{2,1,0:T(8,128)(2,1)} async-done(((bf16[1,256,256]{2,1,0:T(8,128)(2,1)}), bf16[128,256,256]{2,1,0:T(8,128)(2,1)}) %all-gather.2.cloned.1.call-update) | async-done | bytes 16777232 | tf_op jit(solution)/shard_map/all_gather | solution.py:95
  93.9 224.7 %while.14 = (s32[]{:T(128)}, f32[8,32]{1,0:T(8,128)S(1)}, s32[8]{0:T(128)S(1)}, s32[128,2]{1,0:T(8,128)S(1)}, bf16[32,256,256]{2,1,0:T(8,128)(2,1)}, /*index=5*/...) while((s32[]{:T(128)}, f32[8,32]{1,0:T(8,128)S(1)}, ...), condition=%wide.region_9.10_spmd.clone.clone, body=%wide.region_6.9_spmd.clone.clone.sunk | while | flops 3233940480 | bytes 44123944 | solution.py:66
  93.9 0.6 dynamic_slice.35
  96.5 5.0 %gather_fusion = bf16[32,256,256]{2,1,0:T(8,128)(2,1)} fusion(bf16[32,256,256]{2,1,0:T(8,128)(2,1)} %get-tuple-element.688, s32[1024]{0:T(1024)S(1)} %pad_clamp_fusion.2), kind=kCustom, calls=%fused_computation.clone.clone.clone.1 | custom fusion | bytes 8388736 | tf_op jit(solution)/shard_map/while/body/eval_jaxpr/gather | solution.py:56
  101.5 4.4 %maximum_convert_fusion.2 = bf16[16,2,256,256]{3,2,1,0:T(8,128)(2,1)S(1)} fusion(bf16[16,2,256,256]{3,2,1,0:T(8,128)(2,1)} %bitcast.126, bf16[128,1,256,256]{3,2,0,1:T(8,128)(2,1)} %get-tuple-element.689, s32[]{:T(128)S(6)} %select_n.224), kind=kOutput, calls=%fused_computation.8.clone.1 | convolution fusion | flops 1077936128 | bytes 10485764 | tf_op jit(solution)/shard_map/while/body/eval_jaxpr/scq,skcd->skqd/dot_general | solution.py:57
  105.9 7.1 %fusion.81 = f32[32,256,256]{1,2,0:T(8,128)S(1)} fusion(bf16[32,256,256]{1,2,0:T(8,128)(2,1)S(1)} %bitcast.124, f32[]{:T(128)} %get-tuple-element.704, f32[]{:T(128)} %get-tuple-element.701, f32[]{:T(128)} %get-tuple-element.699, f32[]{:T(128)} %get-tuple-element.697, f32[]{:T(128)} %get-tuple-element.695, f32[]{:T(128)} %get-tuple-element.694, ...), kind=kOutput, calls=%fused_computation.23.clone.1 | convolution fusion | flops 1075904512 | bytes 12589092 | tf_op jit(solution)/shard_map/while/body/eval_jaxpr/qa,nab->nqb/dot_general | solution.py:40
  113.0 8.9 %fusion.82 = f32[32,256]{1,0:T(8,128)S(1)} fusion(f32[32,256,256]{1,2,0:T(8,128)S(1)} %fusion.81, bf16[32,256,256]{1,2,0:T(8,128)(2,1)S(1)} %bitcast.125, f32[]{:T(128)} %get-tuple-element.713, f32[]{:T(128)} %get-tuple-element.712, f32[]{:T(128)} %get-tuple-element.711, f32[]{:T(128)} %get-tuple-element.710, f32[]{:T(128)} %get-tuple-element.709, ...), kind=kOutput, calls=%fused_computation.7.clone.1 | convolution fusion | flops 1080090624 | bytes 12621860 | tf_op jit(solution)/shard_map/while/body/eval_jaxpr/nqa,ba->nqb/dot_general | solution.py:41
  121.9 0.1 reduce_sum.48
  122.0 0.6 dynamic_slice.35
  124.6 5.0 %gather_fusion = bf16[32,256,256]{2,1,0:T(8,128)(2,1)} fusion(bf16[32,256,256]{2,1,0:T(8,128)(2,1)} %get-tuple-element.688, s32[1024]{0:T(1024)S(1)} %pad_clamp_fusion.2), kind=kCustom, calls=%fused_computation.clone.clone.clone.1 | custom fusion | bytes 8388736 | tf_op jit(solution)/shard_map/while/body/eval_jaxpr/gather | solution.py:56
  129.6 4.4 %maximum_convert_fusion.2 = bf16[16,2,256,256]{3,2,1,0:T(8,128)(2,1)S(1)} fusion(bf16[16,2,256,256]{3,2,1,0:T(8,128)(2,1)} %bitcast.126, bf16[128,1,256,256]{3,2,0,1:T(8,128)(2,1)} %get-tuple-element.689, s32[]{:T(128)S(6)} %select_n.224), kind=kOutput, calls=%fused_computation.8.clone.1 | convolution fusion | flops 1077936128 | bytes 10485764 | tf_op jit(solution)/shard_map/while/body/eval_jaxpr/scq,skcd->skqd/dot_general | solution.py:57
  133.9 7.1 %fusion.81 = f32[32,256,256]{1,2,0:T(8,128)S(1)} fusion(bf16[32,256,256]{1,2,0:T(8,128)(2,1)S(1)} %bitcast.124, f32[]{:T(128)} %get-tuple-element.704, f32[]{:T(128)} %get-tuple-element.701, f32[]{:T(128)} %get-tuple-element.699, f32[]{:T(128)} %get-tuple-element.697, f32[]{:T(128)} %get-tuple-element.695, f32[]{:T(128)} %get-tuple-element.694, ...), kind=kOutput, calls=%fused_computation.23.clone.1 | convolution fusion | flops 1075904512 | bytes 12589092 | tf_op jit(solution)/shard_map/while/body/eval_jaxpr/qa,nab->nqb/dot_general | solution.py:40
  141.1 8.9 %fusion.82 = f32[32,256]{1,0:T(8,128)S(1)} fusion(f32[32,256,256]{1,2,0:T(8,128)S(1)} %fusion.81, bf16[32,256,256]{1,2,0:T(8,128)(2,1)S(1)} %bitcast.125, f32[]{:T(128)} %get-tuple-element.713, f32[]{:T(128)} %get-tuple-element.712, f32[]{:T(128)} %get-tuple-element.711, f32[]{:T(128)} %get-tuple-element.710, f32[]{:T(128)} %get-tuple-element.709, ...), kind=kOutput, calls=%fused_computation.7.clone.1 | convolution fusion | flops 1080090624 | bytes 12621860 | tf_op jit(solution)/shard_map/while/body/eval_jaxpr/nqa,ba->nqb/dot_general | solution.py:41
  150.1 0.6 dynamic_slice.35
  152.7 5.0 %gather_fusion = bf16[32,256,256]{2,1,0:T(8,128)(2,1)} fusion(bf16[32,256,256]{2,1,0:T(8,128)(2,1)} %get-tuple-element.688, s32[1024]{0:T(1024)S(1)} %pad_clamp_fusion.2), kind=kCustom, calls=%fused_computation.clone.clone.clone.1 | custom fusion | bytes 8388736 | tf_op jit(solution)/shard_map/while/body/eval_jaxpr/gather | solution.py:56
  157.7 4.4 %maximum_convert_fusion.2 = bf16[16,2,256,256]{3,2,1,0:T(8,128)(2,1)S(1)} fusion(bf16[16,2,256,256]{3,2,1,0:T(8,128)(2,1)} %bitcast.126, bf16[128,1,256,256]{3,2,0,1:T(8,128)(2,1)} %get-tuple-element.689, s32[]{:T(128)S(6)} %select_n.224), kind=kOutput, calls=%fused_computation.8.clone.1 | convolution fusion | flops 1077936128 | bytes 10485764 | tf_op jit(solution)/shard_map/while/body/eval_jaxpr/scq,skcd->skqd/dot_general | solution.py:57
  162.0 7.1 %fusion.81 = f32[32,256,256]{1,2,0:T(8,128)S(1)} fusion(bf16[32,256,256]{1,2,0:T(8,128)(2,1)S(1)} %bitcast.124, f32[]{:T(128)} %get-tuple-element.704, f32[]{:T(128)} %get-tuple-element.701, f32[]{:T(128)} %get-tuple-element.699, f32[]{:T(128)} %get-tuple-element.697, f32[]{:T(128)} %get-tuple-element.695, f32[]{:T(128)} %get-tuple-element.694, ...), kind=kOutput, calls=%fused_computation.23.clone.1 | convolution fusion | flops 1075904512 | bytes 12589092 | tf_op jit(solution)/shard_map/while/body/eval_jaxpr/qa,nab->nqb/dot_general | solution.py:40
  169.2 8.9 %fusion.82 = f32[32,256]{1,0:T(8,128)S(1)} fusion(f32[32,256,256]{1,2,0:T(8,128)S(1)} %fusion.81, bf16[32,256,256]{1,2,0:T(8,128)(2,1)S(1)} %bitcast.125, f32[]{:T(128)} %get-tuple-element.713, f32[]{:T(128)} %get-tuple-element.712, f32[]{:T(128)} %get-tuple-element.711, f32[]{:T(128)} %get-tuple-element.710, f32[]{:T(128)} %get-tuple-element.709, ...), kind=kOutput, calls=%fused_computation.7.clone.1 | convolution fusion | flops 1080090624 | bytes 12621860 | tf_op jit(solution)/shard_map/while/body/eval_jaxpr/nqa,ba->nqb/dot_general | solution.py:41
  178.1 0.1 reduce_sum.48
  178.2 0.6 dynamic_slice.35
  180.8 5.0 %gather_fusion = bf16[32,256,256]{2,1,0:T(8,128)(2,1)} fusion(bf16[32,256,256]{2,1,0:T(8,128)(2,1)} %get-tuple-element.688, s32[1024]{0:T(1024)S(1)} %pad_clamp_fusion.2), kind=kCustom, calls=%fused_computation.clone.clone.clone.1 | custom fusion | bytes 8388736 | tf_op jit(solution)/shard_map/while/body/eval_jaxpr/gather | solution.py:56
  185.8 4.4 %maximum_convert_fusion.2 = bf16[16,2,256,256]{3,2,1,0:T(8,128)(2,1)S(1)} fusion(bf16[16,2,256,256]{3,2,1,0:T(8,128)(2,1)} %bitcast.126, bf16[128,1,256,256]{3,2,0,1:T(8,128)(2,1)} %get-tuple-element.689, s32[]{:T(128)S(6)} %select_n.224), kind=kOutput, calls=%fused_computation.8.clone.1 | convolution fusion | flops 1077936128 | bytes 10485764 | tf_op jit(solution)/shard_map/while/body/eval_jaxpr/scq,skcd->skqd/dot_general | solution.py:57
  190.1 7.1 %fusion.81 = f32[32,256,256]{1,2,0:T(8,128)S(1)} fusion(bf16[32,256,256]{1,2,0:T(8,128)(2,1)S(1)} %bitcast.124, f32[]{:T(128)} %get-tuple-element.704, f32[]{:T(128)} %get-tuple-element.701, f32[]{:T(128)} %get-tuple-element.699, f32[]{:T(128)} %get-tuple-element.697, f32[]{:T(128)} %get-tuple-element.695, f32[]{:T(128)} %get-tuple-element.694, ...), kind=kOutput, calls=%fused_computation.23.clone.1 | convolution fusion | flops 1075904512 | bytes 12589092 | tf_op jit(solution)/shard_map/while/body/eval_jaxpr/qa,nab->nqb/dot_general | solution.py:40
  197.3 8.9 %fusion.82 = f32[32,256]{1,0:T(8,128)S(1)} fusion(f32[32,256,256]{1,2,0:T(8,128)S(1)} %fusion.81, bf16[32,256,256]{1,2,0:T(8,128)(2,1)S(1)} %bitcast.125, f32[]{:T(128)} %get-tuple-element.713, f32[]{:T(128)} %get-tuple-element.712, f32[]{:T(128)} %get-tuple-element.711, f32[]{:T(128)} %get-tuple-element.710, f32[]{:T(128)} %get-tuple-element.709, ...), kind=kOutput, calls=%fused_computation.7.clone.1 | convolution fusion | flops 1080090624 | bytes 12621860 | tf_op jit(solution)/shard_map/while/body/eval_jaxpr/nqa,ba->nqb/dot_general | solution.py:41
  206.3 0.6 dynamic_slice.35
  208.9 5.0 %gather_fusion = bf16[32,256,256]{2,1,0:T(8,128)(2,1)} fusion(bf16[32,256,256]{2,1,0:T(8,128)(2,1)} %get-tuple-element.688, s32[1024]{0:T(1024)S(1)} %pad_clamp_fusion.2), kind=kCustom, calls=%fused_computation.clone.clone.clone.1 | custom fusion | bytes 8388736 | tf_op jit(solution)/shard_map/while/body/eval_jaxpr/gather | solution.py:56
  213.9 4.4 %maximum_convert_fusion.2 = bf16[16,2,256,256]{3,2,1,0:T(8,128)(2,1)S(1)} fusion(bf16[16,2,256,256]{3,2,1,0:T(8,128)(2,1)} %bitcast.126, bf16[128,1,256,256]{3,2,0,1:T(8,128)(2,1)} %get-tuple-element.689, s32[]{:T(128)S(6)} %select_n.224), kind=kOutput, calls=%fused_computation.8.clone.1 | convolution fusion | flops 1077936128 | bytes 10485764 | tf_op jit(solution)/shard_map/while/body/eval_jaxpr/scq,skcd->skqd/dot_general | solution.py:57
  218.2 7.1 %fusion.81 = f32[32,256,256]{1,2,0:T(8,128)S(1)} fusion(bf16[32,256,256]{1,2,0:T(8,128)(2,1)S(1)} %bitcast.124, f32[]{:T(128)} %get-tuple-element.704, f32[]{:T(128)} %get-tuple-element.701, f32[]{:T(128)} %get-tuple-element.699, f32[]{:T(128)} %get-tuple-element.697, f32[]{:T(128)} %get-tuple-element.695, f32[]{:T(128)} %get-tuple-element.694, ...), kind=kOutput, calls=%fused_computation.23.clone.1 | convolution fusion | flops 1075904512 | bytes 12589092 | tf_op jit(solution)/shard_map/while/body/eval_jaxpr/qa,nab->nqb/dot_general | solution.py:40
  225.4 8.9 %fusion.82 = f32[32,256]{1,0:T(8,128)S(1)} fusion(f32[32,256,256]{1,2,0:T(8,128)S(1)} %fusion.81, bf16[32,256,256]{1,2,0:T(8,128)(2,1)S(1)} %bitcast.125, f32[]{:T(128)} %get-tuple-element.713, f32[]{:T(128)} %get-tuple-element.712, f32[]{:T(128)} %get-tuple-element.711, f32[]{:T(128)} %get-tuple-element.710, f32[]{:T(128)} %get-tuple-element.709, ...), kind=kOutput, calls=%fused_computation.7.clone.1 | convolution fusion | flops 1080090624 | bytes 12621860 | tf_op jit(solution)/shard_map/while/body/eval_jaxpr/nqa,ba->nqb/dot_general | solution.py:41
  234.2 0.1 reduce_sum.48
  234.4 0.6 dynamic_slice.35
  237.0 5.0 %gather_fusion = bf16[32,256,256]{2,1,0:T(8,128)(2,1)} fusion(bf16[32,256,256]{2,1,0:T(8,128)(2,1)} %get-tuple-element.688, s32[1024]{0:T(1024)S(1)} %pad_clamp_fusion.2), kind=kCustom, calls=%fused_computation.clone.clone.clone.1 | custom fusion | bytes 8388736 | tf_op jit(solution)/shard_map/while/body/eval_jaxpr/gather | solution.py:56
  242.0 4.4 %maximum_convert_fusion.2 = bf16[16,2,256,256]{3,2,1,0:T(8,128)(2,1)S(1)} fusion(bf16[16,2,256,256]{3,2,1,0:T(8,128)(2,1)} %bitcast.126, bf16[128,1,256,256]{3,2,0,1:T(8,128)(2,1)} %get-tuple-element.689, s32[]{:T(128)S(6)} %select_n.224), kind=kOutput, calls=%fused_computation.8.clone.1 | convolution fusion | flops 1077936128 | bytes 10485764 | tf_op jit(solution)/shard_map/while/body/eval_jaxpr/scq,skcd->skqd/dot_general | solution.py:57
  246.3 7.1 %fusion.81 = f32[32,256,256]{1,2,0:T(8,128)S(1)} fusion(bf16[32,256,256]{1,2,0:T(8,128)(2,1)S(1)} %bitcast.124, f32[]{:T(128)} %get-tuple-element.704, f32[]{:T(128)} %get-tuple-element.701, f32[]{:T(128)} %get-tuple-element.699, f32[]{:T(128)} %get-tuple-element.697, f32[]{:T(128)} %get-tuple-element.695, f32[]{:T(128)} %get-tuple-element.694, ...), kind=kOutput, calls=%fused_computation.23.clone.1 | convolution fusion | flops 1075904512 | bytes 12589092 | tf_op jit(solution)/shard_map/while/body/eval_jaxpr/qa,nab->nqb/dot_general | solution.py:40
  253.5 8.9 %fusion.82 = f32[32,256]{1,0:T(8,128)S(1)} fusion(f32[32,256,256]{1,2,0:T(8,128)S(1)} %fusion.81, bf16[32,256,256]{1,2,0:T(8,128)(2,1)S(1)} %bitcast.125, f32[]{:T(128)} %get-tuple-element.713, f32[]{:T(128)} %get-tuple-element.712, f32[]{:T(128)} %get-tuple-element.711, f32[]{:T(128)} %get-tuple-element.710, f32[]{:T(128)} %get-tuple-element.709, ...), kind=kOutput, calls=%fused_computation.7.clone.1 | convolution fusion | flops 1080090624 | bytes 12621860 | tf_op jit(solution)/shard_map/while/body/eval_jaxpr/nqa,ba->nqb/dot_general | solution.py:41
  262.3 0.1 reduce_sum.48
  262.5 0.6 dynamic_slice.35
  265.1 5.0 %gather_fusion = bf16[32,256,256]{2,1,0:T(8,128)(2,1)} fusion(bf16[32,256,256]{2,1,0:T(8,128)(2,1)} %get-tuple-element.688, s32[1024]{0:T(1024)S(1)} %pad_clamp_fusion.2), kind=kCustom, calls=%fused_computation.clone.clone.clone.1 | custom fusion | bytes 8388736 | tf_op jit(solution)/shard_map/while/body/eval_jaxpr/gather | solution.py:56
  270.0 4.4 %maximum_convert_fusion.2 = bf16[16,2,256,256]{3,2,1,0:T(8,128)(2,1)S(1)} fusion(bf16[16,2,256,256]{3,2,1,0:T(8,128)(2,1)} %bitcast.126, bf16[128,1,256,256]{3,2,0,1:T(8,128)(2,1)} %get-tuple-element.689, s32[]{:T(128)S(6)} %select_n.224), kind=kOutput, calls=%fused_computation.8.clone.1 | convolution fusion | flops 1077936128 | bytes 10485764 | tf_op jit(solution)/shard_map/while/body/eval_jaxpr/scq,skcd->skqd/dot_general | solution.py:57
  274.4 7.1 %fusion.81 = f32[32,256,256]{1,2,0:T(8,128)S(1)} fusion(bf16[32,256,256]{1,2,0:T(8,128)(2,1)S(1)} %bitcast.124, f32[]{:T(128)} %get-tuple-element.704, f32[]{:T(128)} %get-tuple-element.701, f32[]{:T(128)} %get-tuple-element.699, f32[]{:T(128)} %get-tuple-element.697, f32[]{:T(128)} %get-tuple-element.695, f32[]{:T(128)} %get-tuple-element.694, ...), kind=kOutput, calls=%fused_computation.23.clone.1 | convolution fusion | flops 1075904512 | bytes 12589092 | tf_op jit(solution)/shard_map/while/body/eval_jaxpr/qa,nab->nqb/dot_general | solution.py:40
  281.5 8.9 %fusion.82 = f32[32,256]{1,0:T(8,128)S(1)} fusion(f32[32,256,256]{1,2,0:T(8,128)S(1)} %fusion.81, bf16[32,256,256]{1,2,0:T(8,128)(2,1)S(1)} %bitcast.125, f32[]{:T(128)} %get-tuple-element.713, f32[]{:T(128)} %get-tuple-element.712, f32[]{:T(128)} %get-tuple-element.711, f32[]{:T(128)} %get-tuple-element.710, f32[]{:T(128)} %get-tuple-element.709, ...), kind=kOutput, calls=%fused_computation.7.clone.1 | convolution fusion | flops 1080090624 | bytes 12621860 | tf_op jit(solution)/shard_map/while/body/eval_jaxpr/nqa,ba->nqb/dot_general | solution.py:41
  290.6 0.6 dynamic_slice.35
  293.2 5.0 %gather_fusion = bf16[32,256,256]{2,1,0:T(8,128)(2,1)} fusion(bf16[32,256,256]{2,1,0:T(8,128)(2,1)} %get-tuple-element.688, s32[1024]{0:T(1024)S(1)} %pad_clamp_fusion.2), kind=kCustom, calls=%fused_computation.clone.clone.clone.1 | custom fusion | bytes 8388736 | tf_op jit(solution)/shard_map/while/body/eval_jaxpr/gather | solution.py:56
  298.1 4.4 %maximum_convert_fusion.2 = bf16[16,2,256,256]{3,2,1,0:T(8,128)(2,1)S(1)} fusion(bf16[16,2,256,256]{3,2,1,0:T(8,128)(2,1)} %bitcast.126, bf16[128,1,256,256]{3,2,0,1:T(8,128)(2,1)} %get-tuple-element.689, s32[]{:T(128)S(6)} %select_n.224), kind=kOutput, calls=%fused_computation.8.clone.1 | convolution fusion | flops 1077936128 | bytes 10485764 | tf_op jit(solution)/shard_map/while/body/eval_jaxpr/scq,skcd->skqd/dot_general | solution.py:57
  302.5 7.1 %fusion.81 = f32[32,256,256]{1,2,0:T(8,128)S(1)} fusion(bf16[32,256,256]{1,2,0:T(8,128)(2,1)S(1)} %bitcast.124, f32[]{:T(128)} %get-tuple-element.704, f32[]{:T(128)} %get-tuple-element.701, f32[]{:T(128)} %get-tuple-element.699, f32[]{:T(128)} %get-tuple-element.697, f32[]{:T(128)} %get-tuple-element.695, f32[]{:T(128)} %get-tuple-element.694, ...), kind=kOutput, calls=%fused_computation.23.clone.1 | convolution fusion | flops 1075904512 | bytes 12589092 | tf_op jit(solution)/shard_map/while/body/eval_jaxpr/qa,nab->nqb/dot_general | solution.py:40
  309.6 8.9 %fusion.82 = f32[32,256]{1,0:T(8,128)S(1)} fusion(f32[32,256,256]{1,2,0:T(8,128)S(1)} %fusion.81, bf16[32,256,256]{1,2,0:T(8,128)(2,1)S(1)} %bitcast.125, f32[]{:T(128)} %get-tuple-element.713, f32[]{:T(128)} %get-tuple-element.712, f32[]{:T(128)} %get-tuple-element.711, f32[]{:T(128)} %get-tuple-element.710, f32[]{:T(128)} %get-tuple-element.709, ...), kind=kOutput, calls=%fused_computation.7.clone.1 | convolution fusion | flops 1080090624 | bytes 12621860 | tf_op jit(solution)/shard_map/while/body/eval_jaxpr/nqa,ba->nqb/dot_general | solution.py:41
  318.5 0.1 reduce_sum.48
  318.8 17.0 %all_to_all.17 = f32[128,1,2]{2,1,0:T(1,128)S(1)} all-to-all(f32[128,1,2]{2,1,0:T(1,128)S(1)} %bitcast.131), channel_id=1, replica_groups=mesh['db'=32,'pb'=4] {'db','pb'}, dimensions={0} | all-to-all | bytes 2048 | tf_op jit(solution)/shard_map/all_to_all | solution.py:103
  335.8 1.3 gather_fusion.1
  337.1 2.6 top_k.9
  (66 shorter events, 1.9 us)
Async XLA Ops:
  7.2 86.8 %all-gather.2.cloned.1.call-start = ((), (), s32[]{:S(2)}) async-start(), calls=%async_computation.2 | async-start | bytes 16908288 | tf_op jit(solution)/shard_map/all_gather | solution.py:95
  25.1 20.7 %all-to-all-start = ((s32[2,128,2]{2,0,1:T(2,128)}), s32[2,128,2]{2,0,1:T(2,128)S(1)}, u32[]{:S(2)}, u32[]{:S(2)}) async-start(s32[2,128,2]{2,0,1:T(2,128)} %copy.23), calls=%async_computation | async-start | bytes 262144 | tf_op jit(solution)/shard_map/all_to_all | solution.py:98
  36.3 6.5 %copy-start = (bf16[32,256,256]{2,1,0:T(8,128)(2,1)S(1)}, bf16[32,256,256]{2,1,0:T(8,128)(2,1)}, u32[]{:S(2)}) copy-start(bf16[32,256,256]{2,1,0:T(8,128)(2,1)} %param.8) | copy-start | bytes 12582916
  337.1 2.7 copy-start.1
Sparse Core Ops, SparseCore 0:
  11.1 82.7 all-gather.1
where the time goes:
time: 350 us; the launch traced here: 347 us
  matrix products  163 us (47%)
  local copies, waits for them, and re-layouts  64 us (18%)
  waiting for transfers between devices  48.1 us (14%)
  blocking collectives  17 us (5%)
  loops' own time  15.1 us (4%)
  other arithmetic  14.2 us (4%)
  between operations  14.2 us (4%)
  starting transfers between devices  11.2 us (3%)
    dot_general x8, matrix products, finish_pairs(): jnp.einsum('nqa,ba->nqb', rectified, conv_db, preferred_element_type=jnp....  70.9 us
    dot_general x8, matrix products, finish_pairs(): jnp.einsum('qa,nab->nqb', conv_query, rectified, preferred_element_type=j...  57.1 us
    all_gather x1, waiting for transfers between devices, body(): gathered = lax.all_gather(query_unit, ('db', 'pb'), axis=0, tiled=True)  48.1 us
    gather x8, local copies, waits for them, and re-layouts, score_block(): images = db_unit[slot_block]  39.8 us
    dot_general x8, matrix products, score_block(): jnp.einsum('scq,skcd->skqd', group_block[:, 0], images, preferred_element...  34.8 us
    all_to_all x1, blocking collectives, body(): lax.all_to_all(found, ('db', 'pb'), split_axis=0, concat_axis=0, tiled=True)  17 us
    another operation x1, loops' own time, shard_scores(): return lax.map(score_block, starts).reshape(source_count, width)  15.1 us
    all_to_all x1, starting transfers between devices, body(): lax.all_to_all(requests, ('db', 'pb'), split_axis=1, concat_axis=1, tiled...  11.1 us
  transfers between devices with their start and end apart: 2, of which 1 were waited for; matrix products, arithmetic and copies ran while one was open for 7% of the time, Pallas kernels for 0%

commit v1 on v0

v1 whole, which is shorter than its diff:
```python
import jax
import jax.numpy as jnp
from jax import lax
from jax.experimental import pallas as pl
from jax.experimental.pallas import tpu as pltpu
from jax.sharding import Mesh, PartitionSpec as P

GRID = 16
CELLS = GRID * GRID
TOPK = 100
CAND = 128
IMAGES = 32
NODES = 64
ROWS = CELLS + 16
UNROLL = 8
SPARE = 4 * NODES

epsilon = 1e-06
score_scale = 8.0
f32 = jnp.float32
bf16 = jnp.bfloat16

MAIN = ("x", "y", "c", "z")
NODE = ("x", "y", "z")


def unit_maps(maps):
    values = maps.astype(f32)
    squares = jnp.sum(values * values, axis=1, keepdims=True)
    return (values * lax.rsqrt(squares + epsilon)).astype(bf16)


def conv_matrix(kernel):
    cell_index = jnp.arange(CELLS)
    row_out = (cell_index // GRID)[:, None]
    col_out = (cell_index % GRID)[:, None]
    row_in = (cell_index // GRID)[None, :]
    col_in = (cell_index % GRID)[None, :]
    weights = kernel.astype(f32)
    matrix = jnp.zeros((CELLS, CELLS), f32)
    for i in range(3):
        for j in range(3):
            hit = (row_in == row_out + i - 1) & (col_in == col_out + j - 1)
            matrix = matrix + weights[i, j] * hit.astype(f32)
    return matrix.astype(bf16)


def pack_kernel(query_ref, ids_ref, out_ref):
    values = query_ref[0].astype(f32)
    squares = jnp.sum(values * values, axis=0, keepdims=True)
    unit = values * lax.rsqrt(squares + epsilon)
    out_ref[0, :CELLS, :] = unit.T.astype(bf16)
    ids = ids_ref[...]
    high = lax.shift_right_logical(ids, 6).astype(f32)
    low = (ids & 63).astype(f32)
    row = jnp.concatenate([high, low], axis=1)
    first = lax.broadcasted_iota(jnp.int32, (16, 2 * CAND), 0) == 0
    out_ref[0, CELLS:, :] = jnp.where(first, jnp.broadcast_to(row, first.shape), 0.0).astype(bf16)


def pack(query_maps, shortlist):
    return pl.pallas_call(
        pack_kernel,
        out_shape=jax.ShapeDtypeStruct((1, ROWS, CELLS), bf16),
    )(query_maps, shortlist)


def pair_kernel(
    shard_ref, maps_hbm, own_hbm, other_hbm, conv_q_ref, conv_d_ref, out_ref,
    query_v, image_v, ids_v, table_v, column_v, peak_v, table_s, pair_s, sems,
):
    copies = [
        pltpu.make_async_copy(maps_hbm.at[:, pl.ds(CELLS, 16), :], ids_v, sems.at[0]),
        pltpu.make_async_copy(maps_hbm.at[:, pl.ds(0, CELLS), :], query_v, sems.at[1]),
        pltpu.make_async_copy(own_hbm, image_v.at[pl.ds(0, IMAGES)], sems.at[2]),
        pltpu.make_async_copy(other_hbm, image_v.at[pl.ds(IMAGES, IMAGES)], sems.at[3]),
    ]
    for copy in copies:
        copy.start()
    copies[0].wait()
    packed = jnp.sum(ids_v[...].astype(f32), axis=1)
    ids = packed[:, :CAND].astype(jnp.int32) * 64 + packed[:, CAND:].astype(jnp.int32)
    lane = lax.broadcasted_iota(jnp.int32, (NODES, CAND), 1)
    shard = lax.shift_right_logical(ids, 5)
    slot = ids & (IMAGES - 1)
    table = jnp.full((NODES, CAND), -1, jnp.int32)
    for side in range(2):
        held = shard == shard_ref[side]
        first = jnp.min(jnp.where(held, lane, CAND), axis=1, keepdims=True)
        last = jnp.max(jnp.where(held, lane, -1), axis=1, keepdims=True)
        last = jnp.where(last > first, last, -1)
        for which, column in ((2 * side, first), (2 * side + 1, last)):
            at = lane == column
            image = jnp.max(jnp.where(at, slot, -1), axis=1, keepdims=True)
            image = jnp.where(image >= 0, image + side * IMAGES, -1)
            table = jnp.where(lane == which, image, table)
            column_v[which] = jnp.broadcast_to(column, (NODES, CAND))
    table_v[...] = table
    move = pltpu.make_async_copy(table_v, table_s, sems.at[4])
    move.start()
    move.wait()

    def fill(query, count):
        for which in range(4):
            image = table_s[query, which]
            pair_s[count] = query * 65536 + (which * NODES + query) * 64 + jnp.maximum(image, 0)
            count = count + (image >= 0).astype(jnp.int32)
        return count

    count = lax.fori_loop(0, NODES, fill, jnp.int32(0))
    for extra in range(UNROLL):
        pair_s[count + extra] = SPARE * 64
    for copy in copies[1:]:
        copy.wait()

    def group(step, carry):
        found = []
        for part in range(UNROLL):
            code = pair_s[step * UNROLL + part]
            query = lax.shift_right_logical(code, 16)
            image = code & 63
            correlation = jnp.dot(query_v[query], image_v[image], preferred_element_type=f32)
            rectified = jnp.maximum(correlation, 0.0).astype(bf16)
            found.append((lax.shift_right_logical(code, 6) & 1023, rectified))
        for row, rectified in found:
            filtered = jnp.dot(conv_q_ref[...], rectified, preferred_element_type=f32)
            filtered = filtered + jnp.dot(rectified, conv_d_ref[...], preferred_element_type=f32)
            peak_v[pl.ds(row, 1), :] = jnp.max(filtered, axis=0, keepdims=True)
        return carry

    lax.fori_loop(0, (count + UNROLL - 1) // UNROLL, group, 0)
    total = jnp.zeros((NODES, CAND), f32)
    for which in range(4):
        peaks = peak_v[pl.ds(which * NODES, NODES), :]
        score = jnp.sum(peaks, axis=1, keepdims=True) * (score_scale / CELLS)
        total = jnp.where(lane == column_v[which], score, total)
    out_ref[...] = total


def pair_scores(shards, maps, own, other, conv_q, conv_d):
    smem = pl.BlockSpec(memory_space=pltpu.SMEM)
    vmem = pl.BlockSpec(memory_space=pltpu.VMEM)
    hbm = pl.BlockSpec(memory_space=pl.ANY)
    return pl.pallas_call(
        pair_kernel,
        out_shape=jax.ShapeDtypeStruct((NODES, CAND), f32),
        in_specs=[smem, hbm, hbm, hbm, vmem, vmem],
        out_specs=vmem,
        scratch_shapes=[
            pltpu.VMEM((NODES, CELLS, CELLS), bf16),
            pltpu.VMEM((2 * IMAGES, CELLS, CELLS), bf16),
            pltpu.VMEM((NODES, 16, CELLS), bf16),
            pltpu.VMEM((NODES, CAND), jnp.int32),
            pltpu.VMEM((4, NODES, CAND), jnp.int32),
            pltpu.VMEM((4 * NODES + 8, CELLS), f32),
            pltpu.SMEM((NODES, CAND), jnp.int32),
            pltpu.SMEM((4 * NODES + UNROLL,), jnp.int32),
            pltpu.SemaphoreType.DMA((5,)),
        ],
        compiler_params=pltpu.CompilerParams(vmem_limit_bytes=48 * 2**20),
    )(shards, maps, own, other, conv_q, conv_d)


def finish_kernel(parts_ref, scores_ref, top_ref):
    row = jnp.sum(parts_ref[...], axis=0, keepdims=True)
    scores_ref[...] = row
    across = jnp.broadcast_to(row, (CAND, CAND))
    down = across.T
    at_row = lax.broadcasted_iota(jnp.int32, (CAND, CAND), 0)
    at_col = lax.broadcasted_iota(jnp.int32, (CAND, CAND), 1)
    ahead = (across > down) | ((across == down) & (at_col < at_row))
    rank = jnp.sum(ahead.astype(f32), axis=1, keepdims=True)
    placed = jnp.where(rank == at_col.astype(f32), down, 0.0)
    top_ref[...] = jnp.sum(placed, axis=0, keepdims=True)[:, :TOPK]


def finish(parts):
    return pl.pallas_call(
        finish_kernel,
        out_shape=(
            jax.ShapeDtypeStruct((1, CAND), f32),
            jax.ShapeDtypeStruct((1, TOPK), f32),
        ),
    )(parts)


def body(query_maps, database, shortlist, kernel_query, kernel_db):
    payload = pack(query_maps, shortlist)
    maps = lax.all_gather(payload, NODE, axis=0, tiled=True)
    own = unit_maps(database)
    other = lax.ppermute(own, "c", [(0, 1), (1, 0)])
    conv_q = conv_matrix(kernel_query)
    conv_d = conv_matrix(kernel_db).T
    me = lax.axis_index("c")
    base = (lax.axis_index("x") * 4 + lax.axis_index("y")) * 8 + lax.axis_index("z")
    shards = jnp.stack([base + 4 * me, base + 4 * (1 - me)]).astype(jnp.int32)
    parts = pair_scores(shards, maps, own, other, conv_q, conv_d)
    parts = lax.all_to_all(parts, NODE, split_axis=0, concat_axis=0, tiled=True)
    return finish(parts)


def solution(mesh):
    fine = Mesh(mesh.devices.reshape(4, 4, 2, 4), MAIN)
    in_specs = (P(MAIN, None, None), P(MAIN, None, None), P(MAIN, None), P(), P())
    out_specs = (P(MAIN, None), P(MAIN, None))
    return jax.shard_map(body, mesh=fine, in_specs=in_specs, out_specs=out_specs, check_vma=False)
```

time: 350 us -> 149 us (0.43); the launches traced: 347 us -> 150 us
  matrix products: 163 us -> 0 us
  local copies, waits for them, and re-layouts: 64 us -> 1.37 us
  Pallas kernels: 0 us -> 24.9 us
  loops' own time: 15.1 us -> 0 us
  waiting for transfers between devices: 48.1 us -> 62.7 us
  starting transfers between devices: 11.2 us -> 0.04 us
  blocking collectives: 17 us -> 26.3 us
  other arithmetic: 14.2 us -> 20.8 us
    dot_general x24 -> x0, matrix products: 163 us -> none  [the longest x8 70.9 us: finish_pairs(): jnp.einsum('nqa,ba->nqb', rectified, conv_db, preferred_element_type=jnp....]
    gather x9 -> x0, local copies, waits for them, and re-layouts: 41 us -> none  [the longest x8 39.8 us: score_block(): images = db_unit[slot_block]]
    pallas_call x0 -> x3, Pallas kernels: none -> 24.9 us  [the longest x1 21.7 us: pair_scores(): pl.pallas_call(pair_kernel, out_shape=jax.ShapeDtypeStruct((NODES, CAND),...]
    another operation x1 -> x0, loops' own time: 15.1 us -> none  [shard_scores(): return lax.map(score_block, starts).reshape(source_count, width)]
    all_gather x1, waiting for transfers between devices: 48.1 us -> 62.7 us  [body(): maps = lax.all_gather(payload, NODE, axis=0, tiled=True)]
    convert_element_type x3, other arithmetic: 4.67 us -> 17.7 us  [the longest x2 12.4 us: conv_matrix(): return matrix.astype(bf16)]
    scatter x2 -> x0, local copies, waits for them, and re-layouts: 12.7 us -> none  [the longest x1 6.37 us: body(): send_slot = empty.at[shard_of, bucket_pos].set(slot_of)]
    all_to_all x1 -> x0, starting transfers between devices: 11.1 us -> none  [body(): lax.all_to_all(requests, ('db', 'pb'), split_axis=1, concat_axis=1, tiled...]
  transfers between devices with their start and end apart: 2 -> 2, of which waited for: 1 -> 1; matrix products, arithmetic and copies ran while one was open for 7% -> 15% of each run, Pallas kernels for 0% -> 0%
where the time goes in v1:
time: 149 us; the launch traced here: 150 us
  waiting for transfers between devices  62.7 us (42%)
  blocking collectives  26.3 us (18%)
  Pallas kernels  24.9 us (17%)
  other arithmetic  20.8 us (14%)
  between operations  14.1 us (9%)
    all_gather x1, waiting for transfers between devices, body(): maps = lax.all_gather(payload, NODE, axis=0, tiled=True)  62.7 us
    all_to_all x1, blocking collectives, body(): parts = lax.all_to_all(parts, NODE, split_axis=0, concat_axis=0, tiled=True)  26.3 us
    pallas_call x1, Pallas kernels, pair_scores(): pl.pallas_call(pair_kernel, out_shape=jax.ShapeDtypeStruct((NODES, CAND),...  21.7 us
    convert_element_type x2, other arithmetic, conv_matrix(): return matrix.astype(bf16)  12.4 us
    convert_element_type x1, other arithmetic, unit_maps(): return (values * lax.rsqrt(squares + epsilon)).astype(bf16)  5.31 us
    reduce_sum x1, other arithmetic, unit_maps(): squares = jnp.sum(values * values, axis=1, keepdims=True)  3.05 us
  transfers between devices with their start and end apart: 2, of which 1 were waited for; matrix products, arithmetic and copies ran while one was open for 15% of the time, Pallas kernels for 0%

profile of v1, /device:TPU:0, one launch (start us, length us, event | category | flops | bytes accessed | tf_op | source)
XLA Modules:
  0.0 150.2 jit_solution(1060936968325268582)
XLA Ops:
  7.2 0.0 copy-start
  7.2 0.0 copy-start.1
  7.2 0.0 all-gather.2.cloned.1.call-start
  7.2 1.7 %shard_map.68 = bf16[1,272,256]{2,1,0:T(8,128)(2,1)} custom-call(bf16[1,256,256]{2,1,0:T(8,128)(2,1)} %query_ref.1, s32[1,128]{1,0:T(1,128)} %ids_ref.1), custom_call_target="tpu_custom_call" | custom-call | tf_op jit(solution)/shard_map/pallas_call | solution.py:62
  8.9 0.0 all-gather.2.cloned.1.call-update
  9.0 3.1 %fusion = f32[32,256]{1,0:T(8,128)S(1)} fusion(bf16[32,256,256]{2,1,0:T(8,128)(2,1)} %param.6), kind=kLoop, calls=%fused_computation.2 | loop fusion | flops 6283264 | bytes 4227072 | tf_op jit(solution)/shard_map/reduce_sum | solution.py:29
  12.0 5.3 %fusion.1.own_hbm = bf16[32,256,256]{2,1,0:T(8,128)(2,1)} fusion(bf16[32,256,256]{2,1,0:T(8,128)(2,1)} %param.6, f32[32,256]{1,0:T(8,128)S(1)} %add_rsqrt_fusion), kind=kLoop, calls=%fused_computation.3 | loop fusion | flops 6291456 | bytes 8421376 | tf_op jit(solution)/shard_map/convert_element_type | solution.py:30
  17.3 0.0 collective-permute-start
  17.4 0.1 pad_add_fusion.shard_ref
  17.4 0.0 copy-done
  17.4 0.7 fusion.6
  18.1 0.0 copy-done.1
  18.1 0.7 fusion.5
  18.8 6.2 %add_convert_fusion.conv_d_ref = bf16[256,256]{1,0:T(8,128)(2,1)S(1)} fusion(f32[]{:T(128)} %bitcast.19, f32[]{:T(128)} %bitcast.18, f32[]{:T(128)} %bitcast.17, s32[256]{0:T(256)S(1)} %get-tuple-element.25, f32[]{:T(128)} %bitcast.16, f32[]{:T(128)} %bitcast.15, f32[]{:T(128)} %bitcast.14, f32[]{:T(128)} %bitcast.13, s32[256]{0:T(256)S(1)} %get-tuple-element.24, ...), kind=kLoop, calls=%fused_computation.22 | loop fusion | flops 2162688 | bytes 137252 | tf_op jit(solution)/shard_map/convert_element_type | solution.py:45
  25.0 6.2 %add_convert_fusion.1.conv_q_ref = bf16[256,256]{1,0:T(8,128)(2,1)S(1)} fusion(f32[]{:T(128)} %bitcast.10, f32[]{:T(128)} %bitcast.9, f32[]{:T(128)} %bitcast.8, f32[]{:T(128)} %bitcast.7, f32[]{:T(128)} %bitcast.6, f32[]{:T(128)} %bitcast.5, f32[]{:T(128)} %bitcast.4, f32[]{:T(128)} %bitcast.3, f32[]{:T(128)} %bitcast.2, s32[256]{0:T(256)S(1)} %get-tuple-element.20, ...), kind=kLoop, calls=%fused_computation.23 | loop fusion | flops 2162688 | bytes 137252 | tf_op jit(solution)/shard_map/convert_element_type | solution.py:45
  31.2 0.0 collective-permute-done.other_hbm
  31.2 62.7 %all-gather.2.cloned.1.call-done.maps_hbm = bf16[64,272,256]{2,1,0:T(8,128)(2,1)} async-done(((bf16[1,272,256]{2,1,0:T(8,128)(2,1)}), bf16[64,272,256]{2,1,0:T(8,128)(2,1)}) %all-gather.2.cloned.1.call-update) | async-done | bytes 8912912 | tf_op jit(solution)/shard_map/all_gather | solution.py:189
  93.9 21.7 %shard_map.69 = f32[64,128]{1,0:T(8,128)S(1)} custom-call(s32[2]{0:T(128)S(1)} %pad_add_fusion.shard_ref, bf16[64,272,256]{2,1,0:T(8,128)(2,1)} %all-gather.2.cloned.1.call-done.maps_hbm, bf16[32,256,256]{2,1,0:T(8,128)(2,1)} %fusion.1.own_hbm, bf16[32,256,256]{2,1,0:T(8,128)(2,1)} %collective-permute-done.other_hbm, ...), custom_call_target="tpu_custom_call" | custom-call | tf_op jit(solution)/shard_map/pallas_call | solution.py:144
  115.6 26.3 %all_to_all.11 = f32[64,1,128]{2,1,0:T(1,128)} all-to-all(f32[64,1,128]{2,1,0:T(1,128)S(1)} %bitcast.24), channel_id=1, replica_groups=mesh['x'=4,'y'=4,'c'=2,'z'=4] {'x','y','z'}, dimensions={0} | all-to-all | bytes 65536 | tf_op jit(solution)/shard_map/all_to_all | solution.py:198
  141.9 1.5 shard_map.70
  (4 shorter events, 0.0 us)
Async XLA Ops:
  7.2 10.3 %copy-start = (bf16[3,3]{1,0:T(4,128)(2,1)S(1)}, bf16[3,3]{1,0:T(4,128)(2,1)}, u32[]{:S(2)}) copy-start(bf16[3,3]{1,0:T(4,128)(2,1)} %param.8) | copy-start | bytes 58
  7.2 11.0 %copy-start.1 = (bf16[3,3]{1,0:T(4,128)(2,1)S(1)}, bf16[3,3]{1,0:T(4,128)(2,1)}, u32[]{:S(2)}) copy-start(bf16[3,3]{1,0:T(4,128)(2,1)} %param.9) | copy-start | bytes 58
  7.2 86.7 %all-gather.2.cloned.1.call-start = ((), (), s32[]{:S(2)}) async-start(), calls=%async_computation.1 | async-start | bytes 9052160 | tf_op jit(solution)/shard_map/all_gather | solution.py:189
  17.3 13.8 %collective-permute-start = (bf16[32,256,256]{2,1,0:T(8,128)(2,1)}, bf16[32,256,256]{2,1,0:T(8,128)(2,1)}, u32[]{:S(2)}, u32[]{:S(2)}) collective-permute-start(bf16[32,256,256]{2,1,0:T(8,128)(2,1)} %fusion.1.own_hbm), channel_id=1, source_target_pairs={{0,4},{4,0},{1,5},{5,1},{2,6},{6,2},{3,7},{7,3},{8,12},{12,8},{9,1... | collective-permute-start | bytes 12582920 | tf_op jit(solution)/shard_map/ppermute | solution.py:191
Sparse Core Ops, SparseCore 0:
  10.9 82.9 all-gather.1

commit v2 on v1

v2 whole, which is shorter than its diff:
```python
import jax
import jax.numpy as jnp
from jax import lax
from jax.experimental import pallas as pl
from jax.experimental.pallas import tpu as pltpu
from jax.sharding import Mesh, PartitionSpec as P

GRID = 16
CELLS = GRID * GRID
TOPK = 100
CAND = 128
IMAGES = 32
NODES = 64
CUTS = (0, 80, 176, CELLS)
UNROLL = 8
SPARE = 4 * NODES

epsilon = 1e-06
score_scale = 8.0
f32 = jnp.float32
bf16 = jnp.bfloat16

MAIN = ("x", "y", "c", "z")
NODE = ("x", "y", "z")
ORDERS = ("xyz", "yzx", "zxy")
PLACE = {"x": 0, "y": 1, "z": 2}


def exchange_pairs(axis, near):
    pairs = []
    for x in range(4):
        for y in range(4):
            for c in range(2):
                for z in range(4):
                    at = {"x": x, "y": y, "z": z}
                    to = dict(at)
                    to[axis] = at[axis] ^ (1 if (c == 0) == near else 3)
                    pairs.append(
                        (((x * 4 + y) * 2 + c) * 4 + z, ((to["x"] * 4 + to["y"]) * 2 + c) * 4 + to["z"])
                    )
    return pairs


PAIRS = {(axis, near): exchange_pairs(axis, near) for axis in "xyz" for near in (True, False)}


def unit(values):
    squares = jnp.sum(values * values, axis=0, keepdims=True)
    return values * lax.rsqrt(squares + epsilon)


def pack_kernel(query_ref, ids_ref, out0_ref, out1_ref, out2_ref):
    maps = unit(query_ref[0].astype(f32)).T.astype(bf16)
    ids = ids_ref[...]
    high = lax.shift_right_logical(ids, 6).astype(f32)
    low = (ids & 63).astype(f32)
    row = jnp.concatenate([high, low], axis=1)
    first = lax.broadcasted_iota(jnp.int32, (16, 2 * CAND), 0) == 0
    out0_ref[0, :16, :] = jnp.where(first, jnp.broadcast_to(row, first.shape), 0.0).astype(bf16)
    out0_ref[0, 16:, :] = maps[: CUTS[1]]
    out1_ref[0] = maps[CUTS[1] : CUTS[2]]
    out2_ref[0] = maps[CUTS[2] :]


def pack(query_maps, shortlist):
    rows = (CUTS[1] + 16, CUTS[2] - CUTS[1], CUTS[3] - CUTS[2])
    return pl.pallas_call(
        pack_kernel,
        out_shape=tuple(jax.ShapeDtypeStruct((1, r, CELLS), bf16) for r in rows),
    )(query_maps, shortlist)


def images_kernel(tap_q_ref, tap_d_ref, maps_ref, unit_ref, conv_q_ref, conv_d_ref):
    for image in range(maps_ref.shape[0]):
        unit_ref[image] = unit(maps_ref[image].astype(f32)).astype(bf16)

    @pl.when(pl.program_id(0) == 0)
    def _():
        near = lax.broadcasted_iota(jnp.int32, (CELLS, CELLS), 0)
        far = lax.broadcasted_iota(jnp.int32, (CELLS, CELLS), 1)
        for tap_ref, out_ref, result, source in (
            (tap_q_ref, conv_q_ref, near, far),
            (tap_d_ref, conv_d_ref, far, near),
        ):
            down = lax.shift_right_logical(source, 4) - lax.shift_right_logical(result, 4)
            right = (source & (GRID - 1)) - (result & (GRID - 1))
            matrix = jnp.zeros((CELLS, CELLS), f32)
            for i in range(3):
                for j in range(3):
                    hit = (down == i - 1) & (right == j - 1)
                    matrix = jnp.where(hit, tap_ref[i, j], matrix)
            out_ref[...] = matrix.astype(bf16)


def prepare_images(database, tap_q, tap_d):
    block = 4
    maps = pl.BlockSpec((block, CELLS, CELLS), lambda i: (i, 0, 0))
    square = pl.BlockSpec((CELLS, CELLS), lambda i: (0, 0))
    smem = pl.BlockSpec(memory_space=pltpu.SMEM)
    square_shape = jax.ShapeDtypeStruct((CELLS, CELLS), bf16)
    return pl.pallas_call(
        images_kernel,
        grid=(database.shape[0] // block,),
        in_specs=[smem, smem, maps],
        out_specs=(maps, square, square),
        out_shape=(jax.ShapeDtypeStruct(database.shape, bf16), square_shape, square_shape),
    )(tap_q, tap_d, database)


def spread(chunks):
    held = list(chunks)
    for phase in range(3):
        axes = [order[phase] for order in ORDERS]
        near = [lax.ppermute(m, MAIN, PAIRS[axis, True]) for m, axis in zip(held, axes)]
        far = [lax.ppermute(m, MAIN, PAIRS[axis, False]) for m, axis in zip(held, axes)]
        both = [lax.ppermute(m, MAIN, PAIRS[axis, False]) for m, axis in zip(near, axes)]
        parts = list(zip(held, near, far, both))
        held = [jnp.concatenate(part, axis=0) for part in parts] if phase < 2 else parts
    return held


def pair_kernel(
    place_ref, *refs,
):
    parts, refs = refs[:12], refs[12:]
    own_hbm, other_hbm, conv_q_ref, conv_d_ref, out_ref = refs[:5]
    query_v, image_v, ids_v, table_v, column_v, peak_v, total_v, table_s, pair_s, sems = refs[5:]
    id_copies, copies = [], []
    for piece, order in enumerate(ORDERS):
        size = CUTS[piece + 1] - CUTS[piece]
        skip = 16 if piece == 0 else 0
        for last in range(4):
            for middle in range(4):
                index = [0, 0, 0]
                index[PLACE[order[0]]] = slice(None)
                index[PLACE[order[1]]] = middle
                index[PLACE[order[2]]] = last
                source = parts[4 * piece + last]
                blocks = pl.ds(4 * middle, 4)
                copies.append(
                    pltpu.make_async_copy(
                        source.at[blocks, pl.ds(skip, size), :],
                        query_v.at[*index, pl.ds(CUTS[piece], size), :],
                        sems.at[1],
                    )
                )
                if piece == 0:
                    id_copies.append(
                        pltpu.make_async_copy(
                            source.at[blocks, pl.ds(0, 16), :], ids_v.at[*index], sems.at[0]
                        )
                    )
    image_copies = [
        pltpu.make_async_copy(own_hbm, image_v.at[pl.ds(0, IMAGES)], sems.at[2]),
        pltpu.make_async_copy(other_hbm, image_v.at[pl.ds(IMAGES, IMAGES)], sems.at[3]),
    ]
    for copy in id_copies + image_copies + copies:
        copy.start()
    pltpu.make_async_copy(ids_v, ids_v, sems.at[0]).wait()
    packed = jnp.sum(ids_v[...].reshape(NODES, 16, CELLS).astype(f32), axis=1)
    ids = packed[:, :CAND].astype(jnp.int32) * 64 + packed[:, CAND:].astype(jnp.int32)
    lane = lax.broadcasted_iota(jnp.int32, (NODES, CAND), 1)
    shard = lax.shift_right_logical(ids, 5)
    slot = ids & (IMAGES - 1)
    table = jnp.full((NODES, CAND), -1, jnp.int32)
    for side in range(2):
        held = shard == place_ref[side]
        first = jnp.min(jnp.where(held, lane, CAND), axis=1, keepdims=True)
        last = jnp.max(jnp.where(held, lane, -1), axis=1, keepdims=True)
        last = jnp.where(last > first, last, -1)
        for which, column in ((2 * side, first), (2 * side + 1, last)):
            at = lane == column
            image = jnp.max(jnp.where(at, slot, -1), axis=1, keepdims=True)
            image = jnp.where(image >= 0, image + side * IMAGES, -1)
            table = jnp.where(lane == which, image, table)
            column_v[which] = jnp.broadcast_to(column, (NODES, CAND))
    table_v[...] = table
    move = pltpu.make_async_copy(table_v, table_s, sems.at[4])
    move.start()
    move.wait()

    def fill(query, count):
        for which in range(4):
            image = table_s[query, which]
            pair_s[count] = query * 65536 + (which * NODES + query) * 64 + jnp.maximum(image, 0)
            count = count + (image >= 0).astype(jnp.int32)
        return count

    count = lax.fori_loop(0, NODES, fill, jnp.int32(0))
    for extra in range(UNROLL):
        pair_s[count + extra] = SPARE * 64
    for copy in image_copies:
        copy.wait()
    pltpu.make_async_copy(query_v, query_v, sems.at[1]).wait()

    def group(step, carry):
        found = []
        for part in range(UNROLL):
            code = pair_s[step * UNROLL + part]
            node = lax.shift_right_logical(code, 16)
            query = query_v[
                lax.shift_right_logical(node, 4), lax.shift_right_logical(node, 2) & 3, node & 3
            ]
            image = code & 63
            correlation = jnp.dot(query, image_v[image], preferred_element_type=f32)
            rectified = jnp.maximum(correlation, 0.0).astype(bf16)
            found.append((lax.shift_right_logical(code, 6) & 1023, rectified))
        for row, rectified in found:
            filtered = jnp.dot(conv_q_ref[...], rectified, preferred_element_type=f32)
            filtered = filtered + jnp.dot(rectified, conv_d_ref[...], preferred_element_type=f32)
            peak_v[pl.ds(row, 1), :] = jnp.max(filtered, axis=0, keepdims=True)
        return carry

    lax.fori_loop(0, (count + UNROLL - 1) // UNROLL, group, 0)
    total = jnp.zeros((NODES, CAND), f32)
    for which in range(4):
        peaks = peak_v[pl.ds(which * NODES, NODES), :]
        score = jnp.sum(peaks, axis=1, keepdims=True) * (score_scale / CELLS)
        total = jnp.where(lane == column_v[which], score, total)
    total_v[...] = total

    def settle(query, carry):
        out_ref[pl.ds(place_ref[2 + query], 1), :] = total_v[pl.ds(query, 1), :]
        return carry

    lax.fori_loop(0, NODES, settle, 0, unroll=8)


def pair_scores(place, parts, own, other, conv_q, conv_d):
    smem = pl.BlockSpec(memory_space=pltpu.SMEM)
    vmem = pl.BlockSpec(memory_space=pltpu.VMEM)
    hbm = pl.BlockSpec(memory_space=pl.ANY)
    return pl.pallas_call(
        pair_kernel,
        out_shape=jax.ShapeDtypeStruct((NODES, CAND), f32),
        in_specs=[smem] + [hbm] * 14 + [vmem, vmem],
        out_specs=vmem,
        scratch_shapes=[
            pltpu.VMEM((4, 4, 4, CELLS, CELLS), bf16),
            pltpu.VMEM((2 * IMAGES, CELLS, CELLS), bf16),
            pltpu.VMEM((4, 4, 4, 16, CELLS), bf16),
            pltpu.VMEM((NODES, CAND), jnp.int32),
            pltpu.VMEM((4, NODES, CAND), jnp.int32),
            pltpu.VMEM((4 * NODES + 8, CELLS), f32),
            pltpu.VMEM((NODES, CAND), f32),
            pltpu.SMEM((NODES, CAND), jnp.int32),
            pltpu.SMEM((4 * NODES + UNROLL,), jnp.int32),
            pltpu.SemaphoreType.DMA((5,)),
        ],
        compiler_params=pltpu.CompilerParams(vmem_limit_bytes=48 * 2**20),
    )(place, *parts, own, other, conv_q, conv_d)


def finish_kernel(parts_ref, scores_ref, top_ref):
    row = jnp.sum(parts_ref[...], axis=0, keepdims=True)
    scores_ref[...] = row
    across = jnp.broadcast_to(row, (CAND, CAND))
    down = across.T
    at_row = lax.broadcasted_iota(jnp.int32, (CAND, CAND), 0)
    at_col = lax.broadcasted_iota(jnp.int32, (CAND, CAND), 1)
    ahead = (across > down) | ((across == down) & (at_col < at_row))
    rank = jnp.sum(ahead.astype(f32), axis=1, keepdims=True)
    placed = jnp.where(rank == at_col.astype(f32), down, 0.0)
    top_ref[...] = jnp.sum(placed, axis=0, keepdims=True)[:, :TOPK]


def finish(parts):
    return pl.pallas_call(
        finish_kernel,
        out_shape=(
            jax.ShapeDtypeStruct((1, CAND), f32),
            jax.ShapeDtypeStruct((1, TOPK), f32),
        ),
    )(parts)


def body(query_maps, database, shortlist, kernel_query, kernel_db):
    chunks = pack(query_maps, shortlist)
    own, conv_q, conv_d = prepare_images(database, kernel_query.astype(f32), kernel_db.astype(f32))
    other = lax.ppermute(own, "c", [(0, 1), (1, 0)])
    parts = spread(chunks)
    me = lax.axis_index("c")
    at = [lax.axis_index(axis) for axis in NODE]
    base = (at[0] * 4 + at[1]) * 8 + at[2]
    step = jnp.arange(4, dtype=jnp.int32)
    offset = jnp.where(me == 0, step ^ lax.shift_right_logical(step, 1), (4 - step) & 3)
    offset = jnp.where((me == 1) & (step > 0), jnp.where(step == 1, 3, jnp.where(step == 2, 1, 2)), offset)
    spot = [a ^ offset for a in at]
    order = (spot[0][:, None, None] * 4 + spot[1][None, :, None]) * 4 + spot[2][None, None, :]
    place = jnp.concatenate(
        [jnp.stack([base + 4 * me, base + 4 * (1 - me)]), order.reshape(-1)]
    ).astype(jnp.int32)
    scores = pair_scores(place, [p for part in parts for p in part], own, other, conv_q, conv_d)
    scores = lax.all_to_all(scores, NODE, split_axis=0, concat_axis=0, tiled=True)
    return finish(scores)


def solution(mesh):
    fine = Mesh(mesh.devices.reshape(4, 4, 2, 4), MAIN)
    in_specs = (P(MAIN, None, None), P(MAIN, None, None), P(MAIN, None), P(), P())
    out_specs = (P(MAIN, None), P(MAIN, None))
    return jax.shard_map(body, mesh=fine, in_specs=in_specs, out_specs=out_specs, check_vma=False)
```

time: 149 us -> 150 us (level); the launches traced: 150 us -> 148 us
  starting transfers between devices: 0.04 us -> 42.2 us
  waiting for transfers between devices: 62.7 us -> 36.2 us
  other arithmetic: 20.8 us -> 2.76 us
  between operations: 14.1 us -> 0.78 us
  local copies, waits for them, and re-layouts: 1.37 us -> 9.39 us
  Pallas kernels: 24.9 us -> 31.5 us
    all_gather x1 -> x0, waiting for transfers between devices: 62.7 us -> none  [body(): maps = lax.all_gather(payload, NODE, axis=0, tiled=True)]
    ppermute x0 -> x27, starting transfers between devices: none -> 42.1 us  [the longest x18 38.4 us: spread(): lax.ppermute(m, MAIN, PAIRS[axis, False])]
    ppermute x0 -> x27, waiting for transfers between devices: none -> 36.2 us  [the longest x18 19.4 us: spread(): lax.ppermute(m, MAIN, PAIRS[axis, False])]
    convert_element_type x3 -> x2, other arithmetic: 17.7 us -> 2.51 us  [the longest x1 1.26 us: body(): kernel_db.astype(f32)]
    unnamed x4 -> x26, local copies, waits for them, and re-layouts: 0.01 us -> 7.95 us
    pallas_call x1 -> x2, Pallas kernels: 1.7 us -> 9.2 us  [the longest x1 7.46 us: prepare_images(): pl.pallas_call(images_kernel, grid=(database.shape[0] // block,), in_spec...]
    reduce_sum x1 -> x0, other arithmetic: 3.05 us -> none  [unit_maps(): squares = jnp.sum(values * values, axis=1, keepdims=True)]
  transfers between devices with their start and end apart: 2 -> 28, of which waited for: 1 -> 9; matrix products, arithmetic and copies ran while one was open for 15% -> 4% of each run, Pallas kernels for 0% -> 1%
where the time goes in v2:
time: 150 us; the launch traced here: 148 us
  starting transfers between devices  42.2 us (28%)
  waiting for transfers between devices  36.2 us (24%)
  Pallas kernels  31.5 us (21%)
  blocking collectives  25.2 us (17%)
  local copies, waits for them, and re-layouts  9.39 us (6%)
  other arithmetic  2.76 us (2%)
    ppermute x18, starting transfers between devices, spread(): lax.ppermute(m, MAIN, PAIRS[axis, False])  38.4 us
    all_to_all x1, blocking collectives, body(): lax.all_to_all(scores, NODE, split_axis=0, concat_axis=0, tiled=True)  25.2 us
    pallas_call x1, Pallas kernels, pair_scores(): pl.pallas_call(pair_kernel, out_shape=jax.ShapeDtypeStruct((NODES, CAND),...  20.8 us
    ppermute x18, waiting for transfers between devices, spread(): lax.ppermute(m, MAIN, PAIRS[axis, False])  19.4 us
    ppermute x9, waiting for transfers between devices, spread(): lax.ppermute(m, MAIN, PAIRS[axis, True])  16.8 us
    unnamed x26, local copies, waits for them, and re-layouts  7.95 us
    pallas_call x1, Pallas kernels, prepare_images(): pl.pallas_call(images_kernel, grid=(database.shape[0] // block,), in_spec...  7.46 us
    ppermute x9, starting transfers between devices, spread(): lax.ppermute(m, MAIN, PAIRS[axis, True])  3.66 us
  transfers between devices with their start and end apart: 28, of which 9 were waited for; matrix products, arithmetic and copies ran while one was open for 4% of the time, Pallas kernels for 1%

profile of v2, /device:TPU:0, one launch (start us, length us, event | category | flops | bytes accessed | tf_op | source)
XLA Modules:
  0.0 148.0 jit_solution(2724654609402105875)
XLA Ops:
  0.6 1.3 convert_element_type.6.tap_q_ref
  1.9 1.3 convert_element_type.7.tap_d_ref
  3.1 7.5 %shard_map.69 = (bf16[32,256,256]{2,1,0:T(8,128)(2,1)}, bf16[256,256]{1,0:T(8,128)(2,1)}, bf16[256,256]{1,0:T(8,128)(2,1)}) custom-call(f32[3,3]{1,0:T(4,128)} %convert_element_type.6.tap_q_ref, f32[3,3]{1,0:T(4,128)} %convert_element_type.7.tap_d_ref, bf16[32,256,256]{2,1,0:T(8,128)(2,1)} %maps_ref.1), custom_call_target="tpu_custom_call" | custom-call | tf_op jit(solution)/shard_map/pallas_call | solution.py:101
  10.6 0.1 collective-permute-start.27
  10.7 1.7 %shard_map.68 = (bf16[1,96,256]{2,1,0:T(8,128)(2,1)}, bf16[1,96,256]{2,1,0:T(8,128)(2,1)}, bf16[1,80,256]{2,1,0:T(8,128)(2,1)}) custom-call(bf16[1,256,256]{2,1,0:T(8,128)(2,1)} %query_ref.1, s32[1,128]{1,0:T(1,128)} %ids_ref.1), custom_call_target="tpu_custom_call" | custom-call | tf_op jit(solution)/shard_map/pallas_call | solution.py:67
  12.4 4.1 %collective-permute-start.19 = (bf16[1,80,256]{2,1,0:T(8,128)(2,1)}, bf16[1,80,256]{2,1,0:T(8,128)(2,1)S(1)}, u32[]{:S(2)}, u32[]{:S(2)}) collective-permute-start(bf16[1,80,256]{2,1,0:T(8,128)(2,1)} %get-tuple-element.10), channel_id=1, source_target_pairs={{0,3},{1,2},{2,1},{3,0},{4,5},{5,4},{6,7},{7,6},{8,11},{9,10},{10,... | collective-permute-start | bytes 122888 | tf_op jit(solution)/shard_map/ppermute | solution.py:115
  16.6 2.8 %collective-permute-start.1 = (bf16[1,96,256]{2,1,0:T(8,128)(2,1)}, bf16[1,96,256]{2,1,0:T(8,128)(2,1)S(1)}, u32[]{:S(2)}, u32[]{:S(2)}) collective-permute-start(bf16[1,96,256]{2,1,0:T(8,128)(2,1)} %get-tuple-element.8), channel_id=1, source_target_pairs={{0,96},{1,97},{2,98},{3,99},{4,36},{5,37},{6,38},{7,39},{8,104},{9... | collective-permute-start | bytes 147464 | tf_op jit(solution)/shard_map/ppermute | solution.py:115
  19.3 0.2 collective-permute-start
  19.6 1.5 constant_dynamic-update-slice_fusion.3
  21.0 0.8 constant_dynamic-update-slice_fusion.25
  21.8 3.1 %collective-permute-start.10 = (bf16[1,96,256]{2,1,0:T(8,128)(2,1)}, bf16[1,96,256]{2,1,0:T(8,128)(2,1)S(1)}, u32[]{:S(2)}, u32[]{:S(2)}) collective-permute-start(bf16[1,96,256]{2,1,0:T(8,128)(2,1)} %get-tuple-element.9), channel_id=1, source_target_pairs={{0,24},{1,25},{2,26},{3,27},{4,12},{5,13},{6,14},{7,15},{8,16},{9,... | collective-permute-start | bytes 147464 | tf_op jit(solution)/shard_map/ppermute | solution.py:115
  24.9 0.0 collective-permute-done.19
  24.9 0.2 collective-permute-start.9
  25.1 0.6 collective-permute-start.20
  25.7 3.6 %collective-permute-done.9 = bf16[1,96,256]{2,1,0:T(8,128)(2,1)S(1)} collective-permute-done((bf16[1,96,256]{2,1,0:T(8,128)(2,1)}, bf16[1,96,256]{2,1,0:T(8,128)(2,1)S(1)}, u32[]{:S(2)}, u32[]{:S(2)}) %collective-permute-start.9) | collective-permute-done | bytes 49184 | tf_op jit(solution)/shard_map/ppermute | solution.py:114
  29.3 1.7 %collective-permute-start.2 = (bf16[1,96,256]{2,1,0:T(8,128)(2,1)S(1)}, bf16[1,96,256]{2,1,0:T(8,128)(2,1)S(1)}, u32[]{:S(2)}, u32[]{:S(2)}) collective-permute-start(bf16[1,96,256]{2,1,0:T(8,128)(2,1)S(1)} %collective-permute-done), channel_id=1, source_target_pairs={{0,96},{1,97},{2,98},{3,99},{4,36},{5,37},{6,38},{7,39},{8,104},{9... | collective-permute-start | bytes 147464 | tf_op jit(solution)/shard_map/ppermute | solution.py:116
  31.0 0.6 constant_dynamic-update-slice_fusion.13
  31.6 0.2 collective-permute-start.11
  31.8 0.6 constant_dynamic-update-slice_fusion.12
  32.4 0.0 collective-permute-done.20
  32.5 1.7 %collective-permute-start.22 = (bf16[4,80,256]{2,1,0:T(8,128)(2,1)S(1)}, bf16[4,80,256]{2,1,0:T(8,128)(2,1)S(1)}, u32[]{:S(2)}, u32[]{:S(2)}) collective-permute-start(bf16[4,80,256]{2,1,0:T(8,128)(2,1)S(1)} %get-tuple-element.30), channel_id=1, source_target_pairs={{0,96},{1,97},{2,98},{3,99},{4,36},{5,37},{6,38},{7,39},{8,104},{9... | collective-permute-start | bytes 491528 | tf_op jit(solution)/shard_map/ppermute | solution.py:115
  34.1 0.6 collective-permute-start.21
  34.7 0.0 collective-permute-done.2
  34.7 3.1 %collective-permute-start.4 = (bf16[4,96,256]{2,1,0:T(8,128)(2,1)S(1)}, bf16[4,96,256]{2,1,0:T(8,128)(2,1)S(1)}, u32[]{:S(2)}, u32[]{:S(2)}) collective-permute-start(bf16[4,96,256]{2,1,0:T(8,128)(2,1)S(1)} %get-tuple-element.22), channel_id=1, source_target_pairs={{0,24},{1,25},{2,26},{3,27},{4,12},{5,13},{6,14},{7,15},{8,16},{9,... | collective-permute-start | bytes 589832 | tf_op jit(solution)/shard_map/ppermute | solution.py:115
  37.8 0.0 collective-permute-done.11
  37.8 0.0 collective-permute-start.3
  37.8 0.6 constant_dynamic-update-slice_fusion.11
  38.4 1.0 collective-permute-done.21
  39.4 0.5 collective-permute-start.13
  40.0 0.0 collective-permute-done.22
  40.0 2.2 %collective-permute-start.23 = (bf16[4,80,256]{2,1,0:T(8,128)(2,1)S(1)}, bf16[4,80,256]{2,1,0:T(8,128)(2,1)S(1)}, u32[]{:S(2)}, u32[]{:S(2)}) collective-permute-start(bf16[4,80,256]{2,1,0:T(8,128)(2,1)S(1)} %collective-permute-done.21), channel_id=1, source_target_pairs={{0,96},{1,97},{2,98},{3,99},{4,36},{5,37},{6,38},{7,39},{8,104},{9... | collective-permute-start | bytes 491528 | tf_op jit(solution)/shard_map/ppermute | solution.py:116
  42.2 1.3 collective-permute-done.3
  43.5 2.0 %collective-permute-start.12 = (bf16[4,96,256]{2,1,0:T(8,128)(2,1)S(1)}, bf16[4,96,256]{2,1,0:T(8,128)(2,1)S(1)}, u32[]{:S(2)}, u32[]{:S(2)}) collective-permute-start(bf16[4,96,256]{2,1,0:T(8,128)(2,1)S(1)} %get-tuple-element.14), channel_id=1, source_target_pairs={{0,1},{1,0},{2,3},{3,2},{4,7},{5,6},{6,5},{7,4},{8,9},{9,8},{10,11... | collective-permute-start | bytes 589832 | tf_op jit(solution)/shard_map/ppermute | solution.py:114
  45.5 1.0 collective-permute-done.23
  46.6 3.1 %collective-permute-start.5 = (bf16[4,96,256]{2,1,0:T(8,128)(2,1)S(1)}, bf16[4,96,256]{2,1,0:T(8,128)(2,1)S(1)}, u32[]{:S(2)}, u32[]{:S(2)}) collective-permute-start(bf16[4,96,256]{2,1,0:T(8,128)(2,1)S(1)} %collective-permute-done.3), channel_id=1, source_target_pairs={{0,24},{1,25},{2,26},{3,27},{4,12},{5,13},{6,14},{7,15},{8,16},{9,... | collective-permute-start | bytes 589832 | tf_op jit(solution)/shard_map/ppermute | solution.py:116
  49.7 0.0 collective-permute-done.12
  49.7 1.2 collective-permute-start.25
  50.9 0.7 constant_dynamic-update-slice_fusion.17
  51.6 0.0 collective-permute-done.4
  51.6 3.2 %collective-permute-start.14 = (bf16[4,96,256]{2,1,0:T(8,128)(2,1)S(1)}, bf16[4,96,256]{2,1,0:T(8,128)(2,1)S(1)}, u32[]{:S(2)}, u32[]{:S(2)}) collective-permute-start(bf16[4,96,256]{2,1,0:T(8,128)(2,1)S(1)} %collective-permute-done.12), channel_id=1, source_target_pairs={{0,3},{1,2},{2,1},{3,0},{4,5},{5,4},{6,7},{7,6},{8,11},{9,10},{10,... | collective-permute-start | bytes 589832 | tf_op jit(solution)/shard_map/ppermute | solution.py:116
  54.9 0.7 constant_dynamic-update-slice_fusion.16
  55.6 0.6 collective-permute-start.6
  56.1 4.5 %collective-permute-done.14 = bf16[4,96,256]{2,1,0:T(8,128)(2,1)S(1)} collective-permute-done((bf16[4,96,256]{2,1,0:T(8,128)(2,1)S(1)}, bf16[4,96,256]{2,1,0:T(8,128)(2,1)S(1)}, u32[]{:S(2)}, u32[]{:S(2)}) %collective-permute-start.14) | collective-permute-done | bytes 196640 | tf_op jit(solution)/shard_map/ppermute | solution.py:116
  60.7 0.7 constant_dynamic-update-slice_fusion.15.refs_4_
  61.4 0.0 collective-permute-start.15
  61.4 3.2 %collective-permute-start.7 = (bf16[16,96,256]{2,1,0:T(8,128)(2,1)S(1)}, bf16[16,96,256]{2,1,0:T(8,128)(2,1)S(1)}, u32[]{:S(2)}, u32[]{:S(2)}) collective-permute-start(bf16[16,96,256]{2,1,0:T(8,128)(2,1)S(1)} %constant_dynamic-update-slice_fusion.4.refs_0_), channel_id=1, source_target_pairs={{0,3},{1,2},{2,1},{3,0},{4,5},{5,4},{6,7},{7,6},{8,11},{9,10},{10,... | collective-permute-start | bytes 2359304 | tf_op jit(solution)/shard_map/ppermute | solution.py:115
  64.6 0.8 copy-done.2
  65.4 11.0 %collective-permute-done.24.refs_9_ = bf16[16,80,256]{2,1,0:T(8,128)(2,1)} collective-permute-done((bf16[16,80,256]{2,1,0:T(8,128)(2,1)S(1)}, bf16[16,80,256]{2,1,0:T(8,128)(2,1)}, u32[]{:S(2)}, u32[]{:S(2)}) %collective-permute-start.24) | collective-permute-done | bytes 655392 | tf_op jit(solution)/shard_map/ppermute | solution.py:114
  76.4 1.9 %collective-permute-start.16 = (bf16[16,96,256]{2,1,0:T(8,128)(2,1)}, bf16[16,96,256]{2,1,0:T(8,128)(2,1)}, u32[]{:S(2)}, u32[]{:S(2)}) collective-permute-start(bf16[16,96,256]{2,1,0:T(8,128)(2,1)} %constant_dynamic-update-slice_fusion.15.refs_4_), channel_id=1, source_target_pairs={{0,96},{1,97},{2,98},{3,99},{4,36},{5,37},{6,38},{7,39},{8,104},{9... | collective-permute-start | bytes 2359304 | tf_op jit(solution)/shard_map/ppermute | solution.py:115
  78.3 3.0 %collective-permute-start.8 = (bf16[16,96,256]{2,1,0:T(8,128)(2,1)S(1)}, bf16[16,96,256]{2,1,0:T(8,128)(2,1)S(1)}, u32[]{:S(2)}, u32[]{:S(2)}) collective-permute-start(bf16[16,96,256]{2,1,0:T(8,128)(2,1)S(1)} %collective-permute-done.6.refs_1_), channel_id=1, source_target_pairs={{0,3},{1,2},{2,1},{3,0},{4,5},{5,4},{6,7},{7,6},{8,11},{9,10},{10,... | collective-permute-start | bytes 2359304 | tf_op jit(solution)/shard_map/ppermute | solution.py:116
  81.3 0.1 collective-permute-start.17
  81.4 2.8 %collective-permute-start.26 = (bf16[16,80,256]{2,1,0:T(8,128)(2,1)}, bf16[16,80,256]{2,1,0:T(8,128)(2,1)}, u32[]{:S(2)}, u32[]{:S(2)}) collective-permute-start(bf16[16,80,256]{2,1,0:T(8,128)(2,1)} %collective-permute-done.24.refs_9_), channel_id=1, source_target_pairs={{0,24},{1,25},{2,26},{3,27},{4,12},{5,13},{6,14},{7,15},{8,16},{9,... | collective-permute-start | bytes 1966088 | tf_op jit(solution)/shard_map/ppermute | solution.py:116
  84.2 0.1 add_multiply_fusion
  84.3 0.1 broadcast_add_fusion
  84.4 0.1 add.57
  84.5 0.1 pad_add_fusion.place_ref
  84.5 5.4 %collective-permute-done.16.refs_6_ = bf16[16,96,256]{2,1,0:T(8,128)(2,1)} collective-permute-done((bf16[16,96,256]{2,1,0:T(8,128)(2,1)}, bf16[16,96,256]{2,1,0:T(8,128)(2,1)}, u32[]{:S(2)}, u32[]{:S(2)}) %collective-permute-start.16) | collective-permute-done | bytes 786464 | tf_op jit(solution)/shard_map/ppermute | solution.py:115
  89.9 3.6 %collective-permute-done.26.refs_11_ = bf16[16,80,256]{2,1,0:T(8,128)(2,1)} collective-permute-done((bf16[16,80,256]{2,1,0:T(8,128)(2,1)}, bf16[16,80,256]{2,1,0:T(8,128)(2,1)}, u32[]{:S(2)}, u32[]{:S(2)}) %collective-permute-start.26) | collective-permute-done | bytes 655392 | tf_op jit(solution)/shard_map/ppermute | solution.py:116
  93.6 4.8 %collective-permute-done.17.refs_7_ = bf16[16,96,256]{2,1,0:T(8,128)(2,1)} collective-permute-done((bf16[16,96,256]{2,1,0:T(8,128)(2,1)}, bf16[16,96,256]{2,1,0:T(8,128)(2,1)}, u32[]{:S(2)}, u32[]{:S(2)}) %collective-permute-start.17) | collective-permute-done | bytes 786464 | tf_op jit(solution)/shard_map/ppermute | solution.py:116
  98.4 1.1 copy-done.1
  99.4 1.1 copy-done.3
  100.5 20.8 %shard_map.70 = f32[64,128]{1,0:T(8,128)S(1)} custom-call(s32[66]{0:T(128)S(1)} %pad_add_fusion.place_ref, bf16[16,96,256]{2,1,0:T(8,128)(2,1)S(1)} %constant_dynamic-update-slice_fusion.4.refs_0_, bf16[16,96,256]{2,1,0:T(8,128)(2,1)S(1)} %collective-permute-done.6.refs_1_, bf16[16,96,256]{2,1,0:T(8,128)(2,1)S(1)} %collective-permute-done.7.refs_2_, ...), custom_call_target="tpu_custom_call" | custom-call | tf_op jit(solution)/shard_map/pallas_call | solution.py:233
  121.3 25.2 %all_to_all.11 = f32[64,1,128]{2,1,0:T(1,128)} all-to-all(f32[64,1,128]{2,1,0:T(1,128)S(1)} %bitcast.6), channel_id=1, replica_groups=mesh['x'=4,'y'=4,'c'=2,'z'=4] {'x','y','z'}, dimensions={0} | all-to-all | bytes 65536 | tf_op jit(solution)/shard_map/all_to_all | solution.py:294
  146.5 1.5 shard_map.71
  (37 shorter events, 0.2 us)
Async XLA Ops:
  10.6 87.7 %copy-start.4 = (bf16[256,256]{1,0:T(8,128)(2,1)S(1)}, bf16[256,256]{1,0:T(8,128)(2,1)}, u32[]{:S(2)}) copy-start(bf16[256,256]{1,0:T(8,128)(2,1)} %get-tuple-element.12.refs_14_) | copy-start | bytes 393220
  10.6 87.7 %copy-start.5 = (bf16[256,256]{1,0:T(8,128)(2,1)S(1)}, bf16[256,256]{1,0:T(8,128)(2,1)}, u32[]{:S(2)}) copy-start(bf16[256,256]{1,0:T(8,128)(2,1)} %get-tuple-element.13.refs_15_) | copy-start | bytes 393220
  10.6 87.7 %collective-permute-start.27 = (bf16[32,256,256]{2,1,0:T(8,128)(2,1)}, bf16[32,256,256]{2,1,0:T(8,128)(2,1)}, u32[]{:S(2)}, u32[]{:S(2)}) collective-permute-start(bf16[32,256,256]{2,1,0:T(8,128)(2,1)} %get-tuple-element.11.refs_12_), channel_id=1, source_target_pairs={{0,4},{4,0},{1,5},{5,1},{2,6},{6,2},{3,7},{7,3},{8,12},{12,8},{9,1... | collective-permute-start | bytes 12582920 | tf_op jit(solution)/shard_map/ppermute | solution.py:280
  12.4 12.5 %collective-permute-start.19 = (bf16[1,80,256]{2,1,0:T(8,128)(2,1)}, bf16[1,80,256]{2,1,0:T(8,128)(2,1)S(1)}, u32[]{:S(2)}, u32[]{:S(2)}) collective-permute-start(bf16[1,80,256]{2,1,0:T(8,128)(2,1)} %get-tuple-element.10), channel_id=1, source_target_pairs={{0,3},{1,2},{2,1},{3,0},{4,5},{5,4},{6,7},{7,6},{8,11},{9,10},{10,... | collective-permute-start | bytes 122888 | tf_op jit(solution)/shard_map/ppermute | solution.py:115
  16.6 5.2 %collective-permute-start.18 = (bf16[1,80,256]{2,1,0:T(8,128)(2,1)}, bf16[1,80,256]{2,1,0:T(8,128)(2,1)S(1)}, u32[]{:S(2)}, u32[]{:S(2)}) collective-permute-start(bf16[1,80,256]{2,1,0:T(8,128)(2,1)} %get-tuple-element.10), channel_id=1, source_target_pairs={{0,1},{1,0},{2,3},{3,2},{4,7},{5,6},{6,5},{7,4},{8,9},{9,8},{10,11... | collective-permute-start | bytes 122888 | tf_op jit(solution)/shard_map/ppermute | solution.py:114
  16.6 15.0 %collective-permute-start.1 = (bf16[1,96,256]{2,1,0:T(8,128)(2,1)}, bf16[1,96,256]{2,1,0:T(8,128)(2,1)S(1)}, u32[]{:S(2)}, u32[]{:S(2)}) collective-permute-start(bf16[1,96,256]{2,1,0:T(8,128)(2,1)} %get-tuple-element.8), channel_id=1, source_target_pairs={{0,96},{1,97},{2,98},{3,99},{4,36},{5,37},{6,38},{7,39},{8,104},{9... | collective-permute-start | bytes 147464 | tf_op jit(solution)/shard_map/ppermute | solution.py:115
  19.3 5.8 %collective-permute-start = (bf16[1,96,256]{2,1,0:T(8,128)(2,1)}, bf16[1,96,256]{2,1,0:T(8,128)(2,1)S(1)}, u32[]{:S(2)}, u32[]{:S(2)}) collective-permute-start(bf16[1,96,256]{2,1,0:T(8,128)(2,1)} %get-tuple-element.8), channel_id=1, source_target_pairs={{0,32},{1,33},{2,34},{3,35},{4,100},{5,101},{6,102},{7,103},{8,40}... | collective-permute-start | bytes 147464 | tf_op jit(solution)/shard_map/ppermute | solution.py:114
  21.8 10.0 %collective-permute-start.10 = (bf16[1,96,256]{2,1,0:T(8,128)(2,1)}, bf16[1,96,256]{2,1,0:T(8,128)(2,1)S(1)}, u32[]{:S(2)}, u32[]{:S(2)}) collective-permute-start(bf16[1,96,256]{2,1,0:T(8,128)(2,1)} %get-tuple-element.9), channel_id=1, source_target_pairs={{0,24},{1,25},{2,26},{3,27},{4,12},{5,13},{6,14},{7,15},{8,16},{9,... | collective-permute-start | bytes 147464 | tf_op jit(solution)/shard_map/ppermute | solution.py:115
  24.9 4.4 %collective-permute-start.9 = (bf16[1,96,256]{2,1,0:T(8,128)(2,1)}, bf16[1,96,256]{2,1,0:T(8,128)(2,1)S(1)}, u32[]{:S(2)}, u32[]{:S(2)}) collective-permute-start(bf16[1,96,256]{2,1,0:T(8,128)(2,1)} %get-tuple-element.9), channel_id=1, source_target_pairs={{0,8},{1,9},{2,10},{3,11},{4,28},{5,29},{6,30},{7,31},{8,0},{9,1},... | collective-permute-start | bytes 147464 | tf_op jit(solution)/shard_map/ppermute | solution.py:114
  25.1 7.3 %collective-permute-start.20 = (bf16[1,80,256]{2,1,0:T(8,128)(2,1)S(1)}, bf16[1,80,256]{2,1,0:T(8,128)(2,1)S(1)}, u32[]{:S(2)}, u32[]{:S(2)}) collective-permute-start(bf16[1,80,256]{2,1,0:T(8,128)(2,1)S(1)} %collective-permute-done.18), channel_id=1, source_target_pairs={{0,3},{1,2},{2,1},{3,0},{4,5},{5,4},{6,7},{7,6},{8,11},{9,10},{10,... | collective-permute-start | bytes 122888 | tf_op jit(solution)/shard_map/ppermute | solution.py:116
  29.3 5.4 %collective-permute-start.2 = (bf16[1,96,256]{2,1,0:T(8,128)(2,1)S(1)}, bf16[1,96,256]{2,1,0:T(8,128)(2,1)S(1)}, u32[]{:S(2)}, u32[]{:S(2)}) collective-permute-start(bf16[1,96,256]{2,1,0:T(8,128)(2,1)S(1)} %collective-permute-done), channel_id=1, source_target_pairs={{0,96},{1,97},{2,98},{3,99},{4,36},{5,37},{6,38},{7,39},{8,104},{9... | collective-permute-start | bytes 147464 | tf_op jit(solution)/shard_map/ppermute | solution.py:116
  31.6 6.2 %collective-permute-start.11 = (bf16[1,96,256]{2,1,0:T(8,128)(2,1)S(1)}, bf16[1,96,256]{2,1,0:T(8,128)(2,1)S(1)}, u32[]{:S(2)}, u32[]{:S(2)}) collective-permute-start(bf16[1,96,256]{2,1,0:T(8,128)(2,1)S(1)} %collective-permute-done.9), channel_id=1, source_target_pairs={{0,24},{1,25},{2,26},{3,27},{4,12},{5,13},{6,14},{7,15},{8,16},{9,... | collective-permute-start | bytes 147464 | tf_op jit(solution)/shard_map/ppermute | solution.py:116
  32.5 7.5 %collective-permute-start.22 = (bf16[4,80,256]{2,1,0:T(8,128)(2,1)S(1)}, bf16[4,80,256]{2,1,0:T(8,128)(2,1)S(1)}, u32[]{:S(2)}, u32[]{:S(2)}) collective-permute-start(bf16[4,80,256]{2,1,0:T(8,128)(2,1)S(1)} %get-tuple-element.30), channel_id=1, source_target_pairs={{0,96},{1,97},{2,98},{3,99},{4,36},{5,37},{6,38},{7,39},{8,104},{9... | collective-permute-start | bytes 491528 | tf_op jit(solution)/shard_map/ppermute | solution.py:115
  34.1 5.3 %collective-permute-start.21 = (bf16[4,80,256]{2,1,0:T(8,128)(2,1)S(1)}, bf16[4,80,256]{2,1,0:T(8,128)(2,1)S(1)}, u32[]{:S(2)}, u32[]{:S(2)}) collective-permute-start(bf16[4,80,256]{2,1,0:T(8,128)(2,1)S(1)} %get-tuple-element.30), channel_id=1, source_target_pairs={{0,32},{1,33},{2,34},{3,35},{4,100},{5,101},{6,102},{7,103},{8,40}... | collective-permute-start | bytes 491528 | tf_op jit(solution)/shard_map/ppermute | solution.py:114
  34.7 16.9 %collective-permute-start.4 = (bf16[4,96,256]{2,1,0:T(8,128)(2,1)S(1)}, bf16[4,96,256]{2,1,0:T(8,128)(2,1)S(1)}, u32[]{:S(2)}, u32[]{:S(2)}) collective-permute-start(bf16[4,96,256]{2,1,0:T(8,128)(2,1)S(1)} %get-tuple-element.22), channel_id=1, source_target_pairs={{0,24},{1,25},{2,26},{3,27},{4,12},{5,13},{6,14},{7,15},{8,16},{9,... | collective-permute-start | bytes 589832 | tf_op jit(solution)/shard_map/ppermute | solution.py:115
  37.8 5.7 %collective-permute-start.3 = (bf16[4,96,256]{2,1,0:T(8,128)(2,1)S(1)}, bf16[4,96,256]{2,1,0:T(8,128)(2,1)S(1)}, u32[]{:S(2)}, u32[]{:S(2)}) collective-permute-start(bf16[4,96,256]{2,1,0:T(8,128)(2,1)S(1)} %get-tuple-element.22), channel_id=1, source_target_pairs={{0,8},{1,9},{2,10},{3,11},{4,28},{5,29},{6,30},{7,31},{8,0},{9,1},... | collective-permute-start | bytes 589832 | tf_op jit(solution)/shard_map/ppermute | solution.py:114
  39.4 15.4 %collective-permute-start.13 = (bf16[4,96,256]{2,1,0:T(8,128)(2,1)S(1)}, bf16[4,96,256]{2,1,0:T(8,128)(2,1)S(1)}, u32[]{:S(2)}, u32[]{:S(2)}) collective-permute-start(bf16[4,96,256]{2,1,0:T(8,128)(2,1)S(1)} %get-tuple-element.14), channel_id=1, source_target_pairs={{0,3},{1,2},{2,1},{3,0},{4,5},{5,4},{6,7},{7,6},{8,11},{9,10},{10,... | collective-permute-start | bytes 589832 | tf_op jit(solution)/shard_map/ppermute | solution.py:115
  40.0 6.6 %collective-permute-start.23 = (bf16[4,80,256]{2,1,0:T(8,128)(2,1)S(1)}, bf16[4,80,256]{2,1,0:T(8,128)(2,1)S(1)}, u32[]{:S(2)}, u32[]{:S(2)}) collective-permute-start(bf16[4,80,256]{2,1,0:T(8,128)(2,1)S(1)} %collective-permute-done.21), channel_id=1, source_target_pairs={{0,96},{1,97},{2,98},{3,99},{4,36},{5,37},{6,38},{7,39},{8,104},{9... | collective-permute-start | bytes 491528 | tf_op jit(solution)/shard_map/ppermute | solution.py:116
  43.5 6.2 %collective-permute-start.12 = (bf16[4,96,256]{2,1,0:T(8,128)(2,1)S(1)}, bf16[4,96,256]{2,1,0:T(8,128)(2,1)S(1)}, u32[]{:S(2)}, u32[]{:S(2)}) collective-permute-start(bf16[4,96,256]{2,1,0:T(8,128)(2,1)S(1)} %get-tuple-element.14), channel_id=1, source_target_pairs={{0,1},{1,0},{2,3},{3,2},{4,7},{5,6},{6,5},{7,4},{8,9},{9,8},{10,11... | collective-permute-start | bytes 589832 | tf_op jit(solution)/shard_map/ppermute | solution.py:114
  46.6 9.0 %collective-permute-start.5 = (bf16[4,96,256]{2,1,0:T(8,128)(2,1)S(1)}, bf16[4,96,256]{2,1,0:T(8,128)(2,1)S(1)}, u32[]{:S(2)}, u32[]{:S(2)}) collective-permute-start(bf16[4,96,256]{2,1,0:T(8,128)(2,1)S(1)} %collective-permute-done.3), channel_id=1, source_target_pairs={{0,24},{1,25},{2,26},{3,27},{4,12},{5,13},{6,14},{7,15},{8,16},{9,... | collective-permute-start | bytes 589832 | tf_op jit(solution)/shard_map/ppermute | solution.py:116
  49.7 28.6 %copy-start = (bf16[16,80,256]{2,1,0:T(8,128)(2,1)}, bf16[16,80,256]{2,1,0:T(8,128)(2,1)S(1)}, u32[]{:S(2)}) copy-start(bf16[16,80,256]{2,1,0:T(8,128)(2,1)S(1)} %constant_dynamic-update-slice_fusion.26.refs_8_) | copy-start | bytes 1966084
  49.7 14.9 %collective-permute-start.25 = (bf16[16,80,256]{2,1,0:T(8,128)(2,1)S(1)}, bf16[16,80,256]{2,1,0:T(8,128)(2,1)S(1)}, u32[]{:S(2)}, u32[]{:S(2)}) collective-permute-start(bf16[16,80,256]{2,1,0:T(8,128)(2,1)S(1)} %constant_dynamic-update-slice_fusion.26.refs_8_), channel_id=1, source_target_pairs={{0,24},{1,25},{2,26},{3,27},{4,12},{5,13},{6,14},{7,15},{8,16},{9,... | collective-permute-start | bytes 1966088 | tf_op jit(solution)/shard_map/ppermute | solution.py:115
  51.6 9.0 %collective-permute-start.14 = (bf16[4,96,256]{2,1,0:T(8,128)(2,1)S(1)}, bf16[4,96,256]{2,1,0:T(8,128)(2,1)S(1)}, u32[]{:S(2)}, u32[]{:S(2)}) collective-permute-start(bf16[4,96,256]{2,1,0:T(8,128)(2,1)S(1)} %collective-permute-done.12), channel_id=1, source_target_pairs={{0,3},{1,2},{2,1},{3,0},{4,5},{5,4},{6,7},{7,6},{8,11},{9,10},{10,... | collective-permute-start | bytes 589832 | tf_op jit(solution)/shard_map/ppermute | solution.py:116
  55.6 22.7 %collective-permute-start.6 = (bf16[16,96,256]{2,1,0:T(8,128)(2,1)S(1)}, bf16[16,96,256]{2,1,0:T(8,128)(2,1)S(1)}, u32[]{:S(2)}, u32[]{:S(2)}) collective-permute-start(bf16[16,96,256]{2,1,0:T(8,128)(2,1)S(1)} %constant_dynamic-update-slice_fusion.4.refs_0_), channel_id=1, source_target_pairs={{0,1},{1,0},{2,3},{3,2},{4,7},{5,6},{6,5},{7,4},{8,9},{9,8},{10,11... | collective-permute-start | bytes 2359304 | tf_op jit(solution)/shard_map/ppermute | solution.py:114
  61.4 19.9 %collective-permute-start.15 = (bf16[16,96,256]{2,1,0:T(8,128)(2,1)}, bf16[16,96,256]{2,1,0:T(8,128)(2,1)}, u32[]{:S(2)}, u32[]{:S(2)}) collective-permute-start(bf16[16,96,256]{2,1,0:T(8,128)(2,1)} %constant_dynamic-update-slice_fusion.15.refs_4_), channel_id=1, source_target_pairs={{0,32},{1,33},{2,34},{3,35},{4,100},{5,101},{6,102},{7,103},{8,40}... | collective-permute-start | bytes 2359304 | tf_op jit(solution)/shard_map/ppermute | solution.py:114
  61.4 20.0 %collective-permute-start.7 = (bf16[16,96,256]{2,1,0:T(8,128)(2,1)S(1)}, bf16[16,96,256]{2,1,0:T(8,128)(2,1)S(1)}, u32[]{:S(2)}, u32[]{:S(2)}) collective-permute-start(bf16[16,96,256]{2,1,0:T(8,128)(2,1)S(1)} %constant_dynamic-update-slice_fusion.4.refs_0_), channel_id=1, source_target_pairs={{0,3},{1,2},{2,1},{3,0},{4,5},{5,4},{6,7},{7,6},{8,11},{9,10},{10,... | collective-permute-start | bytes 2359304 | tf_op jit(solution)/shard_map/ppermute | solution.py:115
  64.6 0.8 copy-start.2
  65.4 11.0 %collective-permute-start.24 = (bf16[16,80,256]{2,1,0:T(8,128)(2,1)S(1)}, bf16[16,80,256]{2,1,0:T(8,128)(2,1)}, u32[]{:S(2)}, u32[]{:S(2)}) collective-permute-start(bf16[16,80,256]{2,1,0:T(8,128)(2,1)S(1)} %constant_dynamic-update-slice_fusion.26.refs_8_), channel_id=1, source_target_pairs={{0,8},{1,9},{2,10},{3,11},{4,28},{5,29},{6,30},{7,31},{8,0},{9,1},... | collective-permute-start | bytes 1966088 | tf_op jit(solution)/shard_map/ppermute | solution.py:114
  76.4 13.5 %collective-permute-start.16 = (bf16[16,96,256]{2,1,0:T(8,128)(2,1)}, bf16[16,96,256]{2,1,0:T(8,128)(2,1)}, u32[]{:S(2)}, u32[]{:S(2)}) collective-permute-start(bf16[16,96,256]{2,1,0:T(8,128)(2,1)} %constant_dynamic-update-slice_fusion.15.refs_4_), channel_id=1, source_target_pairs={{0,96},{1,97},{2,98},{3,99},{4,36},{5,37},{6,38},{7,39},{8,104},{9... | collective-permute-start | bytes 2359304 | tf_op jit(solution)/shard_map/ppermute | solution.py:115
  78.3 15.3 %collective-permute-start.8 = (bf16[16,96,256]{2,1,0:T(8,128)(2,1)S(1)}, bf16[16,96,256]{2,1,0:T(8,128)(2,1)S(1)}, u32[]{:S(2)}, u32[]{:S(2)}) collective-permute-start(bf16[16,96,256]{2,1,0:T(8,128)(2,1)S(1)} %collective-permute-done.6.refs_1_), channel_id=1, source_target_pairs={{0,3},{1,2},{2,1},{3,0},{4,5},{5,4},{6,7},{7,6},{8,11},{9,10},{10,... | collective-permute-start | bytes 2359304 | tf_op jit(solution)/shard_map/ppermute | solution.py:116
  81.3 17.1 %collective-permute-start.17 = (bf16[16,96,256]{2,1,0:T(8,128)(2,1)}, bf16[16,96,256]{2,1,0:T(8,128)(2,1)}, u32[]{:S(2)}, u32[]{:S(2)}) collective-permute-start(bf16[16,96,256]{2,1,0:T(8,128)(2,1)} %collective-permute-done.15.refs_5_), channel_id=1, source_target_pairs={{0,96},{1,97},{2,98},{3,99},{4,36},{5,37},{6,38},{7,39},{8,104},{9... | collective-permute-start | bytes 2359304 | tf_op jit(solution)/shard_map/ppermute | solution.py:116
  81.4 12.2 %collective-permute-start.26 = (bf16[16,80,256]{2,1,0:T(8,128)(2,1)}, bf16[16,80,256]{2,1,0:T(8,128)(2,1)}, u32[]{:S(2)}, u32[]{:S(2)}) collective-permute-start(bf16[16,80,256]{2,1,0:T(8,128)(2,1)} %collective-permute-done.24.refs_9_), channel_id=1, source_target_pairs={{0,24},{1,25},{2,26},{3,27},{4,12},{5,13},{6,14},{7,15},{8,16},{9,... | collective-permute-start | bytes 1966088 | tf_op jit(solution)/shard_map/ppermute | solution.py:116
  98.3 1.1 copy-start.1
  99.4 1.1 copy-start.3

commit v3 on v2

--- a/solution.py
+++ b/solution.py
@@ -22,8 +22,9 @@
 
 MAIN = ("x", "y", "c", "z")
 NODE = ("x", "y", "z")
-ORDERS = ("xyz", "yzx", "zxy")
-PLACE = {"x": 0, "y": 1, "z": 2}
+WHOLE = (("z", True), ("x", True), ("y", False))
+LATE = (("y", True), ("z", False), ("x", False))
+GROUP = 8
 
 
 def exchange_pairs(axis, near):
@@ -49,24 +50,20 @@
     return values * lax.rsqrt(squares + epsilon)
 
 
-def pack_kernel(query_ref, ids_ref, out0_ref, out1_ref, out2_ref):
-    maps = unit(query_ref[0].astype(f32)).T.astype(bf16)
+def pack_kernel(query_ref, ids_ref, out_ref):
+    out_ref[0, 16:, :] = unit(query_ref[0].astype(f32)).T.astype(bf16)
     ids = ids_ref[...]
     high = lax.shift_right_logical(ids, 6).astype(f32)
     low = (ids & 63).astype(f32)
     row = jnp.concatenate([high, low], axis=1)
     first = lax.broadcasted_iota(jnp.int32, (16, 2 * CAND), 0) == 0
-    out0_ref[0, :16, :] = jnp.where(first, jnp.broadcast_to(row, first.shape), 0.0).astype(bf16)
-    out0_ref[0, 16:, :] = maps[: CUTS[1]]
-    out1_ref[0] = maps[CUTS[1] : CUTS[2]]
-    out2_ref[0] = maps[CUTS[2] :]
+    out_ref[0, :16, :] = jnp.where(first, jnp.broadcast_to(row, first.shape), 0.0).astype(bf16)
 
 
 def pack(query_maps, shortlist):
-    rows = (CUTS[1] + 16, CUTS[2] - CUTS[1], CUTS[3] - CUTS[2])
     return pl.pallas_call(
         pack_kernel,
-        out_shape=tuple(jax.ShapeDtypeStruct((1, r, CELLS), bf16) for r in rows),
+        out_shape=jax.ShapeDtypeStruct((1, CELLS + 16, CELLS), bf16),
     )(query_maps, shortlist)
 
 
@@ -85,10 +82,11 @@
             down = lax.shift_right_logical(source, 4) - lax.shift_right_logical(result, 4)
             right = (source & (GRID - 1)) - (result & (GRID - 1))
             matrix = jnp.zeros((CELLS, CELLS), f32)
+            taps = tap_ref[...].astype(f32)
             for i in range(3):
                 for j in range(3):
                     hit = (down == i - 1) & (right == j - 1)
-                    matrix = jnp.where(hit, tap_ref[i, j], matrix)
+                    matrix = jnp.where(hit, taps[i : i + 1, j : j + 1], matrix)
             out_ref[...] = matrix.astype(bf16)
 
 
@@ -96,27 +94,33 @@
     block = 4
     maps = pl.BlockSpec((block, CELLS, CELLS), lambda i: (i, 0, 0))
     square = pl.BlockSpec((CELLS, CELLS), lambda i: (0, 0))
-    smem = pl.BlockSpec(memory_space=pltpu.SMEM)
+    taps = pl.BlockSpec((3, 3), lambda i: (0, 0))
     square_shape = jax.ShapeDtypeStruct((CELLS, CELLS), bf16)
     return pl.pallas_call(
         images_kernel,
         grid=(database.shape[0] // block,),
-        in_specs=[smem, smem, maps],
+        in_specs=[taps, taps, maps],
         out_specs=(maps, square, square),
         out_shape=(jax.ShapeDtypeStruct(database.shape, bf16), square_shape, square_shape),
     )(tap_q, tap_d, database)
 
 
-def spread(chunks):
-    held = list(chunks)
-    for phase in range(3):
-        axes = [order[phase] for order in ORDERS]
-        near = [lax.ppermute(m, MAIN, PAIRS[axis, True]) for m, axis in zip(held, axes)]
-        far = [lax.ppermute(m, MAIN, PAIRS[axis, False]) for m, axis in zip(held, axes)]
-        both = [lax.ppermute(m, MAIN, PAIRS[axis, False]) for m, axis in zip(near, axes)]
-        parts = list(zip(held, near, far, both))
-        held = [jnp.concatenate(part, axis=0) for part in parts] if phase < 2 else parts
-    return held
+def move(array, step):
+    return lax.ppermute(array, MAIN, PAIRS[step])
+
+
+def spread(held):
+    pieces = []
+    for piece in range(3):
+        first = CUTS[piece] + (16 if piece else 0)
+        pieces.append(held[:, first : CUTS[piece + 1] + 16])
+    order = [(LATE[piece % 3], LATE[(piece + 1) % 3], LATE[(piece + 2) % 3]) for piece in (0, 2, 1)]
+    came = [move(p, o[0]) for p, o in zip(pieces, order)]
+    pieces = [jnp.concatenate(pair, axis=0) for pair in zip(pieces, came)]
+    second = [move(p, o[1]) for p, o in zip(pieces, order)]
+    third = [move(p, o[2]) for p, o in zip(pieces, order)]
+    fourth = [move(p, o[2]) for p, o in zip(second, order)]
+    return [list(part) for part in zip(pieces, second, third, fourth)]
 
 
 def pair_kernel(
@@ -126,30 +130,27 @@
     own_hbm, other_hbm, conv_q_ref, conv_d_ref, out_ref = refs[:5]
     query_v, image_v, ids_v, table_v, column_v, peak_v, total_v, table_s, pair_s, sems = refs[5:]
     id_copies, copies = [], []
-    for piece, order in enumerate(ORDERS):
-        size = CUTS[piece + 1] - CUTS[piece]
-        skip = 16 if piece == 0 else 0
-        for last in range(4):
-            for middle in range(4):
-                index = [0, 0, 0]
-                index[PLACE[order[0]]] = slice(None)
-                index[PLACE[order[1]]] = middle
-                index[PLACE[order[2]]] = last
-                source = parts[4 * piece + last]
-                blocks = pl.ds(4 * middle, 4)
-                copies.append(
+    for combo in range(8):
+        bits = (combo & 1, combo >> 1 & 1, combo >> 2)
+        here = pl.ds(GROUP * combo, GROUP)
+        for piece, turn in enumerate((0, 2, 1)):
+            source = parts[4 * piece + bits[(turn + 1) % 3] + 2 * bits[(turn + 2) % 3]]
+            blocks = pl.ds(GROUP * bits[turn], GROUP)
+            size = CUTS[piece + 1] - CUTS[piece]
+            skip = 0 if piece else 16
+            copies.append(
+                pltpu.make_async_copy(
+                    source.at[blocks, pl.ds(skip, size), :],
+                    query_v.at[here, pl.ds(CUTS[piece], size), :],
+                    sems.at[1],
+                )
+            )
+            if piece == 0:
+                id_copies.append(
                     pltpu.make_async_copy(
-                        source.at[blocks, pl.ds(skip, size), :],
-                        query_v.at[*index, pl.ds(CUTS[piece], size), :],
-                        sems.at[1],
+                        source.at[blocks, pl.ds(0, 16), :], ids_v.at[here], sems.at[0]
                     )
                 )
-                if piece == 0:
-                    id_copies.append(
-                        pltpu.make_async_copy(
-                            source.at[blocks, pl.ds(0, 16), :], ids_v.at[*index], sems.at[0]
-                        )
-                    )
     image_copies = [
         pltpu.make_async_copy(own_hbm, image_v.at[pl.ds(0, IMAGES)], sems.at[2]),
         pltpu.make_async_copy(other_hbm, image_v.at[pl.ds(IMAGES, IMAGES)], sems.at[3]),
@@ -157,7 +158,7 @@
     for copy in id_copies + image_copies + copies:
         copy.start()
     pltpu.make_async_copy(ids_v, ids_v, sems.at[0]).wait()
-    packed = jnp.sum(ids_v[...].reshape(NODES, 16, CELLS).astype(f32), axis=1)
+    packed = jnp.sum(ids_v[...].astype(f32), axis=1)
     ids = packed[:, :CAND].astype(jnp.int32) * 64 + packed[:, CAND:].astype(jnp.int32)
     lane = lax.broadcasted_iota(jnp.int32, (NODES, CAND), 1)
     shard = lax.shift_right_logical(ids, 5)
@@ -198,11 +199,8 @@
         for part in range(UNROLL):
             code = pair_s[step * UNROLL + part]
             node = lax.shift_right_logical(code, 16)
-            query = query_v[
-                lax.shift_right_logical(node, 4), lax.shift_right_logical(node, 2) & 3, node & 3
-            ]
             image = code & 63
-            correlation = jnp.dot(query, image_v[image], preferred_element_type=f32)
+            correlation = jnp.dot(query_v[node], image_v[image], preferred_element_type=f32)
             rectified = jnp.maximum(correlation, 0.0).astype(bf16)
             found.append((lax.shift_right_logical(code, 6) & 1023, rectified))
         for row, rectified in found:
@@ -236,9 +234,9 @@
         in_specs=[smem] + [hbm] * 14 + [vmem, vmem],
         out_specs=vmem,
         scratch_shapes=[
-            pltpu.VMEM((4, 4, 4, CELLS, CELLS), bf16),
+            pltpu.VMEM((NODES, CELLS, CELLS), bf16),
             pltpu.VMEM((2 * IMAGES, CELLS, CELLS), bf16),
-            pltpu.VMEM((4, 4, 4, 16, CELLS), bf16),
+            pltpu.VMEM((NODES, 16, CELLS), bf16),
             pltpu.VMEM((NODES, CAND), jnp.int32),
             pltpu.VMEM((4, NODES, CAND), jnp.int32),
             pltpu.VMEM((4 * NODES + 8, CELLS), f32),
@@ -274,23 +272,31 @@
     )(parts)
 
 
+def place_table():
+    me = lax.axis_index("c")
+    x, y, z = [lax.axis_index(axis) for axis in NODE]
+    base = (x * 4 + y) * 8 + z
+    near = jnp.where(me == 0, 1, 3)
+    far = 4 - near
+    index = jnp.arange(NODES, dtype=jnp.int32)
+    bit = [lax.shift_right_logical(index, k) & 1 for k in range(6)]
+    z = z ^ (bit[0] * near) ^ (bit[4] * far)
+    x = x ^ (bit[1] * near) ^ (bit[5] * far)
+    y = y ^ (bit[2] * far) ^ (bit[3] * near)
+    shards = jnp.stack([base + 4 * me, base + 4 * (1 - me)])
+    return jnp.concatenate([shards, (x * 4 + y) * 4 + z]).astype(jnp.int32)
+
+
 def body(query_maps, database, shortlist, kernel_query, kernel_db):
-    chunks = pack(query_maps, shortlist)
-    own, conv_q, conv_d = prepare_images(database, kernel_query.astype(f32), kernel_db.astype(f32))
+    held = pack(query_maps, shortlist)
+    for count, step in enumerate(WHOLE):
+        held = jnp.concatenate([held, move(held, step)], axis=0)
+        if count == 1:
+            database, held = lax.optimization_barrier((database, held))
+    own, conv_q, conv_d = prepare_images(database, kernel_query, kernel_db)
     other = lax.ppermute(own, "c", [(0, 1), (1, 0)])
-    parts = spread(chunks)
-    me = lax.axis_index("c")
-    at = [lax.axis_index(axis) for axis in NODE]
-    base = (at[0] * 4 + at[1]) * 8 + at[2]
-    step = jnp.arange(4, dtype=jnp.int32)
-    offset = jnp.where(me == 0, step ^ lax.shift_right_logical(step, 1), (4 - step) & 3)
-    offset = jnp.where((me == 1) & (step > 0), jnp.where(step == 1, 3, jnp.where(step == 2, 1, 2)), offset)
-    spot = [a ^ offset for a in at]
-    order = (spot[0][:, None, None] * 4 + spot[1][None, :, None]) * 4 + spot[2][None, None, :]
-    place = jnp.concatenate(
-        [jnp.stack([base + 4 * me, base + 4 * (1 - me)]), order.reshape(-1)]
-    ).astype(jnp.int32)
-    scores = pair_scores(place, [p for part in parts for p in part], own, other, conv_q, conv_d)
+    parts = [p for part in spread(held) for p in part]
+    scores = pair_scores(place_table(), parts, own, other, conv_q, conv_d)
     scores = lax.all_to_all(scores, NODE, split_axis=0, concat_axis=0, tiled=True)
     return finish(scores)
 

time: 150 us -> 134 us (0.89)
  starting transfers between devices: 42.2 us -> 29.1 us
  local copies, waits for them, and re-layouts: 9.39 us -> 2.1 us
  waiting for transfers between devices: 36.2 us -> 41.6 us
  blocking collectives: 25.2 us -> 21 us
  Pallas kernels: 31.5 us -> 34.6 us
    ppermute x27 -> x15, starting transfers between devices: 42.1 us -> 28 us  [move(): return lax.ppermute(array, MAIN, PAIRS[step])]
    unnamed x26 -> x9, local copies, waits for them, and re-layouts: 7.95 us -> 1.96 us
    ppermute x27 -> x15, waiting for transfers between devices: 36.2 us -> 41.6 us  [move(): return lax.ppermute(array, MAIN, PAIRS[step])]
    all_to_all x1, blocking collectives: 25.2 us -> 21 us  [body(): lax.all_to_all(scores, NODE, split_axis=0, concat_axis=0, tiled=True)]
    concatenate x1 -> x6, other arithmetic: 0.08 us -> 3.13 us  [the longest x2 1.9 us: body(): held = jnp.concatenate([held, move(held, step)], axis=0)]
    pallas_call x1, Pallas kernels: 20.8 us -> 23.8 us  [pair_scores(): pl.pallas_call(pair_kernel, out_shape=jax.ShapeDtypeStruct((NODES, CAND),...]
    convert_element_type x2 -> x0, other arithmetic: 2.51 us -> none  [the longest x1 1.26 us: body(): kernel_db.astype(f32)]
  transfers between devices with their start and end apart: 28 -> 16, of which waited for: 9 -> 12; matrix products, arithmetic and copies ran while one was open for 4% -> 1% of each run, Pallas kernels for 1% -> 0%
where the time goes in v3:
time: 134 us; the launch traced here: 132 us
  waiting for transfers between devices  41.6 us (31%)
  Pallas kernels  34.6 us (26%)
  starting transfers between devices  29.1 us (22%)
  blocking collectives  21 us (16%)
  other arithmetic  3.14 us (2%)
  local copies, waits for them, and re-layouts  2.1 us (2%)
    ppermute x15, waiting for transfers between devices, move(): return lax.ppermute(array, MAIN, PAIRS[step])  41.6 us
    ppermute x15, starting transfers between devices, move(): return lax.ppermute(array, MAIN, PAIRS[step])  28 us
    pallas_call x1, Pallas kernels, pair_scores(): pl.pallas_call(pair_kernel, out_shape=jax.ShapeDtypeStruct((NODES, CAND),...  23.8 us
    all_to_all x1, blocking collectives, body(): lax.all_to_all(scores, NODE, split_axis=0, concat_axis=0, tiled=True)  21 us
    pallas_call x1, Pallas kernels, prepare_images(): pl.pallas_call(images_kernel, grid=(database.shape[0] // block,), in_spec...  7.57 us
  transfers between devices with their start and end apart: 16, of which 12 were waited for; matrix products, arithmetic and copies ran while one was open for 1% of the time, Pallas kernels for 0%

profile of v3, /device:TPU:0, one launch (start us, length us, event | category | flops | bytes accessed | tf_op | source)
XLA Modules:
  0.0 132.3 jit_solution(1061297452739813824)
XLA Ops:
  0.6 1.7 %shard_map.68 = bf16[1,272,256]{2,1,0:T(8,128)(2,1)} custom-call(bf16[1,256,256]{2,1,0:T(8,128)(2,1)} %query_ref.1, s32[1,128]{1,0:T(1,128)} %ids_ref.1), custom_call_target="tpu_custom_call" | custom-call | tf_op jit(solution)/shard_map/pallas_call | solution.py:64
  2.3 2.0 %collective-permute-start = (bf16[1,272,256]{2,1,0:T(8,128)(2,1)}, bf16[1,272,256]{2,1,0:T(8,128)(2,1)S(1)}, u32[]{:S(2)}, u32[]{:S(2)}) collective-permute-start(bf16[1,272,256]{2,1,0:T(8,128)(2,1)} %shard_map.68), channel_id=1, source_target_pairs={{0,1},{1,0},{2,3},{3,2},{4,7},{5,6},{6,5},{7,4},{8,9},{9,8},{10,11... | collective-permute-start | bytes 417800 | tf_op jit(solution)/shard_map/ppermute | solution.py:109
  4.3 3.3 %collective-permute-done = bf16[1,272,256]{2,1,0:T(8,128)(2,1)S(1)} collective-permute-done((bf16[1,272,256]{2,1,0:T(8,128)(2,1)}, bf16[1,272,256]{2,1,0:T(8,128)(2,1)S(1)}, u32[]{:S(2)}, u32[]{:S(2)}) %collective-permute-start) | collective-permute-done | bytes 139296 | tf_op jit(solution)/shard_map/ppermute | solution.py:109
  7.6 0.9 pad_maximum_fusion.4
  8.5 1.7 %collective-permute-start.1 = (bf16[2,272,256]{2,1,0:T(8,128)(2,1)S(1)}, bf16[2,272,256]{2,1,0:T(8,128)(2,1)S(1)}, u32[]{:S(2)}, u32[]{:S(2)}) collective-permute-start(bf16[2,272,256]{2,1,0:T(8,128)(2,1)S(1)} %pad_maximum_fusion.4), channel_id=1, source_target_pairs={{0,32},{1,33},{2,34},{3,35},{4,100},{5,101},{6,102},{7,103},{8,40}... | collective-permute-start | bytes 835592 | tf_op jit(solution)/shard_map/ppermute | solution.py:109
  10.2 5.0 %collective-permute-done.1 = bf16[2,272,256]{2,1,0:T(8,128)(2,1)S(1)} collective-permute-done((bf16[2,272,256]{2,1,0:T(8,128)(2,1)S(1)}, bf16[2,272,256]{2,1,0:T(8,128)(2,1)S(1)}, u32[]{:S(2)}, u32[]{:S(2)}) %collective-permute-start.1) | collective-permute-done | bytes 278560 | tf_op jit(solution)/shard_map/ppermute | solution.py:109
  15.2 1.0 pad_maximum_fusion.3
  16.1 7.6 %shard_map.69 = (bf16[32,256,256]{2,1,0:T(8,128)(2,1)}, bf16[256,256]{1,0:T(8,128)(2,1)}, bf16[256,256]{1,0:T(8,128)(2,1)}) custom-call(bf16[3,3]{1,0:T(4,128)(2,1)} %tap_q_ref.1, bf16[3,3]{1,0:T(4,128)(2,1)} %tap_d_ref.1, bf16[32,256,256]{2,1,0:T(8,128)(2,1)} %maps_ref), custom_call_target="tpu_custom_call" | custom-call | tf_op jit(solution)/shard_map/pallas_call | solution.py:99
  23.7 1.1 collective-permute-start.15
  24.8 3.0 %collective-permute-start.2 = (bf16[4,272,256]{2,1,0:T(8,128)(2,1)S(1)}, bf16[4,272,256]{2,1,0:T(8,128)(2,1)S(1)}, u32[]{:S(2)}, u32[]{:S(2)}) collective-permute-start(bf16[4,272,256]{2,1,0:T(8,128)(2,1)S(1)} %pad_maximum_fusion.3), channel_id=1, source_target_pairs={{0,24},{1,25},{2,26},{3,27},{4,12},{5,13},{6,14},{7,15},{8,16},{9,... | collective-permute-start | bytes 1671176 | tf_op jit(solution)/shard_map/ppermute | solution.py:109
  27.9 7.7 %collective-permute-done.2 = bf16[4,272,256]{2,1,0:T(8,128)(2,1)S(1)} collective-permute-done((bf16[4,272,256]{2,1,0:T(8,128)(2,1)S(1)}, bf16[4,272,256]{2,1,0:T(8,128)(2,1)S(1)}, u32[]{:S(2)}, u32[]{:S(2)}) %collective-permute-start.2) | collective-permute-done | bytes 557088 | tf_op jit(solution)/shard_map/ppermute | solution.py:109
  35.6 3.2 %collective-permute-start.11 = (bf16[8,80,256]{2,1,0:T(8,128)(2,1)S(1)}, bf16[8,80,256]{2,1,0:T(8,128)(2,1)S(1)}, u32[]{:S(2)}, u32[]{:S(2)}) collective-permute-start(bf16[8,80,256]{2,1,0:T(8,128)(2,1)S(1)} %slice.14), channel_id=1, source_target_pairs={{0,3},{1,2},{2,1},{3,0},{4,5},{5,4},{6,7},{7,6},{8,11},{9,10},{10,... | collective-permute-start | bytes 983048 | tf_op jit(solution)/shard_map/ppermute | solution.py:109
  38.8 0.1 fusion
  38.9 0.4 collective-permute-start.3
  39.3 2.8 %collective-permute-start.7 = (bf16[8,96,256]{2,1,0:T(8,128)(2,1)S(1)}, bf16[8,96,256]{2,1,0:T(8,128)(2,1)S(1)}, u32[]{:S(2)}, u32[]{:S(2)}) collective-permute-start(bf16[8,96,256]{2,1,0:T(8,128)(2,1)S(1)} %get-tuple-element.12), channel_id=1, source_target_pairs={{0,96},{1,97},{2,98},{3,99},{4,36},{5,37},{6,38},{7,39},{8,104},{9... | collective-permute-start | bytes 1179656 | tf_op jit(solution)/shard_map/ppermute | solution.py:109
  42.1 1.9 %collective-permute-done.11 = bf16[8,80,256]{2,1,0:T(8,128)(2,1)S(1)} collective-permute-done((bf16[8,80,256]{2,1,0:T(8,128)(2,1)S(1)}, bf16[8,80,256]{2,1,0:T(8,128)(2,1)S(1)}, u32[]{:S(2)}, u32[]{:S(2)}) %collective-permute-start.11) | collective-permute-done | bytes 327712 | tf_op jit(solution)/shard_map/ppermute | solution.py:109
  44.0 0.1 pad_maximum_fusion.2.refs_8_
  44.1 0.4 collective-permute-start.13
  44.5 2.2 %collective-permute-done.3 = bf16[8,96,256]{2,1,0:T(8,128)(2,1)S(1)} collective-permute-done((bf16[8,96,256]{2,1,0:T(8,128)(2,1)S(1)}, bf16[8,96,256]{2,1,0:T(8,128)(2,1)S(1)}, u32[]{:S(2)}, u32[]{:S(2)}) %collective-permute-start.3) | collective-permute-done | bytes 393248 | tf_op jit(solution)/shard_map/ppermute | solution.py:109
  46.7 0.1 pad_maximum_fusion.refs_0_
  46.8 0.0 copy-start.2
  46.8 0.0 copy-start.3
  46.8 0.9 collective-permute-start.4
  47.8 0.5 collective-permute-done.7
  48.3 1.0 pad_maximum_fusion.1.refs_4_
  49.3 1.7 %collective-permute-start.8 = (bf16[16,96,256]{2,1,0:T(8,128)(2,1)}, bf16[16,96,256]{2,1,0:T(8,128)(2,1)}, u32[]{:S(2)}, u32[]{:S(2)}) collective-permute-start(bf16[16,96,256]{2,1,0:T(8,128)(2,1)} %pad_maximum_fusion.1.refs_4_), channel_id=1, source_target_pairs={{0,8},{1,9},{2,10},{3,11},{4,28},{5,29},{6,30},{7,31},{8,0},{9,1},... | collective-permute-start | bytes 2359304 | tf_op jit(solution)/shard_map/ppermute | solution.py:109
  51.0 2.8 %collective-permute-start.12 = (bf16[16,80,256]{2,1,0:T(8,128)(2,1)S(1)}, bf16[16,80,256]{2,1,0:T(8,128)(2,1)}, u32[]{:S(2)}, u32[]{:S(2)}) collective-permute-start(bf16[16,80,256]{2,1,0:T(8,128)(2,1)S(1)} %pad_maximum_fusion.2.refs_8_), channel_id=1, source_target_pairs={{0,96},{1,97},{2,98},{3,99},{4,36},{5,37},{6,38},{7,39},{8,104},{9... | collective-permute-start | bytes 1966088 | tf_op jit(solution)/shard_map/ppermute | solution.py:109
  53.8 1.0 collective-permute-done.13.refs_10_
  54.7 0.0 copy-start
  54.7 0.8 copy-done
  55.6 2.8 %collective-permute-start.5 = (bf16[16,96,256]{2,1,0:T(8,128)(2,1)S(1)}, bf16[16,96,256]{2,1,0:T(8,128)(2,1)S(1)}, u32[]{:S(2)}, u32[]{:S(2)}) collective-permute-start(bf16[16,96,256]{2,1,0:T(8,128)(2,1)S(1)} %pad_maximum_fusion.refs_0_), channel_id=1, source_target_pairs={{0,96},{1,97},{2,98},{3,99},{4,36},{5,37},{6,38},{7,39},{8,104},{9... | collective-permute-start | bytes 2359304 | tf_op jit(solution)/shard_map/ppermute | solution.py:109
  58.3 4.6 %collective-permute-done.12.refs_9_ = bf16[16,80,256]{2,1,0:T(8,128)(2,1)} collective-permute-done((bf16[16,80,256]{2,1,0:T(8,128)(2,1)S(1)}, bf16[16,80,256]{2,1,0:T(8,128)(2,1)}, u32[]{:S(2)}, u32[]{:S(2)}) %collective-permute-start.12) | collective-permute-done | bytes 655392 | tf_op jit(solution)/shard_map/ppermute | solution.py:109
  62.9 0.5 collective-permute-start.9
  63.5 0.0 collective-permute-done.4.refs_1_
  63.5 2.8 %collective-permute-start.6 = (bf16[16,96,256]{2,1,0:T(8,128)(2,1)S(1)}, bf16[16,96,256]{2,1,0:T(8,128)(2,1)}, u32[]{:S(2)}, u32[]{:S(2)}) collective-permute-start(bf16[16,96,256]{2,1,0:T(8,128)(2,1)S(1)} %collective-permute-done.4.refs_1_), channel_id=1, source_target_pairs={{0,96},{1,97},{2,98},{3,99},{4,36},{5,37},{6,38},{7,39},{8,104},{9... | collective-permute-start | bytes 2359304 | tf_op jit(solution)/shard_map/ppermute | solution.py:109
  66.2 0.0 collective-permute-done.8.refs_5_
  66.2 2.7 %collective-permute-start.10 = (bf16[16,96,256]{2,1,0:T(8,128)(2,1)}, bf16[16,96,256]{2,1,0:T(8,128)(2,1)}, u32[]{:S(2)}, u32[]{:S(2)}) collective-permute-start(bf16[16,96,256]{2,1,0:T(8,128)(2,1)} %collective-permute-done.8.refs_5_), channel_id=1, source_target_pairs={{0,3},{1,2},{2,1},{3,0},{4,5},{5,4},{6,7},{7,6},{8,11},{9,10},{10,... | collective-permute-start | bytes 2359304 | tf_op jit(solution)/shard_map/ppermute | solution.py:109
  68.9 2.3 %collective-permute-done.5.refs_2_ = bf16[16,96,256]{2,1,0:T(8,128)(2,1)S(1)} collective-permute-done((bf16[16,96,256]{2,1,0:T(8,128)(2,1)S(1)}, bf16[16,96,256]{2,1,0:T(8,128)(2,1)S(1)}, u32[]{:S(2)}, u32[]{:S(2)}) %collective-permute-start.5) | collective-permute-done | bytes 786464 | tf_op jit(solution)/shard_map/ppermute | solution.py:109
  71.2 0.4 collective-permute-start.14
  71.6 0.1 pad_add_fusion.place_ref
  71.7 4.7 %collective-permute-done.9.refs_6_ = bf16[16,96,256]{2,1,0:T(8,128)(2,1)} collective-permute-done((bf16[16,96,256]{2,1,0:T(8,128)(2,1)}, bf16[16,96,256]{2,1,0:T(8,128)(2,1)}, u32[]{:S(2)}, u32[]{:S(2)}) %collective-permute-start.9) | collective-permute-done | bytes 786464 | tf_op jit(solution)/shard_map/ppermute | solution.py:109
  76.4 5.7 %collective-permute-done.14.refs_11_ = bf16[16,80,256]{2,1,0:T(8,128)(2,1)} collective-permute-done((bf16[16,80,256]{2,1,0:T(8,128)(2,1)}, bf16[16,80,256]{2,1,0:T(8,128)(2,1)}, u32[]{:S(2)}, u32[]{:S(2)}) %collective-permute-start.14) | collective-permute-done | bytes 655392 | tf_op jit(solution)/shard_map/ppermute | solution.py:109
  82.1 0.0 collective-permute-done.6.refs_3_
  82.1 2.7 %collective-permute-done.10.refs_7_ = bf16[16,96,256]{2,1,0:T(8,128)(2,1)} collective-permute-done((bf16[16,96,256]{2,1,0:T(8,128)(2,1)}, bf16[16,96,256]{2,1,0:T(8,128)(2,1)}, u32[]{:S(2)}, u32[]{:S(2)}) %collective-permute-start.10) | collective-permute-done | bytes 786464 | tf_op jit(solution)/shard_map/ppermute | solution.py:109
  84.9 0.0 collective-permute-done.15.refs_13_
  84.9 0.0 copy-done.2
  84.9 0.0 copy-done.3
  84.9 0.0 copy-start.1
  84.9 1.1 copy-done.1
  86.0 23.8 %shard_map.70 = f32[64,128]{1,0:T(8,128)S(1)} custom-call(s32[66]{0:T(128)S(1)} %pad_add_fusion.place_ref, bf16[16,96,256]{2,1,0:T(8,128)(2,1)S(1)} %pad_maximum_fusion.refs_0_, bf16[16,96,256]{2,1,0:T(8,128)(2,1)S(1)} %collective-permute-done.4.refs_1_, bf16[16,96,256]{2,1,0:T(8,128)(2,1)S(1)} %collective-permute-done.5.refs_2_, ...), custom_call_target="tpu_custom_call" | custom-call | tf_op jit(solution)/shard_map/pallas_call | solution.py:231
  109.8 21.0 %all_to_all.11 = f32[64,1,128]{2,1,0:T(1,128)} all-to-all(f32[64,1,128]{2,1,0:T(1,128)S(1)} %bitcast.6), channel_id=1, replica_groups=mesh['x'=4,'y'=4,'c'=2,'z'=4] {'x','y','z'}, dimensions={0} | all-to-all | bytes 65536 | tf_op jit(solution)/shard_map/all_to_all | solution.py:300
  130.8 1.5 %shard_map.71 = (f32[1,128]{1,0:T(1,128)}, f32[1,100]{1,0:T(1,128)}) custom-call(f32[64,128]{1,0:T(8,128)} %bitcast.7), custom_call_target="tpu_custom_call" | custom-call | tf_op jit(solution)/shard_map/pallas_call | solution.py:266
  (4 shorter events, 0.1 us)
Async XLA Ops:
  2.3 5.3 %collective-permute-start = (bf16[1,272,256]{2,1,0:T(8,128)(2,1)}, bf16[1,272,256]{2,1,0:T(8,128)(2,1)S(1)}, u32[]{:S(2)}, u32[]{:S(2)}) collective-permute-start(bf16[1,272,256]{2,1,0:T(8,128)(2,1)} %shard_map.68), channel_id=1, source_target_pairs={{0,1},{1,0},{2,3},{3,2},{4,7},{5,6},{6,5},{7,4},{8,9},{9,8},{10,11... | collective-permute-start | bytes 417800 | tf_op jit(solution)/shard_map/ppermute | solution.py:109
  8.5 6.6 %collective-permute-start.1 = (bf16[2,272,256]{2,1,0:T(8,128)(2,1)S(1)}, bf16[2,272,256]{2,1,0:T(8,128)(2,1)S(1)}, u32[]{:S(2)}, u32[]{:S(2)}) collective-permute-start(bf16[2,272,256]{2,1,0:T(8,128)(2,1)S(1)} %pad_maximum_fusion.4), channel_id=1, source_target_pairs={{0,32},{1,33},{2,34},{3,35},{4,100},{5,101},{6,102},{7,103},{8,40}... | collective-permute-start | bytes 835592 | tf_op jit(solution)/shard_map/ppermute | solution.py:109
  23.7 61.2 %collective-permute-start.15 = (bf16[32,256,256]{2,1,0:T(8,128)(2,1)}, bf16[32,256,256]{2,1,0:T(8,128)(2,1)}, u32[]{:S(2)}, u32[]{:S(2)}) collective-permute-start(bf16[32,256,256]{2,1,0:T(8,128)(2,1)} %get-tuple-element.9.refs_12_), channel_id=1, source_target_pairs={{0,4},{4,0},{1,5},{5,1},{2,6},{6,2},{3,7},{7,3},{8,12},{12,8},{9,1... | collective-permute-start | bytes 12582920 | tf_op jit(solution)/shard_map/ppermute | solution.py:297
  24.8 10.7 %collective-permute-start.2 = (bf16[4,272,256]{2,1,0:T(8,128)(2,1)S(1)}, bf16[4,272,256]{2,1,0:T(8,128)(2,1)S(1)}, u32[]{:S(2)}, u32[]{:S(2)}) collective-permute-start(bf16[4,272,256]{2,1,0:T(8,128)(2,1)S(1)} %pad_maximum_fusion.3), channel_id=1, source_target_pairs={{0,24},{1,25},{2,26},{3,27},{4,12},{5,13},{6,14},{7,15},{8,16},{9,... | collective-permute-start | bytes 1671176 | tf_op jit(solution)/shard_map/ppermute | solution.py:109
  35.6 8.4 %collective-permute-start.11 = (bf16[8,80,256]{2,1,0:T(8,128)(2,1)S(1)}, bf16[8,80,256]{2,1,0:T(8,128)(2,1)S(1)}, u32[]{:S(2)}, u32[]{:S(2)}) collective-permute-start(bf16[8,80,256]{2,1,0:T(8,128)(2,1)S(1)} %slice.14), channel_id=1, source_target_pairs={{0,3},{1,2},{2,1},{3,0},{4,5},{5,4},{6,7},{7,6},{8,11},{9,10},{10,... | collective-permute-start | bytes 983048 | tf_op jit(solution)/shard_map/ppermute | solution.py:109
  38.9 7.9 %collective-permute-start.3 = (bf16[8,96,256]{2,1,0:T(8,128)(2,1)S(1)}, bf16[8,96,256]{2,1,0:T(8,128)(2,1)S(1)}, u32[]{:S(2)}, u32[]{:S(2)}) collective-permute-start(bf16[8,96,256]{2,1,0:T(8,128)(2,1)S(1)} %get-tuple-element.13), channel_id=1, source_target_pairs={{0,8},{1,9},{2,10},{3,11},{4,28},{5,29},{6,30},{7,31},{8,0},{9,1},... | collective-permute-start | bytes 1179656 | tf_op jit(solution)/shard_map/ppermute | solution.py:109
  39.3 9.0 %collective-permute-start.7 = (bf16[8,96,256]{2,1,0:T(8,128)(2,1)S(1)}, bf16[8,96,256]{2,1,0:T(8,128)(2,1)S(1)}, u32[]{:S(2)}, u32[]{:S(2)}) collective-permute-start(bf16[8,96,256]{2,1,0:T(8,128)(2,1)S(1)} %get-tuple-element.12), channel_id=1, source_target_pairs={{0,96},{1,97},{2,98},{3,99},{4,36},{5,37},{6,38},{7,39},{8,104},{9... | collective-permute-start | bytes 1179656 | tf_op jit(solution)/shard_map/ppermute | solution.py:109
  44.1 10.7 %collective-permute-start.13 = (bf16[16,80,256]{2,1,0:T(8,128)(2,1)S(1)}, bf16[16,80,256]{2,1,0:T(8,128)(2,1)S(1)}, u32[]{:S(2)}, u32[]{:S(2)}) collective-permute-start(bf16[16,80,256]{2,1,0:T(8,128)(2,1)S(1)} %pad_maximum_fusion.2.refs_8_), channel_id=1, source_target_pairs={{0,8},{1,9},{2,10},{3,11},{4,28},{5,29},{6,30},{7,31},{8,0},{9,1},... | collective-permute-start | bytes 1966088 | tf_op jit(solution)/shard_map/ppermute | solution.py:109
  46.8 38.0 %copy-start.2 = (bf16[256,256]{1,0:T(8,128)(2,1)S(1)}, bf16[256,256]{1,0:T(8,128)(2,1)}, u32[]{:S(2)}) copy-start(bf16[256,256]{1,0:T(8,128)(2,1)} %get-tuple-element.10.refs_14_) | copy-start | bytes 393220
  46.8 38.0 %copy-start.3 = (bf16[256,256]{1,0:T(8,128)(2,1)S(1)}, bf16[256,256]{1,0:T(8,128)(2,1)}, u32[]{:S(2)}) copy-start(bf16[256,256]{1,0:T(8,128)(2,1)} %get-tuple-element.11.refs_15_) | copy-start | bytes 393220
  46.8 16.6 %collective-permute-start.4 = (bf16[16,96,256]{2,1,0:T(8,128)(2,1)S(1)}, bf16[16,96,256]{2,1,0:T(8,128)(2,1)S(1)}, u32[]{:S(2)}, u32[]{:S(2)}) collective-permute-start(bf16[16,96,256]{2,1,0:T(8,128)(2,1)S(1)} %pad_maximum_fusion.refs_0_), channel_id=1, source_target_pairs={{0,3},{1,2},{2,1},{3,0},{4,5},{5,4},{6,7},{7,6},{8,11},{9,10},{10,... | collective-permute-start | bytes 2359304 | tf_op jit(solution)/shard_map/ppermute | solution.py:109
  49.3 16.9 %collective-permute-start.8 = (bf16[16,96,256]{2,1,0:T(8,128)(2,1)}, bf16[16,96,256]{2,1,0:T(8,128)(2,1)}, u32[]{:S(2)}, u32[]{:S(2)}) collective-permute-start(bf16[16,96,256]{2,1,0:T(8,128)(2,1)} %pad_maximum_fusion.1.refs_4_), channel_id=1, source_target_pairs={{0,8},{1,9},{2,10},{3,11},{4,28},{5,29},{6,30},{7,31},{8,0},{9,1},... | collective-permute-start | bytes 2359304 | tf_op jit(solution)/shard_map/ppermute | solution.py:109
  51.0 11.9 %collective-permute-start.12 = (bf16[16,80,256]{2,1,0:T(8,128)(2,1)S(1)}, bf16[16,80,256]{2,1,0:T(8,128)(2,1)}, u32[]{:S(2)}, u32[]{:S(2)}) collective-permute-start(bf16[16,80,256]{2,1,0:T(8,128)(2,1)S(1)} %pad_maximum_fusion.2.refs_8_), channel_id=1, source_target_pairs={{0,96},{1,97},{2,98},{3,99},{4,36},{5,37},{6,38},{7,39},{8,104},{9... | collective-permute-start | bytes 1966088 | tf_op jit(solution)/shard_map/ppermute | solution.py:109
  54.7 0.8 copy-start
  55.6 15.7 %collective-permute-start.5 = (bf16[16,96,256]{2,1,0:T(8,128)(2,1)S(1)}, bf16[16,96,256]{2,1,0:T(8,128)(2,1)S(1)}, u32[]{:S(2)}, u32[]{:S(2)}) collective-permute-start(bf16[16,96,256]{2,1,0:T(8,128)(2,1)S(1)} %pad_maximum_fusion.refs_0_), channel_id=1, source_target_pairs={{0,96},{1,97},{2,98},{3,99},{4,36},{5,37},{6,38},{7,39},{8,104},{9... | collective-permute-start | bytes 2359304 | tf_op jit(solution)/shard_map/ppermute | solution.py:109
  62.9 13.5 %collective-permute-start.9 = (bf16[16,96,256]{2,1,0:T(8,128)(2,1)}, bf16[16,96,256]{2,1,0:T(8,128)(2,1)}, u32[]{:S(2)}, u32[]{:S(2)}) collective-permute-start(bf16[16,96,256]{2,1,0:T(8,128)(2,1)} %pad_maximum_fusion.1.refs_4_), channel_id=1, source_target_pairs={{0,3},{1,2},{2,1},{3,0},{4,5},{5,4},{6,7},{7,6},{8,11},{9,10},{10,... | collective-permute-start | bytes 2359304 | tf_op jit(solution)/shard_map/ppermute | solution.py:109
  63.5 18.7 %collective-permute-start.6 = (bf16[16,96,256]{2,1,0:T(8,128)(2,1)S(1)}, bf16[16,96,256]{2,1,0:T(8,128)(2,1)}, u32[]{:S(2)}, u32[]{:S(2)}) collective-permute-start(bf16[16,96,256]{2,1,0:T(8,128)(2,1)S(1)} %collective-permute-done.4.refs_1_), channel_id=1, source_target_pairs={{0,96},{1,97},{2,98},{3,99},{4,36},{5,37},{6,38},{7,39},{8,104},{9... | collective-permute-start | bytes 2359304 | tf_op jit(solution)/shard_map/ppermute | solution.py:109
  66.2 18.6 %collective-permute-start.10 = (bf16[16,96,256]{2,1,0:T(8,128)(2,1)}, bf16[16,96,256]{2,1,0:T(8,128)(2,1)}, u32[]{:S(2)}, u32[]{:S(2)}) collective-permute-start(bf16[16,96,256]{2,1,0:T(8,128)(2,1)} %collective-permute-done.8.refs_5_), channel_id=1, source_target_pairs={{0,3},{1,2},{2,1},{3,0},{4,5},{5,4},{6,7},{7,6},{8,11},{9,10},{10,... | collective-permute-start | bytes 2359304 | tf_op jit(solution)/shard_map/ppermute | solution.py:109
  71.2 10.9 %collective-permute-start.14 = (bf16[16,80,256]{2,1,0:T(8,128)(2,1)}, bf16[16,80,256]{2,1,0:T(8,128)(2,1)}, u32[]{:S(2)}, u32[]{:S(2)}) collective-permute-start(bf16[16,80,256]{2,1,0:T(8,128)(2,1)} %collective-permute-done.12.refs_9_), channel_id=1, source_target_pairs={{0,8},{1,9},{2,10},{3,11},{4,28},{5,29},{6,30},{7,31},{8,0},{9,1},... | collective-permute-start | bytes 1966088 | tf_op jit(solution)/shard_map/ppermute | solution.py:109
  84.9 1.1 copy-start.1

commit v4 on v3

--- a/solution.py
+++ b/solution.py
@@ -1,3 +1,5 @@
+import functools
+
 import jax
 import jax.numpy as jnp
 from jax import lax
@@ -13,7 +15,6 @@
 NODES = 64
 CUTS = (0, 80, 176, CELLS)
 UNROLL = 8
-SPARE = 4 * NODES
 
 epsilon = 1e-06
 score_scale = 8.0
@@ -25,6 +26,7 @@
 WHOLE = (("z", True), ("x", True), ("y", False))
 LATE = (("y", True), ("z", False), ("x", False))
 GROUP = 8
+WAVES = ((0,), (1, 2, 4), (3, 5, 6, 7))
 
 
 def exchange_pairs(axis, near):
@@ -102,6 +104,7 @@
         in_specs=[taps, taps, maps],
         out_specs=(maps, square, square),
         out_shape=(jax.ShapeDtypeStruct(database.shape, bf16), square_shape, square_shape),
+        cost_estimate=pl.CostEstimate(flops=2**24, bytes_accessed=20 * 2**20, transcendentals=0),
     )(tap_q, tap_d, database)
 
 
@@ -123,19 +126,27 @@
     return [list(part) for part in zip(pieces, second, third, fourth)]
 
 
-def pair_kernel(
-    place_ref, *refs,
-):
-    parts, refs = refs[:12], refs[12:]
+def sources(combo):
+    bits = (combo & 1, combo >> 1 & 1, combo >> 2)
+    for turn in (0, 2, 1):
+        yield bits[(turn + 1) % 3] + 2 * bits[(turn + 2) % 3], bits[turn]
+
+
+def pair_kernel(wave, names, place_ref, *refs):
+    held = len(WAVES[wave]) * GROUP
+    spare = 4 * held
+    parts, refs = dict(zip(names, refs)), refs[len(names) :]
+    earlier = ()
+    if wave == 2:
+        earlier, refs = refs[:2], refs[2:]
     own_hbm, other_hbm, conv_q_ref, conv_d_ref, out_ref = refs[:5]
     query_v, image_v, ids_v, table_v, column_v, peak_v, total_v, table_s, pair_s, sems = refs[5:]
     id_copies, copies = [], []
-    for combo in range(8):
-        bits = (combo & 1, combo >> 1 & 1, combo >> 2)
-        here = pl.ds(GROUP * combo, GROUP)
-        for piece, turn in enumerate((0, 2, 1)):
-            source = parts[4 * piece + bits[(turn + 1) % 3] + 2 * bits[(turn + 2) % 3]]
-            blocks = pl.ds(GROUP * bits[turn], GROUP)
+    for local, combo in enumerate(WAVES[wave]):
+        here = pl.ds(GROUP * local, GROUP)
+        for piece, (which, half) in enumerate(sources(combo)):
+            source = parts[piece, which]
+            blocks = pl.ds(GROUP * half, GROUP)
             size = CUTS[piece + 1] - CUTS[piece]
             skip = 0 if piece else 16
             copies.append(
@@ -160,21 +171,21 @@
     pltpu.make_async_copy(ids_v, ids_v, sems.at[0]).wait()
     packed = jnp.sum(ids_v[...].astype(f32), axis=1)
     ids = packed[:, :CAND].astype(jnp.int32) * 64 + packed[:, CAND:].astype(jnp.int32)
-    lane = lax.broadcasted_iota(jnp.int32, (NODES, CAND), 1)
+    lane = lax.broadcasted_iota(jnp.int32, (held, CAND), 1)
     shard = lax.shift_right_logical(ids, 5)
     slot = ids & (IMAGES - 1)
-    table = jnp.full((NODES, CAND), -1, jnp.int32)
+    table = jnp.full((held, CAND), -1, jnp.int32)
     for side in range(2):
-        held = shard == place_ref[side]
-        first = jnp.min(jnp.where(held, lane, CAND), axis=1, keepdims=True)
-        last = jnp.max(jnp.where(held, lane, -1), axis=1, keepdims=True)
+        mine = shard == place_ref[side]
+        first = jnp.min(jnp.where(mine, lane, CAND), axis=1, keepdims=True)
+        last = jnp.max(jnp.where(mine, lane, -1), axis=1, keepdims=True)
         last = jnp.where(last > first, last, -1)
         for which, column in ((2 * side, first), (2 * side + 1, last)):
             at = lane == column
             image = jnp.max(jnp.where(at, slot, -1), axis=1, keepdims=True)
             image = jnp.where(image >= 0, image + side * IMAGES, -1)
             table = jnp.where(lane == which, image, table)
-            column_v[which] = jnp.broadcast_to(column, (NODES, CAND))
+            column_v[which] = jnp.broadcast_to(column, (held, CAND))
     table_v[...] = table
     move = pltpu.make_async_copy(table_v, table_s, sems.at[4])
     move.start()
@@ -183,13 +194,13 @@
     def fill(query, count):
         for which in range(4):
             image = table_s[query, which]
-            pair_s[count] = query * 65536 + (which * NODES + query) * 64 + jnp.maximum(image, 0)
+            pair_s[count] = query * 65536 + (which * held + query) * 64 + jnp.maximum(image, 0)
             count = count + (image >= 0).astype(jnp.int32)
         return count
 
-    count = lax.fori_loop(0, NODES, fill, jnp.int32(0))
+    count = lax.fori_loop(0, held, fill, jnp.int32(0))
     for extra in range(UNROLL):
-        pair_s[count + extra] = SPARE * 64
+        pair_s[count + extra] = spare * 64
     for copy in image_copies:
         copy.wait()
     pltpu.make_async_copy(query_v, query_v, sems.at[1]).wait()
@@ -210,12 +221,19 @@
         return carry
 
     lax.fori_loop(0, (count + UNROLL - 1) // UNROLL, group, 0)
-    total = jnp.zeros((NODES, CAND), f32)
+    total = jnp.zeros((held, CAND), f32)
     for which in range(4):
-        peaks = peak_v[pl.ds(which * NODES, NODES), :]
+        peaks = peak_v[pl.ds(which * held, held), :]
         score = jnp.sum(peaks, axis=1, keepdims=True) * (score_scale / CELLS)
         total = jnp.where(lane == column_v[which], score, total)
-    total_v[...] = total
+    if wave < 2:
+        out_ref[...] = total
+        return
+    done = 0
+    for ref in earlier:
+        total_v[pl.ds(done, ref.shape[0]), :] = ref[...]
+        done += ref.shape[0]
+    total_v[pl.ds(done, held), :] = total
 
     def settle(query, carry):
         out_ref[pl.ds(place_ref[2 + query], 1), :] = total_v[pl.ds(query, 1), :]
@@ -224,29 +242,36 @@
     lax.fori_loop(0, NODES, settle, 0, unroll=8)
 
 
-def pair_scores(place, parts, own, other, conv_q, conv_d):
+def pair_scores(wave, place, parts, earlier, own, other, conv_q, conv_d):
     smem = pl.BlockSpec(memory_space=pltpu.SMEM)
     vmem = pl.BlockSpec(memory_space=pltpu.VMEM)
     hbm = pl.BlockSpec(memory_space=pl.ANY)
+    held = len(WAVES[wave]) * GROUP
+    names = sorted(
+        {(piece, which) for combo in WAVES[wave] for piece, (which, _) in enumerate(sources(combo))}
+    )
     return pl.pallas_call(
-        pair_kernel,
-        out_shape=jax.ShapeDtypeStruct((NODES, CAND), f32),
-        in_specs=[smem] + [hbm] * 14 + [vmem, vmem],
+        functools.partial(pair_kernel, wave, names),
+        out_shape=jax.ShapeDtypeStruct((NODES if wave == 2 else held, CAND), f32),
+        in_specs=[smem] + [hbm] * len(names) + [vmem] * len(earlier) + [hbm, hbm, vmem, vmem],
         out_specs=vmem,
         scratch_shapes=[
-            pltpu.VMEM((NODES, CELLS, CELLS), bf16),
+            pltpu.VMEM((held, CELLS, CELLS), bf16),
             pltpu.VMEM((2 * IMAGES, CELLS, CELLS), bf16),
-            pltpu.VMEM((NODES, 16, CELLS), bf16),
-            pltpu.VMEM((NODES, CAND), jnp.int32),
-            pltpu.VMEM((4, NODES, CAND), jnp.int32),
-            pltpu.VMEM((4 * NODES + 8, CELLS), f32),
+            pltpu.VMEM((held, 16, CELLS), bf16),
+            pltpu.VMEM((held, CAND), jnp.int32),
+            pltpu.VMEM((4, held, CAND), jnp.int32),
+            pltpu.VMEM((4 * held + 8, CELLS), f32),
             pltpu.VMEM((NODES, CAND), f32),
-            pltpu.SMEM((NODES, CAND), jnp.int32),
-            pltpu.SMEM((4 * NODES + UNROLL,), jnp.int32),
+            pltpu.SMEM((held, CAND), jnp.int32),
+            pltpu.SMEM((4 * held + UNROLL,), jnp.int32),
             pltpu.SemaphoreType.DMA((5,)),
         ],
-        compiler_params=pltpu.CompilerParams(vmem_limit_bytes=48 * 2**20),
-    )(place, *parts, own, other, conv_q, conv_d)
+        compiler_params=pltpu.CompilerParams(vmem_limit_bytes=28 * 2**20),
+        cost_estimate=pl.CostEstimate(
+            flops=3 * held * 6 * CELLS**3, bytes_accessed=16 * 2**20, transcendentals=0
+        ),
+    )(place, *[parts[piece][which] for piece, which in names], *earlier, own, other, conv_q, conv_d)
 
 
 def finish_kernel(parts_ref, scores_ref, top_ref):
@@ -278,7 +303,8 @@
     base = (x * 4 + y) * 8 + z
     near = jnp.where(me == 0, 1, 3)
     far = 4 - near
-    index = jnp.arange(NODES, dtype=jnp.int32)
+    combos = jnp.array([combo for wave in WAVES for combo in wave], jnp.int32)
+    index = (combos[:, None] * GROUP + jnp.arange(GROUP, dtype=jnp.int32)).reshape(-1)
     bit = [lax.shift_right_logical(index, k) & 1 for k in range(6)]
     z = z ^ (bit[0] * near) ^ (bit[4] * far)
     x = x ^ (bit[1] * near) ^ (bit[5] * far)
@@ -295,8 +321,11 @@
             database, held = lax.optimization_barrier((database, held))
     own, conv_q, conv_d = prepare_images(database, kernel_query, kernel_db)
     other = lax.ppermute(own, "c", [(0, 1), (1, 0)])
-    parts = [p for part in spread(held) for p in part]
-    scores = pair_scores(place_table(), parts, own, other, conv_q, conv_d)
+    parts = spread(held)
+    place = place_table()
+    first = pair_scores(0, place, parts, (), own, other, conv_q, conv_d)
+    second = pair_scores(1, place, parts, (), own, other, conv_q, conv_d)
+    scores = pair_scores(2, place, parts, (first, second), own, other, conv_q, conv_d)
     scores = lax.all_to_all(scores, NODE, split_axis=0, concat_axis=0, tiled=True)
     return finish(scores)
 

time: 134 us -> 118 us (0.88)
  waiting for transfers between devices: 41.6 us -> 28.6 us
  blocking collectives: 21 us -> 16.9 us
  Pallas kernels: 34.6 us -> 38.2 us
  starting transfers between devices: 29.1 us -> 27.5 us
    ppermute x15, waiting for transfers between devices: 41.6 us -> 28.6 us  [move(): return lax.ppermute(array, MAIN, PAIRS[step])]
    all_to_all x1, blocking collectives: 21 us -> 16.9 us  [body(): lax.all_to_all(scores, NODE, split_axis=0, concat_axis=0, tiled=True)]
    pallas_call x1 -> x3, Pallas kernels: 23.8 us -> 27.4 us  [pair_scores(): pl.pallas_call(functools.partial(pair_kernel, wave, names), out_shape=jax...]
    ppermute x15, starting transfers between devices: 28 us -> 26.4 us  [move(): return lax.ppermute(array, MAIN, PAIRS[step])]
  transfers between devices with their start and end apart: 16 -> 16, of which waited for: 12 -> 8; matrix products, arithmetic and copies ran while one was open for 1% -> 1% of each run, Pallas kernels for 0% -> 13%
where the time goes in v4:
time: 118 us; the launch traced here: 117 us
  Pallas kernels  38.2 us (32%)
  waiting for transfers between devices  28.6 us (24%)
  starting transfers between devices  27.5 us (23%)
  blocking collectives  16.9 us (14%)
  local copies, waits for them, and re-layouts  2.46 us (2%)
  other arithmetic  2.25 us (2%)
    ppermute x15, waiting for transfers between devices, move(): return lax.ppermute(array, MAIN, PAIRS[step])  28.6 us
    pallas_call x3, Pallas kernels, pair_scores(): pl.pallas_call(functools.partial(pair_kernel, wave, names), out_shape=jax...  27.4 us
    ppermute x15, starting transfers between devices, move(): return lax.ppermute(array, MAIN, PAIRS[step])  26.4 us
    all_to_all x1, blocking collectives, body(): lax.all_to_all(scores, NODE, split_axis=0, concat_axis=0, tiled=True)  16.9 us
    pallas_call x1, Pallas kernels, prepare_images(): pl.pallas_call(images_kernel, grid=(database.shape[0] // block,), in_spec...  7.63 us
  transfers between devices with their start and end apart: 16, of which 8 were waited for; matrix products, arithmetic and copies ran while one was open for 1% of the time, Pallas kernels for 13%

profile of v4, /device:TPU:0, one launch (start us, length us, event | category | flops | bytes accessed | tf_op | source)
XLA Modules:
  0.0 116.7 jit_solution(4325943689483564243)
XLA Ops:
  0.6 1.7 %shard_map.77 = bf16[1,272,256]{2,1,0:T(8,128)(2,1)} custom-call(bf16[1,256,256]{2,1,0:T(8,128)(2,1)} %query_ref.1, s32[1,128]{1,0:T(1,128)} %ids_ref.1), custom_call_target="tpu_custom_call" | custom-call | tf_op jit(solution)/shard_map/pallas_call | solution.py:66
  2.3 2.0 %collective-permute-start = (bf16[1,272,256]{2,1,0:T(8,128)(2,1)}, bf16[1,272,256]{2,1,0:T(8,128)(2,1)S(1)}, u32[]{:S(2)}, u32[]{:S(2)}) collective-permute-start(bf16[1,272,256]{2,1,0:T(8,128)(2,1)} %shard_map.77), channel_id=1, source_target_pairs={{0,1},{1,0},{2,3},{3,2},{4,7},{5,6},{6,5},{7,4},{8,9},{9,8},{10,11... | collective-permute-start | bytes 417800 | tf_op jit(solution)/shard_map/ppermute | solution.py:112
  4.3 3.3 %collective-permute-done = bf16[1,272,256]{2,1,0:T(8,128)(2,1)S(1)} collective-permute-done((bf16[1,272,256]{2,1,0:T(8,128)(2,1)}, bf16[1,272,256]{2,1,0:T(8,128)(2,1)S(1)}, u32[]{:S(2)}, u32[]{:S(2)}) %collective-permute-start) | collective-permute-done | bytes 139296 | tf_op jit(solution)/shard_map/ppermute | solution.py:112
  7.6 0.9 pad_maximum_fusion.4
  8.5 1.7 %collective-permute-start.1 = (bf16[2,272,256]{2,1,0:T(8,128)(2,1)S(1)}, bf16[2,272,256]{2,1,0:T(8,128)(2,1)S(1)}, u32[]{:S(2)}, u32[]{:S(2)}) collective-permute-start(bf16[2,272,256]{2,1,0:T(8,128)(2,1)S(1)} %pad_maximum_fusion.4), channel_id=1, source_target_pairs={{0,32},{1,33},{2,34},{3,35},{4,100},{5,101},{6,102},{7,103},{8,40}... | collective-permute-start | bytes 835592 | tf_op jit(solution)/shard_map/ppermute | solution.py:112
  10.2 5.0 %collective-permute-done.1 = bf16[2,272,256]{2,1,0:T(8,128)(2,1)S(1)} collective-permute-done((bf16[2,272,256]{2,1,0:T(8,128)(2,1)S(1)}, bf16[2,272,256]{2,1,0:T(8,128)(2,1)S(1)}, u32[]{:S(2)}, u32[]{:S(2)}) %collective-permute-start.1) | collective-permute-done | bytes 278560 | tf_op jit(solution)/shard_map/ppermute | solution.py:112
  15.2 1.0 pad_maximum_fusion.3
  16.1 7.6 %shard_map.78 = (bf16[32,256,256]{2,1,0:T(8,128)(2,1)}, bf16[256,256]{1,0:T(8,128)(2,1)}, bf16[256,256]{1,0:T(8,128)(2,1)}) custom-call(bf16[3,3]{1,0:T(4,128)(2,1)} %tap_q_ref.1, bf16[3,3]{1,0:T(4,128)(2,1)} %tap_d_ref.1, bf16[32,256,256]{2,1,0:T(8,128)(2,1)} %maps_ref), custom_call_target="tpu_custom_call" | custom-call | flops 16777216 | bytes 20971520 | tf_op jit(solution)/shard_map/pallas_call | solution.py:101
  23.8 1.1 collective-permute-start.15
  24.9 3.0 %collective-permute-start.2 = (bf16[4,272,256]{2,1,0:T(8,128)(2,1)S(1)}, bf16[4,272,256]{2,1,0:T(8,128)(2,1)S(1)}, u32[]{:S(2)}, u32[]{:S(2)}) collective-permute-start(bf16[4,272,256]{2,1,0:T(8,128)(2,1)S(1)} %pad_maximum_fusion.3), channel_id=1, source_target_pairs={{0,24},{1,25},{2,26},{3,27},{4,12},{5,13},{6,14},{7,15},{8,16},{9,... | collective-permute-start | bytes 1671176 | tf_op jit(solution)/shard_map/ppermute | solution.py:112
  27.9 7.7 %collective-permute-done.2 = bf16[4,272,256]{2,1,0:T(8,128)(2,1)S(1)} collective-permute-done((bf16[4,272,256]{2,1,0:T(8,128)(2,1)S(1)}, bf16[4,272,256]{2,1,0:T(8,128)(2,1)S(1)}, u32[]{:S(2)}, u32[]{:S(2)}) %collective-permute-start.2) | collective-permute-done | bytes 557088 | tf_op jit(solution)/shard_map/ppermute | solution.py:112
  35.7 0.1 fusion
  35.7 2.8 %collective-permute-start.7 = (bf16[8,96,256]{2,1,0:T(8,128)(2,1)S(1)}, bf16[8,96,256]{2,1,0:T(8,128)(2,1)S(1)}, u32[]{:S(2)}, u32[]{:S(2)}) collective-permute-start(bf16[8,96,256]{2,1,0:T(8,128)(2,1)S(1)} %get-tuple-element.12), channel_id=1, source_target_pairs={{0,96},{1,97},{2,98},{3,99},{4,36},{5,37},{6,38},{7,39},{8,104},{9... | collective-permute-start | bytes 1179656 | tf_op jit(solution)/shard_map/ppermute | solution.py:112
  38.6 3.2 %collective-permute-start.11 = (bf16[8,80,256]{2,1,0:T(8,128)(2,1)S(1)}, bf16[8,80,256]{2,1,0:T(8,128)(2,1)S(1)}, u32[]{:S(2)}, u32[]{:S(2)}) collective-permute-start(bf16[8,80,256]{2,1,0:T(8,128)(2,1)S(1)} %slice.14), channel_id=1, source_target_pairs={{0,3},{1,2},{2,1},{3,0},{4,5},{5,4},{6,7},{7,6},{8,11},{9,10},{10,... | collective-permute-start | bytes 983048 | tf_op jit(solution)/shard_map/ppermute | solution.py:112
  41.8 0.4 collective-permute-start.3
  42.1 2.7 %collective-permute-done.7 = bf16[8,96,256]{2,1,0:T(8,128)(2,1)S(1)} collective-permute-done((bf16[8,96,256]{2,1,0:T(8,128)(2,1)S(1)}, bf16[8,96,256]{2,1,0:T(8,128)(2,1)S(1)}, u32[]{:S(2)}, u32[]{:S(2)}) %collective-permute-start.7) | collective-permute-done | bytes 393248 | tf_op jit(solution)/shard_map/ppermute | solution.py:112
  44.8 0.1 pad_maximum_fusion.1.refs_1_.refs_3_
  44.9 0.4 collective-permute-start.8
  45.3 1.6 %collective-permute-done.11 = bf16[8,80,256]{2,1,0:T(8,128)(2,1)S(1)} collective-permute-done((bf16[8,80,256]{2,1,0:T(8,128)(2,1)S(1)}, bf16[8,80,256]{2,1,0:T(8,128)(2,1)S(1)}, u32[]{:S(2)}, u32[]{:S(2)}) %collective-permute-start.11) | collective-permute-done | bytes 327712 | tf_op jit(solution)/shard_map/ppermute | solution.py:112
  47.0 0.1 pad_maximum_fusion.2.refs_2_.refs_6_
  47.0 0.0 copy-start.5
  47.0 0.0 copy-start.1
  47.1 0.0 copy-start.2
  47.1 1.2 %collective-permute-start.12 = (bf16[16,80,256]{2,1,0:T(8,128)(2,1)S(1)}, bf16[16,80,256]{2,1,0:T(8,128)(2,1)S(1)}, u32[]{:S(2)}, u32[]{:S(2)}) collective-permute-start(bf16[16,80,256]{2,1,0:T(8,128)(2,1)S(1)} %pad_maximum_fusion.2.refs_2_.refs_6_), channel_id=1, source_target_pairs={{0,96},{1,97},{2,98},{3,99},{4,36},{5,37},{6,38},{7,39},{8,104},{9... | collective-permute-start | bytes 1966088 | tf_op jit(solution)/shard_map/ppermute | solution.py:112
  48.3 1.3 %collective-permute-done.3 = bf16[8,96,256]{2,1,0:T(8,128)(2,1)S(1)} collective-permute-done((bf16[8,96,256]{2,1,0:T(8,128)(2,1)S(1)}, bf16[8,96,256]{2,1,0:T(8,128)(2,1)S(1)}, u32[]{:S(2)}, u32[]{:S(2)}) %collective-permute-start.3) | collective-permute-done | bytes 393248 | tf_op jit(solution)/shard_map/ppermute | solution.py:112
  49.5 0.1 pad_maximum_fusion.refs_0_
  49.6 1.9 %collective-permute-start.4 = (bf16[16,96,256]{2,1,0:T(8,128)(2,1)S(1)}, bf16[16,96,256]{2,1,0:T(8,128)(2,1)}, u32[]{:S(2)}, u32[]{:S(2)}) collective-permute-start(bf16[16,96,256]{2,1,0:T(8,128)(2,1)S(1)} %pad_maximum_fusion.refs_0_), channel_id=1, source_target_pairs={{0,3},{1,2},{2,1},{3,0},{4,5},{5,4},{6,7},{7,6},{8,11},{9,10},{10,... | collective-permute-start | bytes 2359304 | tf_op jit(solution)/shard_map/ppermute | solution.py:112
  51.5 1.4 %collective-permute-start.9 = (bf16[16,96,256]{2,1,0:T(8,128)(2,1)S(1)}, bf16[16,96,256]{2,1,0:T(8,128)(2,1)}, u32[]{:S(2)}, u32[]{:S(2)}) collective-permute-start(bf16[16,96,256]{2,1,0:T(8,128)(2,1)S(1)} %pad_maximum_fusion.1.refs_1_.refs_3_), channel_id=1, source_target_pairs={{0,3},{1,2},{2,1},{3,0},{4,5},{5,4},{6,7},{7,6},{8,11},{9,10},{10,... | collective-permute-start | bytes 2359304 | tf_op jit(solution)/shard_map/ppermute | solution.py:112
  52.9 6.0 %collective-permute-done.12.refs_7_.refs_6_ = bf16[16,80,256]{2,1,0:T(8,128)(2,1)S(1)} collective-permute-done((bf16[16,80,256]{2,1,0:T(8,128)(2,1)S(1)}, bf16[16,80,256]{2,1,0:T(8,128)(2,1)S(1)}, u32[]{:S(2)}, u32[]{:S(2)}) %collective-permute-start.12) | collective-permute-done | bytes 655392 | tf_op jit(solution)/shard_map/ppermute | solution.py:112
  58.9 0.0 copy-start.3
  58.9 1.1 collective-permute-start.5
  60.1 0.0 collective-permute-done.8.refs_4_.refs_3_
  60.1 0.0 copy-done.3
  60.1 1.7 %collective-permute-start.13 = (bf16[16,80,256]{2,1,0:T(8,128)(2,1)S(1)}, bf16[16,80,256]{2,1,0:T(8,128)(2,1)}, u32[]{:S(2)}, u32[]{:S(2)}) collective-permute-start(bf16[16,80,256]{2,1,0:T(8,128)(2,1)S(1)} %pad_maximum_fusion.2.refs_2_.refs_6_), channel_id=1, source_target_pairs={{0,8},{1,9},{2,10},{3,11},{4,28},{5,29},{6,30},{7,31},{8,0},{9,1},... | collective-permute-start | bytes 1966088 | tf_op jit(solution)/shard_map/ppermute | solution.py:112
  61.7 0.0 copy-done.5
  61.7 0.1 multiply_add_fusion
  61.8 0.1 reshape.62
  61.9 0.1 pad_add_fusion.place_ref
  62.0 1.0 collective-permute-done.4.refs_1_.refs_0_
  63.0 2.1 %collective-permute-start.10 = (bf16[16,96,256]{2,1,0:T(8,128)(2,1)S(1)}, bf16[16,96,256]{2,1,0:T(8,128)(2,1)S(1)}, u32[]{:S(2)}, u32[]{:S(2)}) collective-permute-start(bf16[16,96,256]{2,1,0:T(8,128)(2,1)S(1)} %collective-permute-done.8.refs_4_.refs_3_), channel_id=1, source_target_pairs={{0,3},{1,2},{2,1},{3,0},{4,5},{5,4},{6,7},{7,6},{8,11},{9,10},{10,... | collective-permute-start | bytes 2359304 | tf_op jit(solution)/shard_map/ppermute | solution.py:112
  65.1 0.0 collective-permute-done.15.refs_4_.refs_10_.refs_12_
  65.1 1.8 %collective-permute-start.6 = (bf16[16,96,256]{2,1,0:T(8,128)(2,1)}, bf16[16,96,256]{2,1,0:T(8,128)(2,1)S(1)}, u32[]{:S(2)}, u32[]{:S(2)}) collective-permute-start(bf16[16,96,256]{2,1,0:T(8,128)(2,1)} %collective-permute-done.4.refs_1_.refs_0_), channel_id=1, source_target_pairs={{0,96},{1,97},{2,98},{3,99},{4,36},{5,37},{6,38},{7,39},{8,104},{9... | collective-permute-start | bytes 2359304 | tf_op jit(solution)/shard_map/ppermute | solution.py:112
  66.9 0.0 copy-done.1
  66.9 0.0 copy-done.2
  66.9 0.0 copy-start
  66.9 2.2 %copy-done = bf16[32,256,256]{2,1,0:T(8,128)(2,1)S(1)} copy-done((bf16[32,256,256]{2,1,0:T(8,128)(2,1)S(1)}, bf16[32,256,256]{2,1,0:T(8,128)(2,1)}, u32[]{:S(2)}) %copy-start) | copy-done | bytes 4194328
  69.1 0.0 copy-start.4
  69.1 5.1 %shard_map.79.refs_9_ = f32[8,128]{1,0:T(8,128)S(1)} custom-call(s32[66]{0:T(128)S(1)} %pad_add_fusion.place_ref, bf16[16,96,256]{2,1,0:T(8,128)(2,1)S(1)} %pad_maximum_fusion.refs_0_, bf16[16,96,256]{2,1,0:T(8,128)(2,1)S(1)} %pad_maximum_fusion.1.refs_1_.refs_3_, bf16[16,80,256]{2,1,0:T(8,128)(2,1)S(1)} %pad_maximum_fusion.2.refs_2_.refs_6_, ...), custom_call_target="tpu_custom_call" | custom-call | flops 2415919104 | bytes 16777216 | tf_op jit(solution)/shard_map/pallas_call | solution.py:253
  74.3 0.0 collective-permute-done.13.refs_8_.refs_7_
  74.3 0.0 copy-done.4
  74.3 1.7 %collective-permute-start.14 = (bf16[16,80,256]{2,1,0:T(8,128)(2,1)S(1)}, bf16[16,80,256]{2,1,0:T(8,128)(2,1)S(1)}, u32[]{:S(2)}, u32[]{:S(2)}) collective-permute-start(bf16[16,80,256]{2,1,0:T(8,128)(2,1)S(1)} %copy-done.4), channel_id=1, source_target_pairs={{0,8},{1,9},{2,10},{3,11},{4,28},{5,29},{6,30},{7,31},{8,0},{9,1},... | collective-permute-start | bytes 1966088 | tf_op jit(solution)/shard_map/ppermute | solution.py:112
  76.0 0.0 collective-permute-done.9.refs_5_.refs_4_
  76.0 0.0 collective-permute-done.5.refs_2_.refs_1_
  76.0 10.6 %shard_map.80.refs_10_ = f32[24,128]{1,0:T(8,128)S(1)} custom-call(s32[66]{0:T(128)S(1)} %pad_add_fusion.place_ref, bf16[16,96,256]{2,1,0:T(8,128)(2,1)S(1)} %pad_maximum_fusion.refs_0_, bf16[16,96,256]{2,1,0:T(8,128)(2,1)} %collective-permute-done.4.refs_1_.refs_0_, bf16[16,96,256]{2,1,0:T(8,128)(2,1)} %collective-permute-done.5.refs_2_.refs_1_, ...), custom_call_target="tpu_custom_call" | custom-call | flops 7247757312 | bytes 16777216 | tf_op jit(solution)/shard_map/pallas_call | solution.py:253
  86.6 0.0 collective-permute-done.14.refs_8_
  86.6 0.0 collective-permute-done.10.refs_5_
  86.6 0.0 collective-permute-done.6.refs_2_
  86.6 11.7 %shard_map.81 = f32[64,128]{1,0:T(8,128)S(1)} custom-call(s32[66]{0:T(128)S(1)} %pad_add_fusion.place_ref, bf16[16,96,256]{2,1,0:T(8,128)(2,1)} %collective-permute-done.4.refs_1_.refs_0_, bf16[16,96,256]{2,1,0:T(8,128)(2,1)} %collective-permute-done.5.refs_2_.refs_1_, bf16[16,96,256]{2,1,0:T(8,128)(2,1)S(1)} %collective-permute-done.6.refs_2_, ...), custom_call_target="tpu_custom_call" | custom-call | flops 9663676416 | bytes 16777216 | tf_op jit(solution)/shard_map/pallas_call | solution.py:253
  98.3 16.9 %all_to_all.11 = f32[64,1,128]{2,1,0:T(1,128)} all-to-all(f32[64,1,128]{2,1,0:T(1,128)S(1)} %bitcast.6), channel_id=1, replica_groups=mesh['x'=4,'y'=4,'c'=2,'z'=4] {'x','y','z'}, dimensions={0} | all-to-all | bytes 65536 | tf_op jit(solution)/shard_map/all_to_all | solution.py:329
  115.3 1.5 %shard_map.82 = (f32[1,128]{1,0:T(1,128)}, f32[1,100]{1,0:T(1,128)}) custom-call(f32[64,128]{1,0:T(8,128)} %bitcast.7), custom_call_target="tpu_custom_call" | custom-call | tf_op jit(solution)/shard_map/pallas_call | solution.py:291
  (3 shorter events, 0.1 us)
Async XLA Ops:
  2.3 5.3 %collective-permute-start = (bf16[1,272,256]{2,1,0:T(8,128)(2,1)}, bf16[1,272,256]{2,1,0:T(8,128)(2,1)S(1)}, u32[]{:S(2)}, u32[]{:S(2)}) collective-permute-start(bf16[1,272,256]{2,1,0:T(8,128)(2,1)} %shard_map.77), channel_id=1, source_target_pairs={{0,1},{1,0},{2,3},{3,2},{4,7},{5,6},{6,5},{7,4},{8,9},{9,8},{10,11... | collective-permute-start | bytes 417800 | tf_op jit(solution)/shard_map/ppermute | solution.py:112
  8.5 6.6 %collective-permute-start.1 = (bf16[2,272,256]{2,1,0:T(8,128)(2,1)S(1)}, bf16[2,272,256]{2,1,0:T(8,128)(2,1)S(1)}, u32[]{:S(2)}, u32[]{:S(2)}) collective-permute-start(bf16[2,272,256]{2,1,0:T(8,128)(2,1)S(1)} %pad_maximum_fusion.4), channel_id=1, source_target_pairs={{0,32},{1,33},{2,34},{3,35},{4,100},{5,101},{6,102},{7,103},{8,40}... | collective-permute-start | bytes 835592 | tf_op jit(solution)/shard_map/ppermute | solution.py:112
  23.8 41.3 %collective-permute-start.15 = (bf16[32,256,256]{2,1,0:T(8,128)(2,1)}, bf16[32,256,256]{2,1,0:T(8,128)(2,1)}, u32[]{:S(2)}, u32[]{:S(2)}) collective-permute-start(bf16[32,256,256]{2,1,0:T(8,128)(2,1)} %get-tuple-element.9.refs_3_.refs_9_.refs_11_), channel_id=1, source_target_pairs={{0,4},{4,0},{1,5},{5,1},{2,6},{6,2},{3,7},{7,3},{8,12},{12,8},{9,1... | collective-permute-start | bytes 12582920 | tf_op jit(solution)/shard_map/ppermute | solution.py:323
  24.9 10.7 %collective-permute-start.2 = (bf16[4,272,256]{2,1,0:T(8,128)(2,1)S(1)}, bf16[4,272,256]{2,1,0:T(8,128)(2,1)S(1)}, u32[]{:S(2)}, u32[]{:S(2)}) collective-permute-start(bf16[4,272,256]{2,1,0:T(8,128)(2,1)S(1)} %pad_maximum_fusion.3), channel_id=1, source_target_pairs={{0,24},{1,25},{2,26},{3,27},{4,12},{5,13},{6,14},{7,15},{8,16},{9,... | collective-permute-start | bytes 1671176 | tf_op jit(solution)/shard_map/ppermute | solution.py:112
  35.7 9.1 %collective-permute-start.7 = (bf16[8,96,256]{2,1,0:T(8,128)(2,1)S(1)}, bf16[8,96,256]{2,1,0:T(8,128)(2,1)S(1)}, u32[]{:S(2)}, u32[]{:S(2)}) collective-permute-start(bf16[8,96,256]{2,1,0:T(8,128)(2,1)S(1)} %get-tuple-element.12), channel_id=1, source_target_pairs={{0,96},{1,97},{2,98},{3,99},{4,36},{5,37},{6,38},{7,39},{8,104},{9... | collective-permute-start | bytes 1179656 | tf_op jit(solution)/shard_map/ppermute | solution.py:112
  38.6 8.4 %collective-permute-start.11 = (bf16[8,80,256]{2,1,0:T(8,128)(2,1)S(1)}, bf16[8,80,256]{2,1,0:T(8,128)(2,1)S(1)}, u32[]{:S(2)}, u32[]{:S(2)}) collective-permute-start(bf16[8,80,256]{2,1,0:T(8,128)(2,1)S(1)} %slice.14), channel_id=1, source_target_pairs={{0,3},{1,2},{2,1},{3,0},{4,5},{5,4},{6,7},{7,6},{8,11},{9,10},{10,... | collective-permute-start | bytes 983048 | tf_op jit(solution)/shard_map/ppermute | solution.py:112
  41.8 7.8 %collective-permute-start.3 = (bf16[8,96,256]{2,1,0:T(8,128)(2,1)S(1)}, bf16[8,96,256]{2,1,0:T(8,128)(2,1)S(1)}, u32[]{:S(2)}, u32[]{:S(2)}) collective-permute-start(bf16[8,96,256]{2,1,0:T(8,128)(2,1)S(1)} %get-tuple-element.13), channel_id=1, source_target_pairs={{0,8},{1,9},{2,10},{3,11},{4,28},{5,29},{6,30},{7,31},{8,0},{9,1},... | collective-permute-start | bytes 1179656 | tf_op jit(solution)/shard_map/ppermute | solution.py:112
  44.9 15.2 %collective-permute-start.8 = (bf16[16,96,256]{2,1,0:T(8,128)(2,1)S(1)}, bf16[16,96,256]{2,1,0:T(8,128)(2,1)S(1)}, u32[]{:S(2)}, u32[]{:S(2)}) collective-permute-start(bf16[16,96,256]{2,1,0:T(8,128)(2,1)S(1)} %pad_maximum_fusion.1.refs_1_.refs_3_), channel_id=1, source_target_pairs={{0,8},{1,9},{2,10},{3,11},{4,28},{5,29},{6,30},{7,31},{8,0},{9,1},... | collective-permute-start | bytes 2359304 | tf_op jit(solution)/shard_map/ppermute | solution.py:112
  47.0 14.7 %copy-start.5 = (s32[8]{0:T(128)S(1)}, s32[8]{0:T(128)}, u32[]{:S(2)}) copy-start(s32[8]{0:T(128)} %constant.41) | copy-start | bytes 100
  47.0 19.9 %copy-start.1 = (bf16[256,256]{1,0:T(8,128)(2,1)S(1)}, bf16[256,256]{1,0:T(8,128)(2,1)}, u32[]{:S(2)}) copy-start(bf16[256,256]{1,0:T(8,128)(2,1)} %get-tuple-element.10.refs_5_.refs_11_.refs_13_) | copy-start | bytes 393220
  47.1 19.9 %copy-start.2 = (bf16[256,256]{1,0:T(8,128)(2,1)S(1)}, bf16[256,256]{1,0:T(8,128)(2,1)}, u32[]{:S(2)}) copy-start(bf16[256,256]{1,0:T(8,128)(2,1)} %get-tuple-element.11.refs_6_.refs_12_.refs_14_) | copy-start | bytes 393220
  47.1 11.9 %collective-permute-start.12 = (bf16[16,80,256]{2,1,0:T(8,128)(2,1)S(1)}, bf16[16,80,256]{2,1,0:T(8,128)(2,1)S(1)}, u32[]{:S(2)}, u32[]{:S(2)}) collective-permute-start(bf16[16,80,256]{2,1,0:T(8,128)(2,1)S(1)} %pad_maximum_fusion.2.refs_2_.refs_6_), channel_id=1, source_target_pairs={{0,96},{1,97},{2,98},{3,99},{4,36},{5,37},{6,38},{7,39},{8,104},{9... | collective-permute-start | bytes 1966088 | tf_op jit(solution)/shard_map/ppermute | solution.py:112
  49.6 13.4 %collective-permute-start.4 = (bf16[16,96,256]{2,1,0:T(8,128)(2,1)S(1)}, bf16[16,96,256]{2,1,0:T(8,128)(2,1)}, u32[]{:S(2)}, u32[]{:S(2)}) collective-permute-start(bf16[16,96,256]{2,1,0:T(8,128)(2,1)S(1)} %pad_maximum_fusion.refs_0_), channel_id=1, source_target_pairs={{0,3},{1,2},{2,1},{3,0},{4,5},{5,4},{6,7},{7,6},{8,11},{9,10},{10,... | collective-permute-start | bytes 2359304 | tf_op jit(solution)/shard_map/ppermute | solution.py:112
  51.5 24.5 %collective-permute-start.9 = (bf16[16,96,256]{2,1,0:T(8,128)(2,1)S(1)}, bf16[16,96,256]{2,1,0:T(8,128)(2,1)}, u32[]{:S(2)}, u32[]{:S(2)}) collective-permute-start(bf16[16,96,256]{2,1,0:T(8,128)(2,1)S(1)} %pad_maximum_fusion.1.refs_1_.refs_3_), channel_id=1, source_target_pairs={{0,3},{1,2},{2,1},{3,0},{4,5},{5,4},{6,7},{7,6},{8,11},{9,10},{10,... | collective-permute-start | bytes 2359304 | tf_op jit(solution)/shard_map/ppermute | solution.py:112
  58.9 1.1 copy-start.3
  58.9 17.1 %collective-permute-start.5 = (bf16[16,96,256]{2,1,0:T(8,128)(2,1)S(1)}, bf16[16,96,256]{2,1,0:T(8,128)(2,1)}, u32[]{:S(2)}, u32[]{:S(2)}) collective-permute-start(bf16[16,96,256]{2,1,0:T(8,128)(2,1)S(1)} %pad_maximum_fusion.refs_0_), channel_id=1, source_target_pairs={{0,96},{1,97},{2,98},{3,99},{4,36},{5,37},{6,38},{7,39},{8,104},{9... | collective-permute-start | bytes 2359304 | tf_op jit(solution)/shard_map/ppermute | solution.py:112
  60.1 14.2 %collective-permute-start.13 = (bf16[16,80,256]{2,1,0:T(8,128)(2,1)S(1)}, bf16[16,80,256]{2,1,0:T(8,128)(2,1)}, u32[]{:S(2)}, u32[]{:S(2)}) collective-permute-start(bf16[16,80,256]{2,1,0:T(8,128)(2,1)S(1)} %pad_maximum_fusion.2.refs_2_.refs_6_), channel_id=1, source_target_pairs={{0,8},{1,9},{2,10},{3,11},{4,28},{5,29},{6,30},{7,31},{8,0},{9,1},... | collective-permute-start | bytes 1966088 | tf_op jit(solution)/shard_map/ppermute | solution.py:112
  63.0 23.6 %collective-permute-start.10 = (bf16[16,96,256]{2,1,0:T(8,128)(2,1)S(1)}, bf16[16,96,256]{2,1,0:T(8,128)(2,1)S(1)}, u32[]{:S(2)}, u32[]{:S(2)}) collective-permute-start(bf16[16,96,256]{2,1,0:T(8,128)(2,1)S(1)} %collective-permute-done.8.refs_4_.refs_3_), channel_id=1, source_target_pairs={{0,3},{1,2},{2,1},{3,0},{4,5},{5,4},{6,7},{7,6},{8,11},{9,10},{10,... | collective-permute-start | bytes 2359304 | tf_op jit(solution)/shard_map/ppermute | solution.py:112
  65.1 21.5 %collective-permute-start.6 = (bf16[16,96,256]{2,1,0:T(8,128)(2,1)}, bf16[16,96,256]{2,1,0:T(8,128)(2,1)S(1)}, u32[]{:S(2)}, u32[]{:S(2)}) collective-permute-start(bf16[16,96,256]{2,1,0:T(8,128)(2,1)} %collective-permute-done.4.refs_1_.refs_0_), channel_id=1, source_target_pairs={{0,96},{1,97},{2,98},{3,99},{4,36},{5,37},{6,38},{7,39},{8,104},{9... | collective-permute-start | bytes 2359304 | tf_op jit(solution)/shard_map/ppermute | solution.py:112
  66.9 2.2 %copy-start = (bf16[32,256,256]{2,1,0:T(8,128)(2,1)S(1)}, bf16[32,256,256]{2,1,0:T(8,128)(2,1)}, u32[]{:S(2)}) copy-start(bf16[32,256,256]{2,1,0:T(8,128)(2,1)} %get-tuple-element.9.refs_3_.refs_9_.refs_11_) | copy-start | bytes 12582916
  69.1 5.2 %copy-start.4 = (bf16[16,80,256]{2,1,0:T(8,128)(2,1)S(1)}, bf16[16,80,256]{2,1,0:T(8,128)(2,1)}, u32[]{:S(2)}) copy-start(bf16[16,80,256]{2,1,0:T(8,128)(2,1)} %copy-done.3) | copy-start | bytes 1966084
  74.3 12.3 %collective-permute-start.14 = (bf16[16,80,256]{2,1,0:T(8,128)(2,1)S(1)}, bf16[16,80,256]{2,1,0:T(8,128)(2,1)S(1)}, u32[]{:S(2)}, u32[]{:S(2)}) collective-permute-start(bf16[16,80,256]{2,1,0:T(8,128)(2,1)S(1)} %copy-done.4), channel_id=1, source_target_pairs={{0,8},{1,9},{2,10},{3,11},{4,28},{5,29},{6,30},{7,31},{8,0},{9,1},... | collective-permute-start | bytes 1966088 | tf_op jit(solution)/shard_map/ppermute | solution.py:112

commit v5 on v4

--- a/solution.py
+++ b/solution.py
@@ -316,10 +316,13 @@
 def body(query_maps, database, shortlist, kernel_query, kernel_db):
     held = pack(query_maps, shortlist)
     for count, step in enumerate(WHOLE):
-        held = jnp.concatenate([held, move(held, step)], axis=0)
+        came = move(held, step)
+        if count == 2:
+            own, conv_q, conv_d = prepare_images(database, kernel_query, kernel_db)
+            came, own = lax.optimization_barrier((came, own))
+        held = jnp.concatenate([held, came], axis=0)
         if count == 1:
             database, held = lax.optimization_barrier((database, held))
-    own, conv_q, conv_d = prepare_images(database, kernel_query, kernel_db)
     other = lax.ppermute(own, "c", [(0, 1), (1, 0)])
     parts = spread(held)
     place = place_table()

time: 118 us -> 113 us (0.958)
  waiting for transfers between devices: 28.6 us -> 22.6 us
  blocking collectives: 16.9 us -> 22.2 us
  starting transfers between devices: 27.5 us -> 24.9 us
    ppermute x15, waiting for transfers between devices: 28.6 us -> 22.6 us  [move(): return lax.ppermute(array, MAIN, PAIRS[step])]
    all_to_all x1, blocking collectives: 16.9 us -> 22.2 us  [body(): lax.all_to_all(scores, NODE, split_axis=0, concat_axis=0, tiled=True)]
    ppermute x15, starting transfers between devices: 26.4 us -> 24.9 us  [move(): return lax.ppermute(array, MAIN, PAIRS[step])]
  transfers between devices with their start and end apart: 16 -> 16, of which waited for: 8 -> 8; matrix products, arithmetic and copies ran while one was open for 1% -> 1% of each run, Pallas kernels for 13% -> 20%
where the time goes in v5:
time: 113 us
  Pallas kernels  37.2 us (33%)
  starting transfers between devices  24.9 us (22%)
  waiting for transfers between devices  22.6 us (20%)
  blocking collectives  22.2 us (20%)
  local copies, waits for them, and re-layouts  2.81 us (2%)
  other arithmetic  2.25 us (2%)
    pallas_call x3, Pallas kernels, pair_scores(): pl.pallas_call(functools.partial(pair_kernel, wave, names), out_shape=jax...  26.4 us
    ppermute x15, starting transfers between devices, move(): return lax.ppermute(array, MAIN, PAIRS[step])  24.9 us
    ppermute x15, waiting for transfers between devices, move(): return lax.ppermute(array, MAIN, PAIRS[step])  22.6 us
    all_to_all x1, blocking collectives, body(): lax.all_to_all(scores, NODE, split_axis=0, concat_axis=0, tiled=True)  22.2 us
    pallas_call x1, Pallas kernels, prepare_images(): pl.pallas_call(images_kernel, grid=(database.shape[0] // block,), in_spec...  7.61 us
    unnamed x13, local copies, waits for them, and re-layouts  2.6 us
  transfers between devices with their start and end apart: 16, of which 8 were waited for; matrix products, arithmetic and copies ran while one was open for 1% of the time, Pallas kernels for 20%

profile of v5, /device:TPU:0, one launch (start us, length us, event | category | flops | bytes accessed | tf_op | source)
XLA Modules:
  0.0 112.8 jit_solution(14819591695281354938)
XLA Ops:
  0.6 1.7 %shard_map.77 = bf16[1,272,256]{2,1,0:T(8,128)(2,1)} custom-call(bf16[1,256,256]{2,1,0:T(8,128)(2,1)} %query_ref.1, s32[1,128]{1,0:T(1,128)} %ids_ref.1), custom_call_target="tpu_custom_call" | custom-call | tf_op jit(solution)/shard_map/pallas_call | solution.py:66
  2.3 2.0 %collective-permute-start = (bf16[1,272,256]{2,1,0:T(8,128)(2,1)}, bf16[1,272,256]{2,1,0:T(8,128)(2,1)S(1)}, u32[]{:S(2)}, u32[]{:S(2)}) collective-permute-start(bf16[1,272,256]{2,1,0:T(8,128)(2,1)} %shard_map.77), channel_id=1, source_target_pairs={{0,1},{1,0},{2,3},{3,2},{4,7},{5,6},{6,5},{7,4},{8,9},{9,8},{10,11... | collective-permute-start | bytes 417800 | tf_op jit(solution)/shard_map/ppermute | solution.py:112
  4.3 3.3 %collective-permute-done = bf16[1,272,256]{2,1,0:T(8,128)(2,1)S(1)} collective-permute-done((bf16[1,272,256]{2,1,0:T(8,128)(2,1)}, bf16[1,272,256]{2,1,0:T(8,128)(2,1)S(1)}, u32[]{:S(2)}, u32[]{:S(2)}) %collective-permute-start) | collective-permute-done | bytes 139296 | tf_op jit(solution)/shard_map/ppermute | solution.py:112
  7.6 0.9 pad_maximum_fusion.4
  8.5 1.7 %collective-permute-start.1 = (bf16[2,272,256]{2,1,0:T(8,128)(2,1)S(1)}, bf16[2,272,256]{2,1,0:T(8,128)(2,1)S(1)}, u32[]{:S(2)}, u32[]{:S(2)}) collective-permute-start(bf16[2,272,256]{2,1,0:T(8,128)(2,1)S(1)} %pad_maximum_fusion.4), channel_id=1, source_target_pairs={{0,32},{1,33},{2,34},{3,35},{4,100},{5,101},{6,102},{7,103},{8,40}... | collective-permute-start | bytes 835592 | tf_op jit(solution)/shard_map/ppermute | solution.py:112
  10.2 5.0 %collective-permute-done.1 = bf16[2,272,256]{2,1,0:T(8,128)(2,1)S(1)} collective-permute-done((bf16[2,272,256]{2,1,0:T(8,128)(2,1)S(1)}, bf16[2,272,256]{2,1,0:T(8,128)(2,1)S(1)}, u32[]{:S(2)}, u32[]{:S(2)}) %collective-permute-start.1) | collective-permute-done | bytes 278560 | tf_op jit(solution)/shard_map/ppermute | solution.py:112
  15.2 1.0 pad_maximum_fusion.3
  16.1 3.2 %collective-permute-start.2 = (bf16[4,272,256]{2,1,0:T(8,128)(2,1)S(1)}, bf16[4,272,256]{2,1,0:T(8,128)(2,1)S(1)}, u32[]{:S(2)}, u32[]{:S(2)}) collective-permute-start(bf16[4,272,256]{2,1,0:T(8,128)(2,1)S(1)} %pad_maximum_fusion.3), channel_id=1, source_target_pairs={{0,24},{1,25},{2,26},{3,27},{4,12},{5,13},{6,14},{7,15},{8,16},{9,... | collective-permute-start | bytes 1671176 | tf_op jit(solution)/shard_map/ppermute | solution.py:112
  19.3 7.6 %shard_map.78 = (bf16[32,256,256]{2,1,0:T(8,128)(2,1)}, bf16[256,256]{1,0:T(8,128)(2,1)}, bf16[256,256]{1,0:T(8,128)(2,1)}) custom-call(bf16[3,3]{1,0:T(4,128)(2,1)} %tap_q_ref.1, bf16[3,3]{1,0:T(4,128)(2,1)} %tap_d_ref.1, bf16[32,256,256]{2,1,0:T(8,128)(2,1)} %maps_ref), custom_call_target="tpu_custom_call" | custom-call | flops 16777216 | bytes 20971520 | tf_op jit(solution)/shard_map/pallas_call | solution.py:101
  26.9 0.0 collective-permute-done.2
  26.9 0.1 collective-permute-start.15
  27.1 0.1 fusion
  27.2 2.9 %collective-permute-start.7 = (bf16[8,96,256]{2,1,0:T(8,128)(2,1)S(1)}, bf16[8,96,256]{2,1,0:T(8,128)(2,1)S(1)}, u32[]{:S(2)}, u32[]{:S(2)}) collective-permute-start(bf16[8,96,256]{2,1,0:T(8,128)(2,1)S(1)} %get-tuple-element.16), channel_id=1, source_target_pairs={{0,96},{1,97},{2,98},{3,99},{4,36},{5,37},{6,38},{7,39},{8,104},{9... | collective-permute-start | bytes 1179656 | tf_op jit(solution)/shard_map/ppermute | solution.py:112
  30.1 4.1 %collective-permute-start.11 = (bf16[8,80,256]{2,1,0:T(8,128)(2,1)S(1)}, bf16[8,80,256]{2,1,0:T(8,128)(2,1)S(1)}, u32[]{:S(2)}, u32[]{:S(2)}) collective-permute-start(bf16[8,80,256]{2,1,0:T(8,128)(2,1)S(1)} %slice.14), channel_id=1, source_target_pairs={{0,3},{1,2},{2,1},{3,0},{4,5},{5,4},{6,7},{7,6},{8,11},{9,10},{10,... | collective-permute-start | bytes 983048 | tf_op jit(solution)/shard_map/ppermute | solution.py:112
  34.2 0.4 collective-permute-start.3
  34.5 1.7 %collective-permute-done.7 = bf16[8,96,256]{2,1,0:T(8,128)(2,1)S(1)} collective-permute-done((bf16[8,96,256]{2,1,0:T(8,128)(2,1)S(1)}, bf16[8,96,256]{2,1,0:T(8,128)(2,1)S(1)}, u32[]{:S(2)}, u32[]{:S(2)}) %collective-permute-start.7) | collective-permute-done | bytes 393248 | tf_op jit(solution)/shard_map/ppermute | solution.py:112
  36.3 0.1 pad_maximum_fusion.1.refs_1_.refs_3_
  36.3 0.6 collective-permute-start.8
  36.9 2.3 %collective-permute-done.11 = bf16[8,80,256]{2,1,0:T(8,128)(2,1)S(1)} collective-permute-done((bf16[8,80,256]{2,1,0:T(8,128)(2,1)S(1)}, bf16[8,80,256]{2,1,0:T(8,128)(2,1)S(1)}, u32[]{:S(2)}, u32[]{:S(2)}) %collective-permute-start.11) | collective-permute-done | bytes 327712 | tf_op jit(solution)/shard_map/ppermute | solution.py:112
  39.2 0.1 pad_maximum_fusion.2.refs_2_.refs_6_
  39.3 0.0 copy-start.5
  39.3 0.0 copy-start.1
  39.3 0.0 copy-start.2
  39.3 0.6 collective-permute-start.12
  39.9 2.1 %collective-permute-done.3 = bf16[8,96,256]{2,1,0:T(8,128)(2,1)S(1)} collective-permute-done((bf16[8,96,256]{2,1,0:T(8,128)(2,1)S(1)}, bf16[8,96,256]{2,1,0:T(8,128)(2,1)S(1)}, u32[]{:S(2)}, u32[]{:S(2)}) %collective-permute-start.3) | collective-permute-done | bytes 393248 | tf_op jit(solution)/shard_map/ppermute | solution.py:112
  42.0 0.1 pad_maximum_fusion.refs_0_
  42.0 1.9 %collective-permute-start.4 = (bf16[16,96,256]{2,1,0:T(8,128)(2,1)S(1)}, bf16[16,96,256]{2,1,0:T(8,128)(2,1)}, u32[]{:S(2)}, u32[]{:S(2)}) collective-permute-start(bf16[16,96,256]{2,1,0:T(8,128)(2,1)S(1)} %pad_maximum_fusion.refs_0_), channel_id=1, source_target_pairs={{0,3},{1,2},{2,1},{3,0},{4,5},{5,4},{6,7},{7,6},{8,11},{9,10},{10,... | collective-permute-start | bytes 2359304 | tf_op jit(solution)/shard_map/ppermute | solution.py:112
  43.9 1.4 %collective-permute-start.9 = (bf16[16,96,256]{2,1,0:T(8,128)(2,1)S(1)}, bf16[16,96,256]{2,1,0:T(8,128)(2,1)}, u32[]{:S(2)}, u32[]{:S(2)}) collective-permute-start(bf16[16,96,256]{2,1,0:T(8,128)(2,1)S(1)} %pad_maximum_fusion.1.refs_1_.refs_3_), channel_id=1, source_target_pairs={{0,3},{1,2},{2,1},{3,0},{4,5},{5,4},{6,7},{7,6},{8,11},{9,10},{10,... | collective-permute-start | bytes 2359304 | tf_op jit(solution)/shard_map/ppermute | solution.py:112
  45.3 5.9 %collective-permute-done.12.refs_7_.refs_6_ = bf16[16,80,256]{2,1,0:T(8,128)(2,1)S(1)} collective-permute-done((bf16[16,80,256]{2,1,0:T(8,128)(2,1)S(1)}, bf16[16,80,256]{2,1,0:T(8,128)(2,1)S(1)}, u32[]{:S(2)}, u32[]{:S(2)}) %collective-permute-start.12) | collective-permute-done | bytes 655392 | tf_op jit(solution)/shard_map/ppermute | solution.py:112
  51.2 0.0 copy-start.3
  51.2 0.5 collective-permute-start.5
  51.7 0.0 collective-permute-done.8.refs_4_.refs_3_
  51.7 0.4 copy-done.3
  52.0 1.1 %collective-permute-start.13 = (bf16[16,80,256]{2,1,0:T(8,128)(2,1)S(1)}, bf16[16,80,256]{2,1,0:T(8,128)(2,1)}, u32[]{:S(2)}, u32[]{:S(2)}) collective-permute-start(bf16[16,80,256]{2,1,0:T(8,128)(2,1)S(1)} %pad_maximum_fusion.2.refs_2_.refs_6_), channel_id=1, source_target_pairs={{0,8},{1,9},{2,10},{3,11},{4,28},{5,29},{6,30},{7,31},{8,0},{9,1},... | collective-permute-start | bytes 1966088 | tf_op jit(solution)/shard_map/ppermute | solution.py:112
  53.2 0.0 copy-done.5
  53.2 0.1 multiply_add_fusion
  53.3 0.1 reshape.62
  53.4 0.1 pad_add_fusion.place_ref
  53.4 2.0 %collective-permute-done.4.refs_1_.refs_0_ = bf16[16,96,256]{2,1,0:T(8,128)(2,1)} collective-permute-done((bf16[16,96,256]{2,1,0:T(8,128)(2,1)S(1)}, bf16[16,96,256]{2,1,0:T(8,128)(2,1)}, u32[]{:S(2)}, u32[]{:S(2)}) %collective-permute-start.4) | collective-permute-done | bytes 786464 | tf_op jit(solution)/shard_map/ppermute | solution.py:112
  55.4 2.1 %collective-permute-start.10 = (bf16[16,96,256]{2,1,0:T(8,128)(2,1)S(1)}, bf16[16,96,256]{2,1,0:T(8,128)(2,1)S(1)}, u32[]{:S(2)}, u32[]{:S(2)}) collective-permute-start(bf16[16,96,256]{2,1,0:T(8,128)(2,1)S(1)} %collective-permute-done.8.refs_4_.refs_3_), channel_id=1, source_target_pairs={{0,3},{1,2},{2,1},{3,0},{4,5},{5,4},{6,7},{7,6},{8,11},{9,10},{10,... | collective-permute-start | bytes 2359304 | tf_op jit(solution)/shard_map/ppermute | solution.py:112
  57.5 0.0 collective-permute-done.15.refs_4_.refs_10_.refs_12_
  57.5 1.8 %collective-permute-start.6 = (bf16[16,96,256]{2,1,0:T(8,128)(2,1)}, bf16[16,96,256]{2,1,0:T(8,128)(2,1)S(1)}, u32[]{:S(2)}, u32[]{:S(2)}) collective-permute-start(bf16[16,96,256]{2,1,0:T(8,128)(2,1)} %collective-permute-done.4.refs_1_.refs_0_), channel_id=1, source_target_pairs={{0,96},{1,97},{2,98},{3,99},{4,36},{5,37},{6,38},{7,39},{8,104},{9... | collective-permute-start | bytes 2359304 | tf_op jit(solution)/shard_map/ppermute | solution.py:112
  59.3 0.0 copy-done.1
  59.3 0.0 copy-done.2
  59.3 0.0 copy-start
  59.3 2.2 %copy-done = bf16[32,256,256]{2,1,0:T(8,128)(2,1)S(1)} copy-done((bf16[32,256,256]{2,1,0:T(8,128)(2,1)S(1)}, bf16[32,256,256]{2,1,0:T(8,128)(2,1)}, u32[]{:S(2)}) %copy-start) | copy-done | bytes 4194328
  61.5 0.0 copy-start.4
  61.5 5.2 %shard_map.79.refs_9_ = f32[8,128]{1,0:T(8,128)S(1)} custom-call(s32[66]{0:T(128)S(1)} %pad_add_fusion.place_ref, bf16[16,96,256]{2,1,0:T(8,128)(2,1)S(1)} %pad_maximum_fusion.refs_0_, bf16[16,96,256]{2,1,0:T(8,128)(2,1)S(1)} %pad_maximum_fusion.1.refs_1_.refs_3_, bf16[16,80,256]{2,1,0:T(8,128)(2,1)S(1)} %pad_maximum_fusion.2.refs_2_.refs_6_, ...), custom_call_target="tpu_custom_call" | custom-call | flops 2415919104 | bytes 16777216 | tf_op jit(solution)/shard_map/pallas_call | solution.py:253
  66.7 0.0 collective-permute-done.13.refs_8_.refs_7_
  66.7 0.0 copy-done.4
  66.7 0.7 collective-permute-start.14
  67.4 0.0 collective-permute-done.9.refs_5_.refs_4_
  67.4 0.0 collective-permute-done.5.refs_2_.refs_1_
  67.4 9.6 %shard_map.80.refs_10_ = f32[24,128]{1,0:T(8,128)S(1)} custom-call(s32[66]{0:T(128)S(1)} %pad_add_fusion.place_ref, bf16[16,96,256]{2,1,0:T(8,128)(2,1)S(1)} %pad_maximum_fusion.refs_0_, bf16[16,96,256]{2,1,0:T(8,128)(2,1)} %collective-permute-done.4.refs_1_.refs_0_, bf16[16,96,256]{2,1,0:T(8,128)(2,1)} %collective-permute-done.5.refs_2_.refs_1_, ...), custom_call_target="tpu_custom_call" | custom-call | flops 7247757312 | bytes 16777216 | tf_op jit(solution)/shard_map/pallas_call | solution.py:253
  77.0 0.4 collective-permute-done.14.refs_8_
  77.4 0.0 collective-permute-done.10.refs_5_
  77.4 0.0 collective-permute-done.6.refs_2_
  77.4 11.7 %shard_map.81 = f32[64,128]{1,0:T(8,128)S(1)} custom-call(s32[66]{0:T(128)S(1)} %pad_add_fusion.place_ref, bf16[16,96,256]{2,1,0:T(8,128)(2,1)} %collective-permute-done.4.refs_1_.refs_0_, bf16[16,96,256]{2,1,0:T(8,128)(2,1)} %collective-permute-done.5.refs_2_.refs_1_, bf16[16,96,256]{2,1,0:T(8,128)(2,1)S(1)} %collective-permute-done.6.refs_2_, ...), custom_call_target="tpu_custom_call" | custom-call | flops 9663676416 | bytes 16777216 | tf_op jit(solution)/shard_map/pallas_call | solution.py:253
  89.1 22.2 %all_to_all.11 = f32[64,1,128]{2,1,0:T(1,128)} all-to-all(f32[64,1,128]{2,1,0:T(1,128)S(1)} %bitcast.6), channel_id=1, replica_groups=mesh['x'=4,'y'=4,'c'=2,'z'=4] {'x','y','z'}, dimensions={0} | all-to-all | bytes 65536 | tf_op jit(solution)/shard_map/all_to_all | solution.py:332
  111.3 1.5 %shard_map.82 = (f32[1,128]{1,0:T(1,128)}, f32[1,100]{1,0:T(1,128)}) custom-call(f32[64,128]{1,0:T(8,128)} %bitcast.7), custom_call_target="tpu_custom_call" | custom-call | tf_op jit(solution)/shard_map/pallas_call | solution.py:291
  (3 shorter events, 0.1 us)
Async XLA Ops:
  2.3 5.3 %collective-permute-start = (bf16[1,272,256]{2,1,0:T(8,128)(2,1)}, bf16[1,272,256]{2,1,0:T(8,128)(2,1)S(1)}, u32[]{:S(2)}, u32[]{:S(2)}) collective-permute-start(bf16[1,272,256]{2,1,0:T(8,128)(2,1)} %shard_map.77), channel_id=1, source_target_pairs={{0,1},{1,0},{2,3},{3,2},{4,7},{5,6},{6,5},{7,4},{8,9},{9,8},{10,11... | collective-permute-start | bytes 417800 | tf_op jit(solution)/shard_map/ppermute | solution.py:112
  8.5 6.6 %collective-permute-start.1 = (bf16[2,272,256]{2,1,0:T(8,128)(2,1)S(1)}, bf16[2,272,256]{2,1,0:T(8,128)(2,1)S(1)}, u32[]{:S(2)}, u32[]{:S(2)}) collective-permute-start(bf16[2,272,256]{2,1,0:T(8,128)(2,1)S(1)} %pad_maximum_fusion.4), channel_id=1, source_target_pairs={{0,32},{1,33},{2,34},{3,35},{4,100},{5,101},{6,102},{7,103},{8,40}... | collective-permute-start | bytes 835592 | tf_op jit(solution)/shard_map/ppermute | solution.py:112
  16.1 10.8 %collective-permute-start.2 = (bf16[4,272,256]{2,1,0:T(8,128)(2,1)S(1)}, bf16[4,272,256]{2,1,0:T(8,128)(2,1)S(1)}, u32[]{:S(2)}, u32[]{:S(2)}) collective-permute-start(bf16[4,272,256]{2,1,0:T(8,128)(2,1)S(1)} %pad_maximum_fusion.3), channel_id=1, source_target_pairs={{0,24},{1,25},{2,26},{3,27},{4,12},{5,13},{6,14},{7,15},{8,16},{9,... | collective-permute-start | bytes 1671176 | tf_op jit(solution)/shard_map/ppermute | solution.py:112
  26.9 30.6 %collective-permute-start.15 = (bf16[32,256,256]{2,1,0:T(8,128)(2,1)}, bf16[32,256,256]{2,1,0:T(8,128)(2,1)}, u32[]{:S(2)}, u32[]{:S(2)}) collective-permute-start(bf16[32,256,256]{2,1,0:T(8,128)(2,1)} %get-tuple-element.13.refs_3_.refs_9_.refs_11_), channel_id=1, source_target_pairs={{0,4},{4,0},{1,5},{5,1},{2,6},{6,2},{3,7},{7,3},{8,12},{12,8},{9,1... | collective-permute-start | bytes 12582920 | tf_op jit(solution)/shard_map/ppermute | solution.py:326
  27.2 9.1 %collective-permute-start.7 = (bf16[8,96,256]{2,1,0:T(8,128)(2,1)S(1)}, bf16[8,96,256]{2,1,0:T(8,128)(2,1)S(1)}, u32[]{:S(2)}, u32[]{:S(2)}) collective-permute-start(bf16[8,96,256]{2,1,0:T(8,128)(2,1)S(1)} %get-tuple-element.16), channel_id=1, source_target_pairs={{0,96},{1,97},{2,98},{3,99},{4,36},{5,37},{6,38},{7,39},{8,104},{9... | collective-permute-start | bytes 1179656 | tf_op jit(solution)/shard_map/ppermute | solution.py:112
  30.1 9.2 %collective-permute-start.11 = (bf16[8,80,256]{2,1,0:T(8,128)(2,1)S(1)}, bf16[8,80,256]{2,1,0:T(8,128)(2,1)S(1)}, u32[]{:S(2)}, u32[]{:S(2)}) collective-permute-start(bf16[8,80,256]{2,1,0:T(8,128)(2,1)S(1)} %slice.14), channel_id=1, source_target_pairs={{0,3},{1,2},{2,1},{3,0},{4,5},{5,4},{6,7},{7,6},{8,11},{9,10},{10,... | collective-permute-start | bytes 983048 | tf_op jit(solution)/shard_map/ppermute | solution.py:112
  34.2 7.8 %collective-permute-start.3 = (bf16[8,96,256]{2,1,0:T(8,128)(2,1)S(1)}, bf16[8,96,256]{2,1,0:T(8,128)(2,1)S(1)}, u32[]{:S(2)}, u32[]{:S(2)}) collective-permute-start(bf16[8,96,256]{2,1,0:T(8,128)(2,1)S(1)} %get-tuple-element.17), channel_id=1, source_target_pairs={{0,8},{1,9},{2,10},{3,11},{4,28},{5,29},{6,30},{7,31},{8,0},{9,1},... | collective-permute-start | bytes 1179656 | tf_op jit(solution)/shard_map/ppermute | solution.py:112
  36.3 15.4 %collective-permute-start.8 = (bf16[16,96,256]{2,1,0:T(8,128)(2,1)S(1)}, bf16[16,96,256]{2,1,0:T(8,128)(2,1)S(1)}, u32[]{:S(2)}, u32[]{:S(2)}) collective-permute-start(bf16[16,96,256]{2,1,0:T(8,128)(2,1)S(1)} %pad_maximum_fusion.1.refs_1_.refs_3_), channel_id=1, source_target_pairs={{0,8},{1,9},{2,10},{3,11},{4,28},{5,29},{6,30},{7,31},{8,0},{9,1},... | collective-permute-start | bytes 2359304 | tf_op jit(solution)/shard_map/ppermute | solution.py:112
  39.3 13.9 %copy-start.5 = (s32[8]{0:T(128)S(1)}, s32[8]{0:T(128)}, u32[]{:S(2)}) copy-start(s32[8]{0:T(128)} %constant.41) | copy-start | bytes 100
  39.3 20.0 %copy-start.1 = (bf16[256,256]{1,0:T(8,128)(2,1)S(1)}, bf16[256,256]{1,0:T(8,128)(2,1)}, u32[]{:S(2)}) copy-start(bf16[256,256]{1,0:T(8,128)(2,1)} %get-tuple-element.14.refs_5_.refs_11_.refs_13_) | copy-start | bytes 393220
  39.3 20.0 %copy-start.2 = (bf16[256,256]{1,0:T(8,128)(2,1)S(1)}, bf16[256,256]{1,0:T(8,128)(2,1)}, u32[]{:S(2)}) copy-start(bf16[256,256]{1,0:T(8,128)(2,1)} %get-tuple-element.15.refs_6_.refs_12_.refs_14_) | copy-start | bytes 393220
  39.3 11.9 %collective-permute-start.12 = (bf16[16,80,256]{2,1,0:T(8,128)(2,1)S(1)}, bf16[16,80,256]{2,1,0:T(8,128)(2,1)S(1)}, u32[]{:S(2)}, u32[]{:S(2)}) collective-permute-start(bf16[16,80,256]{2,1,0:T(8,128)(2,1)S(1)} %pad_maximum_fusion.2.refs_2_.refs_6_), channel_id=1, source_target_pairs={{0,96},{1,97},{2,98},{3,99},{4,36},{5,37},{6,38},{7,39},{8,104},{9... | collective-permute-start | bytes 1966088 | tf_op jit(solution)/shard_map/ppermute | solution.py:112
  42.0 13.4 %collective-permute-start.4 = (bf16[16,96,256]{2,1,0:T(8,128)(2,1)S(1)}, bf16[16,96,256]{2,1,0:T(8,128)(2,1)}, u32[]{:S(2)}, u32[]{:S(2)}) collective-permute-start(bf16[16,96,256]{2,1,0:T(8,128)(2,1)S(1)} %pad_maximum_fusion.refs_0_), channel_id=1, source_target_pairs={{0,3},{1,2},{2,1},{3,0},{4,5},{5,4},{6,7},{7,6},{8,11},{9,10},{10,... | collective-permute-start | bytes 2359304 | tf_op jit(solution)/shard_map/ppermute | solution.py:112
  43.9 23.5 %collective-permute-start.9 = (bf16[16,96,256]{2,1,0:T(8,128)(2,1)S(1)}, bf16[16,96,256]{2,1,0:T(8,128)(2,1)}, u32[]{:S(2)}, u32[]{:S(2)}) collective-permute-start(bf16[16,96,256]{2,1,0:T(8,128)(2,1)S(1)} %pad_maximum_fusion.1.refs_1_.refs_3_), channel_id=1, source_target_pairs={{0,3},{1,2},{2,1},{3,0},{4,5},{5,4},{6,7},{7,6},{8,11},{9,10},{10,... | collective-permute-start | bytes 2359304 | tf_op jit(solution)/shard_map/ppermute | solution.py:112
  51.2 0.8 copy-start.3
  51.2 16.2 %collective-permute-start.5 = (bf16[16,96,256]{2,1,0:T(8,128)(2,1)S(1)}, bf16[16,96,256]{2,1,0:T(8,128)(2,1)}, u32[]{:S(2)}, u32[]{:S(2)}) collective-permute-start(bf16[16,96,256]{2,1,0:T(8,128)(2,1)S(1)} %pad_maximum_fusion.refs_0_), channel_id=1, source_target_pairs={{0,96},{1,97},{2,98},{3,99},{4,36},{5,37},{6,38},{7,39},{8,104},{9... | collective-permute-start | bytes 2359304 | tf_op jit(solution)/shard_map/ppermute | solution.py:112
  52.0 14.7 %collective-permute-start.13 = (bf16[16,80,256]{2,1,0:T(8,128)(2,1)S(1)}, bf16[16,80,256]{2,1,0:T(8,128)(2,1)}, u32[]{:S(2)}, u32[]{:S(2)}) collective-permute-start(bf16[16,80,256]{2,1,0:T(8,128)(2,1)S(1)} %pad_maximum_fusion.2.refs_2_.refs_6_), channel_id=1, source_target_pairs={{0,8},{1,9},{2,10},{3,11},{4,28},{5,29},{6,30},{7,31},{8,0},{9,1},... | collective-permute-start | bytes 1966088 | tf_op jit(solution)/shard_map/ppermute | solution.py:112
  55.4 22.0 %collective-permute-start.10 = (bf16[16,96,256]{2,1,0:T(8,128)(2,1)S(1)}, bf16[16,96,256]{2,1,0:T(8,128)(2,1)S(1)}, u32[]{:S(2)}, u32[]{:S(2)}) collective-permute-start(bf16[16,96,256]{2,1,0:T(8,128)(2,1)S(1)} %collective-permute-done.8.refs_4_.refs_3_), channel_id=1, source_target_pairs={{0,3},{1,2},{2,1},{3,0},{4,5},{5,4},{6,7},{7,6},{8,11},{9,10},{10,... | collective-permute-start | bytes 2359304 | tf_op jit(solution)/shard_map/ppermute | solution.py:112
  57.5 19.9 %collective-permute-start.6 = (bf16[16,96,256]{2,1,0:T(8,128)(2,1)}, bf16[16,96,256]{2,1,0:T(8,128)(2,1)S(1)}, u32[]{:S(2)}, u32[]{:S(2)}) collective-permute-start(bf16[16,96,256]{2,1,0:T(8,128)(2,1)} %collective-permute-done.4.refs_1_.refs_0_), channel_id=1, source_target_pairs={{0,96},{1,97},{2,98},{3,99},{4,36},{5,37},{6,38},{7,39},{8,104},{9... | collective-permute-start | bytes 2359304 | tf_op jit(solution)/shard_map/ppermute | solution.py:112
  59.3 2.2 %copy-start = (bf16[32,256,256]{2,1,0:T(8,128)(2,1)S(1)}, bf16[32,256,256]{2,1,0:T(8,128)(2,1)}, u32[]{:S(2)}) copy-start(bf16[32,256,256]{2,1,0:T(8,128)(2,1)} %get-tuple-element.13.refs_3_.refs_9_.refs_11_) | copy-start | bytes 12582916
  61.5 5.2 %copy-start.4 = (bf16[16,80,256]{2,1,0:T(8,128)(2,1)S(1)}, bf16[16,80,256]{2,1,0:T(8,128)(2,1)}, u32[]{:S(2)}) copy-start(bf16[16,80,256]{2,1,0:T(8,128)(2,1)} %copy-done.3) | copy-start | bytes 1966084
  66.7 10.7 %collective-permute-start.14 = (bf16[16,80,256]{2,1,0:T(8,128)(2,1)S(1)}, bf16[16,80,256]{2,1,0:T(8,128)(2,1)S(1)}, u32[]{:S(2)}, u32[]{:S(2)}) collective-permute-start(bf16[16,80,256]{2,1,0:T(8,128)(2,1)S(1)} %copy-done.4), channel_id=1, source_target_pairs={{0,8},{1,9},{2,10},{3,11},{4,28},{5,29},{6,30},{7,31},{8,0},{9,1},... | collective-permute-start | bytes 1966088 | tf_op jit(solution)/shard_map/ppermute | solution.py:112
